TPU v7x, 32 devices: a whole 2x2x4 slice. The times are simulated.
32 devices in a mesh: grp: 2 (over x), seq: 16 (over z, y, core).
Axes of the slice: x: 2, y: 2, z: 4, core: 2. Of those that a mesh axis runs over, the one named last changes fastest.
Arguments:
- out_grads: bfloat16 [4096, 8192], P(('grp', 'seq')), parts along dimension 0
- layer_inputs: bfloat16 [4096, 28672], P(('grp', 'seq')), parts along dimension 0
- factor_u: bfloat16 [64, 8192], P('seq'), may hold values from -0.0625 to 0.0625
- factor_v: bfloat16 [64, 28672], P('seq'), may hold values from -0.005859375 to 0.005859375
- seq_lengths: int32 [128], P('grp'), parts along dimension 0, may hold values from 1 to 125, as said below
Outputs:
- scores: float32 [2, 128], P(None, ('grp', 'seq')), parts along dimension 1
There are 2 independent parts, one for each index of `grp`. A program takes and returns all parts, laid end to end along the dimension named above; an argument that names none is the same for every part. Nothing has to cross between parts.
Inputs may be any that keep to these rules, and one draw needn't show every extreme that they name: `seq_lengths`: entries b * 4 to (b + 1) * 4 - 1 are the lengths of the sequences in token-row block b, laid out in order from the block's first row. Each block's lengths sum to at most 128, which some block reaches in every draw; all lengths of a part sum to exactly 66 times the number of blocks.
All inputs are finite; a program needn't handle non-finite values.
Results may differ from a plain program's by a relative error of at most 0.0003.
Values may be sent and summed in bfloat16 or wider, within the bound.
No kernel may reach another device: no remote copies, remote signals or barrier semaphores. Data moves between devices by JAX's collectives and lax.ppermute only.
A program may use at most 128 MiB of HBM per device.

v0:
```python
import jax
import jax.numpy as jnp
from jax import lax
from jax.sharding import PartitionSpec as P

D = 8192
FF = 28672
RANK = 32


EPSILON = 1e-06


def inner_rows(left, right):
    return lax.dot_general(
        left, right, (((1,), (1,)), ((), ())), preferred_element_type=jnp.float32
    )


def rank_sums(proj_out, proj_in):
    row_total = proj_out.shape[0]
    query_total = proj_out.shape[1] // RANK
    return jnp.sum((proj_out * proj_in).reshape(row_total, query_total, RANK), axis=2)


def local(out_grads, layer_inputs, factor_u, factor_v, seq_lengths):
    tok_cap = out_grads.shape[0]
    devices = lax.axis_size("seq")
    my_index = lax.axis_index("seq")
    seq_dev = seq_lengths.shape[0] // devices
    length_table = seq_lengths.reshape(devices, seq_dev)
    device_ids = jnp.arange(devices, dtype=jnp.int32)
    is_mine = device_ids == my_index
    own_lengths = jnp.sum(jnp.where(is_mine[:, None], length_table, 0), axis=0)
    own_ends = jnp.cumsum(own_lengths)
    positions = jnp.arange(tok_cap, dtype=jnp.int32)
    local_seq = jnp.sum((positions[:, None] >= own_ends[None, :]).astype(jnp.int32), axis=1)
    member = (local_seq[:, None] == jnp.arange(seq_dev, dtype=jnp.int32)[None, :]).astype(
        jnp.float32
    )
    gram_out = inner_rows(out_grads, out_grads)
    gram_in = inner_rows(layer_inputs, layer_inputs)
    paired = gram_out * gram_in
    self_norm = jnp.sum(
        jnp.dot(paired, member, precision=lax.Precision.HIGHEST) * member, axis=0
    ) / (D * FF)
    gathered_u, gathered_v = (
        lax.all_gather(factor_u, "seq", axis=0, tiled=True),
        lax.all_gather(factor_v, "seq", axis=0, tiled=True),
    )
    proj_out = inner_rows(out_grads, gathered_u)
    proj_in = inner_rows(layer_inputs, gathered_v)
    token_score = rank_sums(proj_out, proj_in)
    numerator = jnp.dot(token_score.T, member, precision=lax.Precision.HIGHEST)
    return numerator / jnp.sqrt(self_norm + EPSILON)[None, :]


def solution(mesh):
    in_specs = (
        P(("grp", "seq"), None),
        P(("grp", "seq"), None),
        P("seq", None),
        P("seq", None),
        P("grp"),
    )
    out_specs = P(None, ("grp", "seq"))
    return jax.shard_map(local, mesh=mesh, in_specs=in_specs, out_specs=out_specs, check_vma=False)
```

profile of v0, /device:TPU:0, one launch (start us, length us, event | category | flops | bytes accessed | tf_op | source)
XLA Modules:
  0.0 118.0 jit_solution(3121426949254590649)
XLA Ops:
  6.5 0.0 copy-start
  6.5 0.0 all-gather.5.cloned.1.call-start
  6.5 0.7 all-gather.5.cloned.1.call-update
  7.3 0.0 all-gather.7.cloned.1.call-start
  7.3 0.7 all-gather.7.cloned.1.call-update
  8.0 0.7 reshape.41
  8.8 0.1 select_reduce_fusion
  8.9 0.2 reduce-window.8
  9.0 0.1 convert_reduce_fusion
  9.1 0.0 copy-done
  9.1 0.7 fusion.4
  9.8 7.6 %convolution_multiply_fusion = f32[128,128]{1,0:T(8,128)S(1)} fusion(f32[128,128]{1,0:T(8,128)S(1)} %fusion.4, bf16[128,28672]{1,0:T(8,128)(2,1)} %param.6), kind=kOutput, calls=%fused_computation | convolution fusion | flops 939540480 | bytes 7471104 | tf_op jit(solution)/shard_map/dot_general | solution.py:15
  17.5 0.3 fusion
  17.8 32.4 %all-gather.5.cloned.1.call-done = bf16[16,4,8192]{2,1,0:T(4,128)(2,1)} async-done(((bf16[1,4,8192]{2,1,0:T(4,128)(2,1)}), bf16[16,4,8192]{2,1,0:T(4,128)(2,1)}) %all-gather.5.cloned.1.call-update) | async-done | bytes 1048592 | tf_op jit(solution)/shard_map/all_gather | solution.py:48
  50.2 1.3 %reshape.45 = bf16[64,8192]{1,0:T(8,128)(2,1)S(1)} reshape(bf16[16,4,8192]{2,1,0:T(4,128)(2,1)} %all-gather.5.cloned.1.call-done) | data formatting | bytes 2097152
  51.5 0.8 fusion.3
  52.4 46.5 %all-gather.7.cloned.1.call-done = bf16[16,4,28672]{2,1,0:T(4,128)(2,1)} async-done(((bf16[1,4,28672]{2,1,0:T(4,128)(2,1)}), bf16[16,4,28672]{2,1,0:T(4,128)(2,1)}) %all-gather.7.cloned.1.call-update) | async-done | bytes 3670032 | tf_op jit(solution)/shard_map/all_gather | solution.py:49
  98.9 4.8 %reshape.47 = bf16[64,28672]{1,0:T(8,128)(2,1)} reshape(bf16[16,4,28672]{2,1,0:T(4,128)(2,1)} %all-gather.7.cloned.1.call-done) | data formatting | bytes 7340032
  103.7 6.8 %bitcast_reduce_fusion = f32[128,2]{0,1:T(2,128)S(1)} fusion(f32[128,64]{0,1:T(8,128)S(1)} %fusion.3, bf16[128,28672]{1,0:T(8,128)(2,1)} %param.6, bf16[64,28672]{1,0:T(8,128)(2,1)} %reshape.47), kind=kOutput, calls=%fused_computation.5 | convolution fusion | flops 469778176 | bytes 11043840 | tf_op jit(solution)/shard_map/dot_general | solution.py:15
  110.5 0.7 convolution_divide_fusion
  (2 shorter events, 0.0 us)
Async XLA Ops:
  6.5 2.6 %copy-start = (bf16[128,8192]{1,0:T(8,128)(2,1)S(1)}, bf16[128,8192]{1,0:T(8,128)(2,1)}, u32[]{:S(2)}) copy-start(bf16[128,8192]{1,0:T(8,128)(2,1)} %param.5) | copy-start | bytes 6291460
  6.5 43.7 %all-gather.5.cloned.1.call-start = ((), (), s32[]{:S(2)}) async-start(), calls=%async_computation | async-start | bytes 1114112 | tf_op jit(solution)/shard_map/all_gather | solution.py:48
  7.3 91.7 %all-gather.7.cloned.1.call-start = ((), (), s32[]{:S(2)}) async-start(), calls=%async_computation.1 | async-start | bytes 3899392 | tf_op jit(solution)/shard_map/all_gather | solution.py:49
Sparse Core Ops, SparseCore 0:
  9.5 40.6 all-gather.4
  52.5 46.4 all-gather.6
where the time goes:
time: 118 us
  waiting for transfers between devices  80.4 us (68%)
  matrix products  17 us (14%)
  between operations  13.4 us (11%)
  local copies, waits for them, and re-layouts  6.85 us (6%)
    all_gather x1, waiting for transfers between devices, local(): lax.all_gather(factor_v, 'seq', axis=0, tiled=True)  46.5 us
    all_gather x1, waiting for transfers between devices, local(): lax.all_gather(factor_u, 'seq', axis=0, tiled=True)  32.4 us
    dot_general x4, matrix products, inner_rows(): lax.dot_general(left, right, (((1,), (1,)), ((), ())), preferred_element_...  16 us
    unnamed x4, local copies, waits for them, and re-layouts  6.12 us
  transfers between devices with their start and end apart: 2, of which 2 were waited for; matrix products, arithmetic and copies ran while one was open for 10% of the time, Pallas kernels for 0%

commit v1 on v0

v1 whole, which is shorter than its diff:
```python
import functools

import jax
import jax.numpy as jnp
from jax import lax
from jax.experimental import pallas as pl
from jax.experimental.pallas import tpu as pltpu
from jax.sharding import PartitionSpec as P

RANK = 32
EPSILON = 1e-06
PACK = 16
VMEM_BYTES = 38 * 1024 * 1024

NT = (((1,), (1,)), ((), ()))


def inner_rows(left, right):
    return lax.dot_general(left, right, NT, preferred_element_type=jnp.float32)


def sequence_ends(lengths_ref, block, seq_dev):
    ends, total = [], 0
    for k in range(seq_dev):
        total = total + lengths_ref[block * seq_dev + k]
        ends.append(total)
    return ends


def in_sequence(positions, ends, k):
    low = 0 if k == 0 else ends[k - 1]
    return ((positions >= low) & (positions < ends[k])).astype(jnp.float32)


def norm_kernel(seq_dev, lengths_ref, out_ref, in_ref, norm_ref):
    tok_cap = out_ref.shape[0]
    width_out, width_in = out_ref.shape[1], in_ref.shape[1]
    gram_out = inner_rows(out_ref[...], out_ref[...])
    gram_in = inner_rows(in_ref[...], in_ref[...])
    paired = gram_out * gram_in
    ends = sequence_ends(lengths_ref, lax.axis_index("seq"), seq_dev)
    rows = lax.broadcasted_iota(jnp.int32, (tok_cap, 1), 0)
    cols = lax.broadcasted_iota(jnp.int32, (1, tok_cap), 1)
    lanes = lax.broadcasted_iota(jnp.int32, norm_ref.shape, 1)
    norms = jnp.zeros(norm_ref.shape, jnp.float32)
    for k in range(seq_dev):
        by_col = jnp.sum(paired * in_sequence(rows, ends, k), axis=0, keepdims=True)
        value = jnp.sum(by_col * in_sequence(cols, ends, k), axis=1, keepdims=True)
        norms = jnp.where(lanes == k, value / (width_out * width_in), norms)
    norm_ref[...] = norms


def score_kernel(seq_dev, rank_rows, by_xor, count, lengths_ref, norm_ref, out_ref, in_ref, *refs):
    block_refs, score_ref = refs[:count], refs[count]
    tok_cap = out_ref.shape[0]
    chunks = PACK // rank_rows
    wide_out, wide_in = out_ref.shape[1] // chunks, in_ref.shape[1] // chunks
    total = sum(ref.shape[0] for ref in block_refs)
    lanes = lax.broadcasted_iota(jnp.int32, (1, total), 1)
    lane_chunk = (lanes % PACK) // rank_rows

    def project(tokens_ref, wide, offset):
        held = jnp.zeros((tok_cap, total), jnp.float32)
        rows = jnp.concatenate([ref[:, offset : offset + wide] for ref in block_refs], axis=0)
        for j in range(chunks):
            part = inner_rows(tokens_ref[:, j * wide : (j + 1) * wide], rows)
            held = jnp.where(lane_chunk == j, part, held)
        summed = held
        for j in range(1, chunks):
            summed = summed + pltpu.roll(held, total - j * rank_rows, 1)
        return summed

    product = project(out_ref, wide_out, 0) * project(in_ref, wide_in, wide_out)
    me = lax.axis_index("seq")
    source = lanes // PACK
    if by_xor:
        source = source ^ me
    query = jnp.where(lane_chunk == 0, (source * rank_rows) // RANK, -1)
    ends = sequence_ends(lengths_ref, me, seq_dev)
    positions = lax.broadcasted_iota(jnp.int32, (tok_cap, 1), 0)
    at_query = lax.broadcasted_iota(jnp.int32, score_ref.shape, 0)
    at_seq = lax.broadcasted_iota(jnp.int32, score_ref.shape, 1)
    numerator = jnp.zeros(score_ref.shape, jnp.float32)
    for k in range(seq_dev):
        by_row = jnp.sum(product * in_sequence(positions, ends, k), axis=0, keepdims=True)
        for q in range(score_ref.shape[0]):
            value = jnp.sum(jnp.where(query == q, by_row, 0.0), axis=1, keepdims=True)
            numerator = jnp.where((at_query == q) & (at_seq == k), value, numerator)
    score_ref[...] = numerator / jnp.sqrt(norm_ref[0:1, 0:seq_dev] + EPSILON)


def gather_blocks(own, devices):
    if devices != 16:
        return False, [lax.all_gather(own, "seq", axis=0, tiled=True)]

    def swap(value, mask):
        return lax.ppermute(value, "seq", [(i, i ^ mask) for i in range(devices)])

    blocks = {0: own}
    blocks[2] = swap(own, 2)
    for z in (4, 8, 12):
        blocks[z] = swap(own, z)
    for z in (4, 8, 12):
        blocks[z + 2] = swap(blocks[z], 2)
    for b in list(blocks):
        blocks[b + 1] = swap(blocks[b], 1)
    return True, [blocks[b] for b in range(devices)]


def local(out_grads, layer_inputs, factor_u, factor_v, seq_lengths):
    devices = lax.axis_size("seq")
    seq_dev = seq_lengths.shape[0] // devices
    rank_rows = factor_u.shape[0]
    chunks = PACK // rank_rows
    queries = rank_rows * devices // RANK
    own = jnp.concatenate(
        [
            jnp.concatenate(jnp.split(factor_u, chunks, axis=1), axis=0),
            jnp.concatenate(jnp.split(factor_v, chunks, axis=1), axis=0),
        ],
        axis=1,
    )
    by_xor, blocks = gather_blocks(own, devices)
    smem = pl.BlockSpec(memory_space=pltpu.SMEM)
    vmem = pl.BlockSpec(memory_space=pltpu.VMEM)
    params = pltpu.CompilerParams(vmem_limit_bytes=VMEM_BYTES)
    tok_cap, width_out = out_grads.shape
    width = width_out + layer_inputs.shape[1]
    norms = pl.pallas_call(
        functools.partial(norm_kernel, seq_dev),
        out_shape=jax.ShapeDtypeStruct((8, 128), jnp.float32),
        in_specs=[smem, vmem, vmem],
        out_specs=vmem,
        compiler_params=params,
        cost_estimate=pl.CostEstimate(
            flops=2 * tok_cap * tok_cap * width, bytes_accessed=2 * tok_cap * width, transcendentals=0
        ),
    )(seq_lengths, out_grads, layer_inputs)
    total = sum(b.shape[0] for b in blocks)
    return pl.pallas_call(
        functools.partial(score_kernel, seq_dev, rank_rows, by_xor, len(blocks)),
        out_shape=jax.ShapeDtypeStruct((queries, seq_dev), jnp.float32),
        in_specs=[smem, vmem, vmem, vmem] + [vmem] * len(blocks),
        out_specs=vmem,
        compiler_params=params,
        cost_estimate=pl.CostEstimate(
            flops=2 * tok_cap * total * width, bytes_accessed=2 * tok_cap * width, transcendentals=0
        ),
    )(seq_lengths, norms, out_grads, layer_inputs, *blocks)


def solution(mesh):
    in_specs = (
        P(("grp", "seq"), None),
        P(("grp", "seq"), None),
        P("seq", None),
        P("seq", None),
        P("grp"),
    )
    out_specs = P(None, ("grp", "seq"))
    return jax.shard_map(local, mesh=mesh, in_specs=in_specs, out_specs=out_specs, check_vma=False)
```

time: 118 us -> 63.7 us (0.54)
  waiting for transfers between devices: 80.4 us -> 33 us
  matrix products: 17 us -> 0 us
  between operations: 13.4 us -> 0.07 us
  starting transfers between devices: 0.04 us -> 12.2 us
  Pallas kernels: 0 us -> 10.8 us
    all_gather x2 -> x0, waiting for transfers between devices: 79 us -> none  [the longest x1 46.5 us: local(): lax.all_gather(factor_v, 'seq', axis=0, tiled=True)]
    ppermute x0 -> x15, waiting for transfers between devices: none -> 33 us  [swap(): return lax.ppermute(value, 'seq', [(i, i ^ mask) for i in range(devices)])]
    dot_general x6 -> x0, matrix products: 17 us -> none  [the longest x4 16 us: inner_rows(): lax.dot_general(left, right, (((1,), (1,)), ((), ())), preferred_element_...]
    ppermute x0 -> x15, starting transfers between devices: none -> 12.2 us  [swap(): return lax.ppermute(value, 'seq', [(i, i ^ mask) for i in range(devices)])]
    pallas_call x0 -> x2, Pallas kernels: none -> 10.8 us  [the longest x1 7.6 us: local(): pl.pallas_call(functools.partial(score_kernel, seq_dev, rank_rows, by_xor...]
    split x0 -> x2, local copies, waits for them, and re-layouts: none -> 1.78 us  [the longest x1 0.98 us: local(): jnp.split(factor_v, chunks, axis=1)]
    unnamed x2 -> x0, waiting for transfers between devices: 1.41 us -> none
    unnamed x4 -> x6, local copies, waits for them, and re-layouts: 6.12 us -> 5.33 us
  transfers between devices with their start and end apart: 2 -> 15, of which waited for: 2 -> 4; matrix products, arithmetic and copies ran while one was open for 10% -> 0% of each run, Pallas kernels for 0% -> 5%
where the time goes in v1:
time: 63.7 us; the launch traced here: 63.4 us
  waiting for transfers between devices  33 us (52%)
  starting transfers between devices  12.2 us (19%)
  Pallas kernels  10.8 us (17%)
  local copies, waits for them, and re-layouts  7.11 us (11%)
    ppermute x15, waiting for transfers between devices, swap(): return lax.ppermute(value, 'seq', [(i, i ^ mask) for i in range(devices)])  33 us
    ppermute x15, starting transfers between devices, swap(): return lax.ppermute(value, 'seq', [(i, i ^ mask) for i in range(devices)])  12.2 us
    pallas_call x1, Pallas kernels, local(): pl.pallas_call(functools.partial(score_kernel, seq_dev, rank_rows, by_xor...  7.6 us
    unnamed x6, local copies, waits for them, and re-layouts  5.33 us
    pallas_call x1, Pallas kernels, local(): pl.pallas_call(functools.partial(norm_kernel, seq_dev), out_shape=jax.Sha...  3.22 us
  transfers between devices with their start and end apart: 15, of which 4 were waited for; matrix products, arithmetic and copies ran while one was open for 0% of the time, Pallas kernels for 5%

profile of v1, /device:TPU:0, one launch (start us, length us, event | category | flops | bytes accessed | tf_op | source)
XLA Modules:
  0.0 63.4 jit_solution(3699789883635296755)
XLA Ops:
  0.0 1.0 %fusion = (bf16[4,7168]{1,0:T(4,128)(2,1)S(1)}, bf16[4,7168]{1,0:T(4,128)(2,1)S(1)}, bf16[4,7168]{1,0:T(4,128)(2,1)S(1)}, bf16[4,7168]{1,0:T(4,128)(2,1)S(1)}) fusion(bf16[4,28672]{1,0:T(4,128)(2,1)} %param.8), kind=kLoop, calls=%fused_computation.1 | loop fusion | bytes 458752 | tf_op jit(solution)/shard_map/split | solution.py:119
  1.0 0.8 %fusion.1 = (bf16[4,2048]{1,0:T(4,128)(2,1)S(1)}, bf16[4,2048]{1,0:T(4,128)(2,1)S(1)}, bf16[4,2048]{1,0:T(4,128)(2,1)S(1)}, bf16[4,2048]{1,0:T(4,128)(2,1)S(1)}) fusion(bf16[4,8192]{1,0:T(4,128)(2,1)} %param.7), kind=kLoop, calls=%fused_computation.2 | loop fusion | bytes 131072 | tf_op jit(solution)/shard_map/split | solution.py:118
  1.8 0.2 maximum_maximum_fusion.refs_0_
  2.0 4.1 %collective-permute-start.7 = (bf16[16,9216]{1,0:T(8,128)(2,1)S(1)}, bf16[16,9216]{1,0:T(8,128)(2,1)S(1)}, u32[]{:S(2)}, u32[]{:S(2)}) collective-permute-start(bf16[16,9216]{1,0:T(8,128)(2,1)S(1)} %maximum_maximum_fusion.refs_0_), channel_id=1, source_target_pairs={{0,8},{1,9},{2,10},{3,11},{4,12},{5,13},{6,14},{7,15},{8,0},{9,1},... | collective-permute-start | bytes 884744 | tf_op jit(solution)/shard_map/ppermute | solution.py:97
  6.1 1.3 %collective-permute-start.11 = (bf16[16,9216]{1,0:T(8,128)(2,1)S(1)}, bf16[16,9216]{1,0:T(8,128)(2,1)S(1)}, u32[]{:S(2)}, u32[]{:S(2)}) collective-permute-start(bf16[16,9216]{1,0:T(8,128)(2,1)S(1)} %maximum_maximum_fusion.refs_0_), channel_id=1, source_target_pairs={{0,12},{1,13},{2,14},{3,15},{4,8},{5,9},{6,10},{7,11},{8,4},{9,5},... | collective-permute-start | bytes 884744 | tf_op jit(solution)/shard_map/ppermute | solution.py:97
  7.4 0.2 collective-permute-start.3
  7.7 1.5 %collective-permute-start.1 = (bf16[16,9216]{1,0:T(8,128)(2,1)S(1)}, bf16[16,9216]{1,0:T(8,128)(2,1)S(1)}, u32[]{:S(2)}, u32[]{:S(2)}) collective-permute-start(bf16[16,9216]{1,0:T(8,128)(2,1)S(1)} %maximum_maximum_fusion.refs_0_), channel_id=1, source_target_pairs={{0,2},{1,3},{2,0},{3,1},{4,6},{5,7},{6,4},{7,5},{8,10},{9,11},{10,... | collective-permute-start | bytes 884744 | tf_op jit(solution)/shard_map/ppermute | solution.py:97
  9.2 0.0 collective-permute-start
  9.2 17.4 %collective-permute-done.7.refs_8_ = bf16[16,9216]{1,0:T(8,128)(2,1)S(1)} collective-permute-done((bf16[16,9216]{1,0:T(8,128)(2,1)S(1)}, bf16[16,9216]{1,0:T(8,128)(2,1)S(1)}, u32[]{:S(2)}, u32[]{:S(2)}) %collective-permute-start.7) | collective-permute-done | bytes 294944 | tf_op jit(solution)/shard_map/ppermute | solution.py:97
  26.6 1.9 %collective-permute-start.9 = (bf16[16,9216]{1,0:T(8,128)(2,1)S(1)}, bf16[16,9216]{1,0:T(8,128)(2,1)S(1)}, u32[]{:S(2)}, u32[]{:S(2)}) collective-permute-start(bf16[16,9216]{1,0:T(8,128)(2,1)S(1)} %collective-permute-done.7.refs_8_), channel_id=1, source_target_pairs={{0,2},{1,3},{2,0},{3,1},{4,6},{5,7},{6,4},{7,5},{8,10},{9,11},{10,... | collective-permute-start | bytes 884744 | tf_op jit(solution)/shard_map/ppermute | solution.py:97
  28.5 0.2 collective-permute-start.13
  28.6 1.9 %collective-permute-start.5 = (bf16[16,9216]{1,0:T(8,128)(2,1)S(1)}, bf16[16,9216]{1,0:T(8,128)(2,1)S(1)}, u32[]{:S(2)}, u32[]{:S(2)}) collective-permute-start(bf16[16,9216]{1,0:T(8,128)(2,1)S(1)} %collective-permute-done.3.refs_4_), channel_id=1, source_target_pairs={{0,2},{1,3},{2,0},{3,1},{4,6},{5,7},{6,4},{7,5},{8,10},{9,11},{10,... | collective-permute-start | bytes 884744 | tf_op jit(solution)/shard_map/ppermute | solution.py:97
  30.5 0.5 collective-permute-start.4
  31.0 5.5 %collective-permute-done.9.refs_10_ = bf16[16,9216]{1,0:T(8,128)(2,1)S(1)} collective-permute-done((bf16[16,9216]{1,0:T(8,128)(2,1)S(1)}, bf16[16,9216]{1,0:T(8,128)(2,1)S(1)}, u32[]{:S(2)}, u32[]{:S(2)}) %collective-permute-start.9) | collective-permute-done | bytes 294944 | tf_op jit(solution)/shard_map/ppermute | solution.py:97
  36.5 6.3 %collective-permute-done.13.refs_14_ = bf16[16,9216]{1,0:T(8,128)(2,1)S(1)} collective-permute-done((bf16[16,9216]{1,0:T(8,128)(2,1)S(1)}, bf16[16,9216]{1,0:T(8,128)(2,1)S(1)}, u32[]{:S(2)}, u32[]{:S(2)}) %collective-permute-start.13) | collective-permute-done | bytes 294944 | tf_op jit(solution)/shard_map/ppermute | solution.py:97
  42.9 3.7 %collective-permute-done.5.refs_6_ = bf16[16,9216]{1,0:T(8,128)(2,1)S(1)} collective-permute-done((bf16[16,9216]{1,0:T(8,128)(2,1)S(1)}, bf16[16,9216]{1,0:T(8,128)(2,1)S(1)}, u32[]{:S(2)}, u32[]{:S(2)}) %collective-permute-start.5) | collective-permute-done | bytes 294944 | tf_op jit(solution)/shard_map/ppermute | solution.py:97
  46.6 0.5 collective-permute-start.14
  47.1 0.1 collective-permute-start.6
  47.2 3.1 %copy-done = bf16[128,28672]{1,0:T(8,128)(2,1)S(1)} copy-done((bf16[128,28672]{1,0:T(8,128)(2,1)S(1)}, bf16[128,28672]{1,0:T(8,128)(2,1)}, u32[]{:S(2)}) %copy-start) | copy-done | bytes 7340056
  50.3 1.6 %copy-done.1 = bf16[128,8192]{1,0:T(8,128)(2,1)S(1)} copy-done((bf16[128,8192]{1,0:T(8,128)(2,1)S(1)}, bf16[128,8192]{1,0:T(8,128)(2,1)}, u32[]{:S(2)}) %copy-start.1) | copy-done | bytes 2097176
  51.9 0.7 %copy-done.2 = s32[64]{0:T(128)S(1)} copy-done((s32[64]{0:T(128)S(1)}, s32[64]{0:T(128)}, u32[]{:S(2)}) %copy-start.2) | copy-done | bytes 280
  52.5 3.2 %shard_map.55.norm_ref = f32[8,128]{1,0:T(8,128)S(1)} custom-call(s32[64]{0:T(128)S(1)} %copy-done.2, bf16[128,8192]{1,0:T(8,128)(2,1)S(1)} %copy-done.1, bf16[128,28672]{1,0:T(8,128)(2,1)S(1)} %copy-done), custom_call_target="tpu_custom_call" | custom-call | flops 1207959552 | bytes 9437184 | tf_op jit(solution)/shard_map/pallas_call | solution.py:129
  55.8 0.0 collective-permute-done.2.refs_3_
  55.8 7.6 %shard_map.56 = f32[2,4]{1,0:T(2,128)} custom-call(s32[64]{0:T(128)S(1)} %copy-done.2, f32[8,128]{1,0:T(8,128)S(1)} %shard_map.55.norm_ref, bf16[128,8192]{1,0:T(8,128)(2,1)S(1)} %copy-done.1, bf16[128,28672]{1,0:T(8,128)(2,1)S(1)} %copy-done, bf16[16,9216]{1,0:T(8,128)(2,1)S(1)} %maximum_maximum_fusion.refs_0_, ...), custom_call_target="tpu_custom_call" | custom-call | flops 2415919104 | bytes 9437184 | tf_op jit(solution)/shard_map/pallas_call | solution.py:140
  (17 shorter events, 0.0 us)
Async XLA Ops:
  2.0 24.6 %collective-permute-start.7 = (bf16[16,9216]{1,0:T(8,128)(2,1)S(1)}, bf16[16,9216]{1,0:T(8,128)(2,1)S(1)}, u32[]{:S(2)}, u32[]{:S(2)}) collective-permute-start(bf16[16,9216]{1,0:T(8,128)(2,1)S(1)} %maximum_maximum_fusion.refs_0_), channel_id=1, source_target_pairs={{0,8},{1,9},{2,10},{3,11},{4,12},{5,13},{6,14},{7,15},{8,0},{9,1},... | collective-permute-start | bytes 884744 | tf_op jit(solution)/shard_map/ppermute | solution.py:97
  6.1 22.4 %collective-permute-start.11 = (bf16[16,9216]{1,0:T(8,128)(2,1)S(1)}, bf16[16,9216]{1,0:T(8,128)(2,1)S(1)}, u32[]{:S(2)}, u32[]{:S(2)}) collective-permute-start(bf16[16,9216]{1,0:T(8,128)(2,1)S(1)} %maximum_maximum_fusion.refs_0_), channel_id=1, source_target_pairs={{0,12},{1,13},{2,14},{3,15},{4,8},{5,9},{6,10},{7,11},{8,4},{9,5},... | collective-permute-start | bytes 884744 | tf_op jit(solution)/shard_map/ppermute | solution.py:97
  7.4 21.2 %collective-permute-start.3 = (bf16[16,9216]{1,0:T(8,128)(2,1)S(1)}, bf16[16,9216]{1,0:T(8,128)(2,1)S(1)}, u32[]{:S(2)}, u32[]{:S(2)}) collective-permute-start(bf16[16,9216]{1,0:T(8,128)(2,1)S(1)} %maximum_maximum_fusion.refs_0_), channel_id=1, source_target_pairs={{0,4},{1,5},{2,6},{3,7},{4,0},{5,1},{6,2},{7,3},{8,12},{9,13},{10,... | collective-permute-start | bytes 884744 | tf_op jit(solution)/shard_map/ppermute | solution.py:97
  7.7 22.8 %collective-permute-start.1 = (bf16[16,9216]{1,0:T(8,128)(2,1)S(1)}, bf16[16,9216]{1,0:T(8,128)(2,1)S(1)}, u32[]{:S(2)}, u32[]{:S(2)}) collective-permute-start(bf16[16,9216]{1,0:T(8,128)(2,1)S(1)} %maximum_maximum_fusion.refs_0_), channel_id=1, source_target_pairs={{0,2},{1,3},{2,0},{3,1},{4,6},{5,7},{6,4},{7,5},{8,10},{9,11},{10,... | collective-permute-start | bytes 884744 | tf_op jit(solution)/shard_map/ppermute | solution.py:97
  9.2 21.3 %collective-permute-start = (bf16[16,9216]{1,0:T(8,128)(2,1)S(1)}, bf16[16,9216]{1,0:T(8,128)(2,1)S(1)}, u32[]{:S(2)}, u32[]{:S(2)}) collective-permute-start(bf16[16,9216]{1,0:T(8,128)(2,1)S(1)} %maximum_maximum_fusion.refs_0_), channel_id=1, source_target_pairs={{0,1},{1,0},{2,3},{3,2},{4,5},{5,4},{6,7},{7,6},{8,9},{9,8},{10,11... | collective-permute-start | bytes 884744 | tf_op jit(solution)/shard_map/ppermute | solution.py:97
  26.6 9.9 %collective-permute-start.9 = (bf16[16,9216]{1,0:T(8,128)(2,1)S(1)}, bf16[16,9216]{1,0:T(8,128)(2,1)S(1)}, u32[]{:S(2)}, u32[]{:S(2)}) collective-permute-start(bf16[16,9216]{1,0:T(8,128)(2,1)S(1)} %collective-permute-done.7.refs_8_), channel_id=1, source_target_pairs={{0,2},{1,3},{2,0},{3,1},{4,6},{5,7},{6,4},{7,5},{8,10},{9,11},{10,... | collective-permute-start | bytes 884744 | tf_op jit(solution)/shard_map/ppermute | solution.py:97
  28.5 14.4 %collective-permute-start.13 = (bf16[16,9216]{1,0:T(8,128)(2,1)S(1)}, bf16[16,9216]{1,0:T(8,128)(2,1)S(1)}, u32[]{:S(2)}, u32[]{:S(2)}) collective-permute-start(bf16[16,9216]{1,0:T(8,128)(2,1)S(1)} %collective-permute-done.11.refs_12_), channel_id=1, source_target_pairs={{0,2},{1,3},{2,0},{3,1},{4,6},{5,7},{6,4},{7,5},{8,10},{9,11},{10,... | collective-permute-start | bytes 884744 | tf_op jit(solution)/shard_map/ppermute | solution.py:97
  28.6 18.0 %collective-permute-start.5 = (bf16[16,9216]{1,0:T(8,128)(2,1)S(1)}, bf16[16,9216]{1,0:T(8,128)(2,1)S(1)}, u32[]{:S(2)}, u32[]{:S(2)}) collective-permute-start(bf16[16,9216]{1,0:T(8,128)(2,1)S(1)} %collective-permute-done.3.refs_4_), channel_id=1, source_target_pairs={{0,2},{1,3},{2,0},{3,1},{4,6},{5,7},{6,4},{7,5},{8,10},{9,11},{10,... | collective-permute-start | bytes 884744 | tf_op jit(solution)/shard_map/ppermute | solution.py:97
  30.5 16.1 %collective-permute-start.12 = (bf16[16,9216]{1,0:T(8,128)(2,1)S(1)}, bf16[16,9216]{1,0:T(8,128)(2,1)S(1)}, u32[]{:S(2)}, u32[]{:S(2)}) collective-permute-start(bf16[16,9216]{1,0:T(8,128)(2,1)S(1)} %collective-permute-done.11.refs_12_), channel_id=1, source_target_pairs={{0,1},{1,0},{2,3},{3,2},{4,5},{5,4},{6,7},{7,6},{8,9},{9,8},{10,11... | collective-permute-start | bytes 884744 | tf_op jit(solution)/shard_map/ppermute | solution.py:97
  30.5 16.6 %collective-permute-start.4 = (bf16[16,9216]{1,0:T(8,128)(2,1)S(1)}, bf16[16,9216]{1,0:T(8,128)(2,1)S(1)}, u32[]{:S(2)}, u32[]{:S(2)}) collective-permute-start(bf16[16,9216]{1,0:T(8,128)(2,1)S(1)} %collective-permute-done.3.refs_4_), channel_id=1, source_target_pairs={{0,1},{1,0},{2,3},{3,2},{4,5},{5,4},{6,7},{7,6},{8,9},{9,8},{10,11... | collective-permute-start | bytes 884744 | tf_op jit(solution)/shard_map/ppermute | solution.py:97
  36.5 19.2 %collective-permute-start.8 = (bf16[16,9216]{1,0:T(8,128)(2,1)S(1)}, bf16[16,9216]{1,0:T(8,128)(2,1)S(1)}, u32[]{:S(2)}, u32[]{:S(2)}) collective-permute-start(bf16[16,9216]{1,0:T(8,128)(2,1)S(1)} %collective-permute-done.7.refs_8_), channel_id=1, source_target_pairs={{0,1},{1,0},{2,3},{3,2},{4,5},{5,4},{6,7},{7,6},{8,9},{9,8},{10,11... | collective-permute-start | bytes 884744 | tf_op jit(solution)/shard_map/ppermute | solution.py:97
  42.9 12.9 %collective-permute-start.2 = (bf16[16,9216]{1,0:T(8,128)(2,1)S(1)}, bf16[16,9216]{1,0:T(8,128)(2,1)S(1)}, u32[]{:S(2)}, u32[]{:S(2)}) collective-permute-start(bf16[16,9216]{1,0:T(8,128)(2,1)S(1)} %collective-permute-done.1.refs_2_), channel_id=1, source_target_pairs={{0,1},{1,0},{2,3},{3,2},{4,5},{5,4},{6,7},{7,6},{8,9},{9,8},{10,11... | collective-permute-start | bytes 884744 | tf_op jit(solution)/shard_map/ppermute | solution.py:97
  46.6 9.2 %collective-permute-start.10 = (bf16[16,9216]{1,0:T(8,128)(2,1)S(1)}, bf16[16,9216]{1,0:T(8,128)(2,1)S(1)}, u32[]{:S(2)}, u32[]{:S(2)}) collective-permute-start(bf16[16,9216]{1,0:T(8,128)(2,1)S(1)} %collective-permute-done.9.refs_10_), channel_id=1, source_target_pairs={{0,1},{1,0},{2,3},{3,2},{4,5},{5,4},{6,7},{7,6},{8,9},{9,8},{10,11... | collective-permute-start | bytes 884744 | tf_op jit(solution)/shard_map/ppermute | solution.py:97
  46.6 9.2 %collective-permute-start.14 = (bf16[16,9216]{1,0:T(8,128)(2,1)S(1)}, bf16[16,9216]{1,0:T(8,128)(2,1)S(1)}, u32[]{:S(2)}, u32[]{:S(2)}) collective-permute-start(bf16[16,9216]{1,0:T(8,128)(2,1)S(1)} %collective-permute-done.13.refs_14_), channel_id=1, source_target_pairs={{0,1},{1,0},{2,3},{3,2},{4,5},{5,4},{6,7},{7,6},{8,9},{9,8},{10,11... | collective-permute-start | bytes 884744 | tf_op jit(solution)/shard_map/ppermute | solution.py:97
  47.1 8.7 %collective-permute-start.6 = (bf16[16,9216]{1,0:T(8,128)(2,1)S(1)}, bf16[16,9216]{1,0:T(8,128)(2,1)S(1)}, u32[]{:S(2)}, u32[]{:S(2)}) collective-permute-start(bf16[16,9216]{1,0:T(8,128)(2,1)S(1)} %collective-permute-done.5.refs_6_), channel_id=1, source_target_pairs={{0,1},{1,0},{2,3},{3,2},{4,5},{5,4},{6,7},{7,6},{8,9},{9,8},{10,11... | collective-permute-start | bytes 884744 | tf_op jit(solution)/shard_map/ppermute | solution.py:97
  47.2 3.1 %copy-start = (bf16[128,28672]{1,0:T(8,128)(2,1)S(1)}, bf16[128,28672]{1,0:T(8,128)(2,1)}, u32[]{:S(2)}) copy-start(bf16[128,28672]{1,0:T(8,128)(2,1)} %in_ref.3) | copy-start | bytes 22020100
  50.3 1.6 %copy-start.1 = (bf16[128,8192]{1,0:T(8,128)(2,1)S(1)}, bf16[128,8192]{1,0:T(8,128)(2,1)}, u32[]{:S(2)}) copy-start(bf16[128,8192]{1,0:T(8,128)(2,1)} %out_ref.3) | copy-start | bytes 6291460
  51.9 0.7 %copy-start.2 = (s32[64]{0:T(128)S(1)}, s32[64]{0:T(128)}, u32[]{:S(2)}) copy-start(s32[64]{0:T(128)} %lengths_ref.3) | copy-start | bytes 772

commit v2 on v1

v2 whole, which is shorter than its diff:
```python
import functools

import jax
import jax.numpy as jnp
from jax import lax
from jax.experimental import pallas as pl
from jax.experimental.pallas import tpu as pltpu
from jax.sharding import PartitionSpec as P

RANK = 32
EPSILON = 1e-06
PACK = 16
TOKEN_PIECES = 8

NT = (((1,), (1,)), ((), ()))


def inner_rows(left, right):
    return lax.dot_general(left, right, NT, preferred_element_type=jnp.float32)


def sequence_ends(lengths_ref, block, seq_dev):
    ends, total = [], 0
    for k in range(seq_dev):
        total = total + lengths_ref[block * seq_dev + k]
        ends.append(total)
    return ends


def in_sequence(positions, ends, k):
    low = 0 if k == 0 else ends[k - 1]
    return ((positions >= low) & (positions < ends[k])).astype(jnp.float32)


def first_half(paired):
    return lax.axis_index("grp") % 2 if paired else 0


def turn(paired, chunks):
    return lax.axis_index("seq") % chunks if paired else 0


def pack_kernel(chunks, paired, u_ref, v_ref, both_ref, *own_refs):
    rank_rows = u_ref.shape[0]
    member = lax.axis_index("seq") % chunks
    wide_u, wide_v = u_ref.shape[1] // (2 * chunks), v_ref.shape[1] // (2 * chunks)
    for side in range(2):
        half = first_half(paired) ^ side
        place = 0
        for ref, wide in ((u_ref, wide_u), (v_ref, wide_v)):
            rows = []
            for g in range(chunks):
                start = pl.multiple_of(((g ^ member) * 2 + half) * wide, 128)
                rows.append(ref[:, pl.ds(start, wide)].astype(jnp.float32))
            piece = jnp.concatenate(rows, axis=0).astype(both_ref.dtype)
            both_ref[side * PACK : (side + 1) * PACK, place : place + wide] = piece
            if side == 0:
                for own_ref in own_refs:
                    own_ref[:, place : place + wide] = piece
            place += wide


def norm_kernel(seq_dev, lengths_ref, out_hbm, in_hbm, norm_ref, out_ref, in_ref, out_sem, in_sem):
    tok_cap = out_ref.shape[0]
    copies = []
    for piece in range(TOKEN_PIECES):
        for hbm, ref, sem in ((out_hbm, out_ref, out_sem), (in_hbm, in_ref, in_sem)):
            wide = ref.shape[1] // TOKEN_PIECES
            cols = pl.ds(piece * wide, wide)
            copy = pltpu.make_async_copy(hbm.at[:, cols], ref.at[:, cols], sem.at[piece])
            copy.start()
            copies.append((copy, ref, cols))
    grams = [jnp.zeros((tok_cap, tok_cap), jnp.float32) for _ in range(2)]
    for i, (copy, ref, cols) in enumerate(copies):
        copy.wait()
        tokens = ref[:, cols]
        grams[i % 2] = grams[i % 2] + inner_rows(tokens, tokens)
    paired = grams[0] * grams[1]
    ends = sequence_ends(lengths_ref, lax.axis_index("seq"), seq_dev)
    rows = lax.broadcasted_iota(jnp.int32, (tok_cap, 1), 0)
    cols = lax.broadcasted_iota(jnp.int32, (1, tok_cap), 1)
    lanes = lax.broadcasted_iota(jnp.int32, norm_ref.shape, 1)
    norms = jnp.zeros(norm_ref.shape, jnp.float32)
    for k in range(seq_dev):
        by_col = jnp.sum(paired * in_sequence(rows, ends, k), axis=0, keepdims=True)
        value = jnp.sum(by_col * in_sequence(cols, ends, k), axis=1, keepdims=True)
        norms = jnp.where(lanes == k, value / (out_ref.shape[1] * in_ref.shape[1]), norms)
    norm_ref[...] = norms


def swap_groups(value, bit, rank_rows):
    lanes = lax.broadcasted_iota(jnp.int32, (1, value.shape[1]), 1)
    shift = bit * rank_rows
    up = pltpu.roll(value, shift, 1)
    down = pltpu.roll(value, value.shape[1] - shift, 1)
    return jnp.where((lanes // shift) % 2 == 0, down, up)


def project(tokens_ref, half, offset, blocks, chunks, rank_rows, paired):
    wide = tokens_ref.shape[1] // (2 * chunks)
    sets = []
    for first in range(0, len(blocks), chunks):
        sets.append(
            [
                ref[row : row + PACK, offset : offset + wide]
                for ref, row in blocks[first : first + chunks]
            ]
        )
    group = lax.broadcasted_iota(jnp.int32, (PACK, wide), 0) // rank_rows
    result = None
    for j in range(chunks):
        rows = []
        for members in sets:
            merged = members[j]
            for g in range(1, chunks):
                merged = jnp.where(group == g, members[g ^ j], merged)
            rows.append(merged)
        rows = jnp.concatenate(rows, axis=0)
        start = pl.multiple_of(((j ^ turn(paired, chunks)) * 2 + half) * wide, 128)
        part = inner_rows(tokens_ref[:, pl.ds(start, wide)], rows)
        bit = 1
        while bit < chunks:
            if j & bit:
                part = swap_groups(part, bit, rank_rows)
            bit *= 2
        result = part if result is None else result + part
    return result


def both_projections(out_ref, in_ref, half, blocks, rank_rows, paired):
    chunks = PACK // rank_rows
    wide_out = out_ref.shape[1] // (2 * chunks)
    return (
        project(out_ref, half, 0, blocks, chunks, rank_rows, paired),
        project(in_ref, half, wide_out, blocks, chunks, rank_rows, paired),
    )


def partial_kernel(rank_rows, paired, rows, out_ref, in_ref, *refs):
    blocks = [(ref, row) for ref, row in zip(refs, rows)]
    held_ref = refs[len(rows)]
    held_out, held_in = both_projections(
        out_ref, in_ref, first_half(paired), blocks, rank_rows, paired
    )
    held_ref[0] = held_out
    held_ref[1] = held_in


def score_kernel(seq_dev, rank_rows, paired, rows, lengths_ref, norm_ref, held_ref, out_ref, in_ref, *refs):
    blocks = [(ref, row) for ref, row in zip(refs, rows)]
    score_ref = refs[len(rows)]
    tok_cap = out_ref.shape[0]
    held_out, held_in = both_projections(
        out_ref, in_ref, 1 - first_half(paired), blocks, rank_rows, paired
    )
    product = (held_ref[0] + held_out) * (held_ref[1] + held_in)
    me = lax.axis_index("seq")
    lanes = lax.broadcasted_iota(jnp.int32, (1, product.shape[1]), 1)
    source = lanes // rank_rows
    if paired:
        source = source ^ me
    query = (source * rank_rows) // RANK
    ends = sequence_ends(lengths_ref, me, seq_dev)
    positions = lax.broadcasted_iota(jnp.int32, (tok_cap, 1), 0)
    at_query = lax.broadcasted_iota(jnp.int32, score_ref.shape, 0)
    at_seq = lax.broadcasted_iota(jnp.int32, score_ref.shape, 1)
    numerator = jnp.zeros(score_ref.shape, jnp.float32)
    for k in range(seq_dev):
        by_row = jnp.sum(product * in_sequence(positions, ends, k), axis=0, keepdims=True)
        for q in range(score_ref.shape[0]):
            value = jnp.sum(jnp.where(query == q, by_row, 0.0), axis=1, keepdims=True)
            numerator = jnp.where((at_query == q) & (at_seq == k), value, numerator)
    score_ref[...] = numerator / jnp.sqrt(norm_ref[0:1, 0:seq_dev] + EPSILON)


def gather_blocks(both, own, devices):
    def swap(value, mask):
        return lax.ppermute(value, "seq", [(i, i ^ mask) for i in range(devices)])

    def across(value):
        return lax.ppermute(value, "grp", [(0, 1), (1, 0)])

    mine, other = {}, {}
    mine[4] = swap(own, 4)
    mine[8] = swap(own, 8)
    pair_y = swap(both, 2)
    own, mine[4] = lax.optimization_barrier((own, mine[4]))
    mine[12] = swap(own, 12)
    for z in (4, 8, 12):
        other[z] = across(mine[z])
        mine[z + 2] = swap(mine[z], 2)
        other[z + 2] = across(mine[z + 2])
    for held in (mine, other):
        for b in list(held):
            held[b + 1] = swap(held[b], 1)
    for b, value in ((0, both), (2, pair_y)):
        core = swap(value, 1)
        mine[b], other[b] = (value, 0), (value, PACK)
        mine[b + 1], other[b + 1] = (core, 0), (core, PACK)
    plain = lambda item: item if isinstance(item, tuple) else (item, 0)
    return [[plain(held[b]) for b in range(devices)] for held in (mine, other)]


def local(out_grads, layer_inputs, factor_u, factor_v, seq_lengths):
    devices = lax.axis_size("seq")
    paired = devices == 16 and lax.axis_size("grp") == 2
    seq_dev = seq_lengths.shape[0] // devices
    rank_rows = factor_u.shape[0]
    chunks = PACK // rank_rows
    queries = rank_rows * devices // RANK
    tok_cap, width_out = out_grads.shape
    width_in = layer_inputs.shape[1]
    width = width_out + width_in
    smem = pl.BlockSpec(memory_space=pltpu.SMEM)
    vmem = pl.BlockSpec(memory_space=pltpu.VMEM)
    hbm = pl.BlockSpec(memory_space=pl.ANY)
    params = pltpu.CompilerParams(vmem_limit_bytes=24 * 1024 * 1024)

    half_width = width // (2 * chunks)
    packed = pl.pallas_call(
        functools.partial(pack_kernel, chunks, paired),
        out_shape=[jax.ShapeDtypeStruct((2 * PACK, half_width), factor_u.dtype)]
        + [jax.ShapeDtypeStruct((PACK, half_width), factor_u.dtype)] * paired,
        in_specs=[vmem, vmem],
        out_specs=[vmem] * (1 + paired),
        compiler_params=params,
    )(factor_u, factor_v)
    if paired:
        mine, other = gather_blocks(packed[0], packed[1], devices)
    else:
        gathered = lax.all_gather(packed[0], "seq", axis=0, tiled=True)
        mine = [(gathered, 2 * PACK * b) for b in range(devices)]
        other = [(gathered, 2 * PACK * b + PACK) for b in range(devices)]

    norms, out_held, in_held = pl.pallas_call(
        functools.partial(norm_kernel, seq_dev),
        out_shape=[
            jax.ShapeDtypeStruct((8, 128), jnp.float32),
            jax.ShapeDtypeStruct(out_grads.shape, out_grads.dtype),
            jax.ShapeDtypeStruct(layer_inputs.shape, layer_inputs.dtype),
        ],
        in_specs=[smem, hbm, hbm],
        out_specs=[vmem] * 3,
        scratch_shapes=[pltpu.SemaphoreType.DMA((TOKEN_PIECES,))] * 2,
        compiler_params=params,
        cost_estimate=pl.CostEstimate(
            flops=2 * tok_cap * tok_cap * width, bytes_accessed=2 * tok_cap * width, transcendentals=0
        ),
    )(seq_lengths, out_grads, layer_inputs)

    frows = devices * rank_rows
    cost = pl.CostEstimate(
        flops=tok_cap * frows * width, bytes_accessed=(tok_cap + frows) * width, transcendentals=0
    )

    def refs_of(blocks):
        return [vmem] * len(blocks), [a for a, _ in blocks], tuple(row for _, row in blocks)

    specs, arrays, rows = refs_of(mine)
    held = pl.pallas_call(
        functools.partial(partial_kernel, rank_rows, paired, rows),
        out_shape=jax.ShapeDtypeStruct((2, tok_cap, frows), jnp.float32),
        in_specs=[vmem, vmem] + specs,
        out_specs=vmem,
        compiler_params=params,
        cost_estimate=cost,
    )(out_held, in_held, *arrays)
    specs, arrays, rows = refs_of(other)
    return pl.pallas_call(
        functools.partial(score_kernel, seq_dev, rank_rows, paired, rows),
        out_shape=jax.ShapeDtypeStruct((queries, seq_dev), jnp.float32),
        in_specs=[smem, vmem, vmem, vmem, vmem] + specs,
        out_specs=vmem,
        compiler_params=params,
        cost_estimate=cost,
    )(seq_lengths, norms, held, out_held, in_held, *arrays)


def solution(mesh):
    in_specs = (
        P(("grp", "seq"), None),
        P(("grp", "seq"), None),
        P("seq", None),
        P("seq", None),
        P("grp"),
    )
    out_specs = P(None, ("grp", "seq"))
    return jax.shard_map(local, mesh=mesh, in_specs=in_specs, out_specs=out_specs, check_vma=False)
```

time: 63.7 us -> 61.9 us (0.972)
  waiting for transfers between devices: 33 us -> 17.6 us
  starting transfers between devices: 12.2 us -> 24.5 us
  Pallas kernels: 10.8 us -> 12.3 us
    ppermute x15 -> x21, waiting for transfers between devices: 33 us -> 6.44 us  [swap(): return lax.ppermute(value, 'seq', [(i, i ^ mask) for i in range(devices)])]
    ppermute x0 -> x6, waiting for transfers between devices: none -> 11.2 us  [across(): return lax.ppermute(value, 'grp', [(0, 1), (1, 0)])]
    ppermute x0 -> x6, starting transfers between devices: none -> 7.04 us  [across(): return lax.ppermute(value, 'grp', [(0, 1), (1, 0)])]
    ppermute x15 -> x21, starting transfers between devices: 12.2 us -> 17.5 us  [swap(): return lax.ppermute(value, 'seq', [(i, i ^ mask) for i in range(devices)])]
    split x2 -> x0, local copies, waits for them, and re-layouts: 1.78 us -> none  [the longest x1 0.98 us: local(): jnp.split(factor_v, chunks, axis=1)]
    unnamed x6 -> x10, local copies, waits for them, and re-layouts: 5.33 us -> 7.11 us
    pallas_call x2 -> x4, Pallas kernels: 10.8 us -> 12.3 us  [the longest x1 7.2 us: local(): pl.pallas_call(functools.partial(norm_kernel, seq_dev), out_shape=[jax.Sh...]
  transfers between devices with their start and end apart: 15 -> 27, of which waited for: 4 -> 11; matrix products, arithmetic and copies ran while one was open for 0% -> 0% of each run, Pallas kernels for 5% -> 15%
where the time goes in v2:
time: 61.9 us; the launch traced here: 61.6 us
  starting transfers between devices  24.5 us (40%)
  waiting for transfers between devices  17.6 us (28%)
  Pallas kernels  12.3 us (20%)
  local copies, waits for them, and re-layouts  7.11 us (11%)
    ppermute x21, starting transfers between devices, swap(): return lax.ppermute(value, 'seq', [(i, i ^ mask) for i in range(devices)])  17.5 us
    ppermute x6, waiting for transfers between devices, across(): return lax.ppermute(value, 'grp', [(0, 1), (1, 0)])  11.2 us
    pallas_call x1, Pallas kernels, local(): pl.pallas_call(functools.partial(norm_kernel, seq_dev), out_shape=[jax.Sh...  7.2 us
    unnamed x10, local copies, waits for them, and re-layouts  7.11 us
    ppermute x6, starting transfers between devices, across(): return lax.ppermute(value, 'grp', [(0, 1), (1, 0)])  7.04 us
    ppermute x21, waiting for transfers between devices, swap(): return lax.ppermute(value, 'seq', [(i, i ^ mask) for i in range(devices)])  6.44 us
    pallas_call x1, Pallas kernels, local(): pl.pallas_call(functools.partial(score_kernel, seq_dev, rank_rows, paired...  3.08 us
    pallas_call x1, Pallas kernels, local(): pl.pallas_call(functools.partial(partial_kernel, rank_rows, paired, rows)...  1.9 us
  transfers between devices with their start and end apart: 27, of which 11 were waited for; matrix products, arithmetic and copies ran while one was open for 0% of the time, Pallas kernels for 15%

profile of v2, /device:TPU:0, one launch (start us, length us, event | category | flops | bytes accessed | tf_op | source)
XLA Modules:
  0.0 61.6 jit_solution(7108072645426223860)
XLA Ops:
  0.0 0.9 %copy-done.2 = bf16[4,28672]{1,0:T(4,128)(2,1)S(1)} copy-done((bf16[4,28672]{1,0:T(4,128)(2,1)S(1)}, bf16[4,28672]{1,0:T(4,128)(2,1)}, u32[]{:S(2)}) %copy-start.2) | copy-done | bytes 229400
  2.4 2.6 %collective-permute-start.3 = (bf16[16,4608]{1,0:T(8,128)(2,1)S(1)}, bf16[16,4608]{1,0:T(8,128)(2,1)S(1)}, u32[]{:S(2)}, u32[]{:S(2)}) collective-permute-start(bf16[16,4608]{1,0:T(8,128)(2,1)S(1)} %get-tuple-element.18), channel_id=1, source_target_pairs={{0,4},{1,5},{2,6},{3,7},{4,0},{5,1},{6,2},{7,3},{8,12},{9,13},{10,... | collective-permute-start | bytes 442376 | tf_op jit(solution)/shard_map/ppermute | solution.py:178
  5.0 1.5 %collective-permute-start.1 = (bf16[32,4608]{1,0:T(8,128)(2,1)S(1)}, bf16[32,4608]{1,0:T(8,128)(2,1)S(1)}, u32[]{:S(2)}, u32[]{:S(2)}) collective-permute-start(bf16[32,4608]{1,0:T(8,128)(2,1)S(1)} %get-tuple-element.15.refs_0_), channel_id=1, source_target_pairs={{0,2},{1,3},{2,0},{3,1},{4,6},{5,7},{6,4},{7,5},{8,10},{9,11},{10,... | collective-permute-start | bytes 884744 | tf_op jit(solution)/shard_map/ppermute | solution.py:178
  6.5 2.6 %collective-permute-start.7 = (bf16[16,4608]{1,0:T(8,128)(2,1)S(1)}, bf16[16,4608]{1,0:T(8,128)(2,1)S(1)}, u32[]{:S(2)}, u32[]{:S(2)}) collective-permute-start(bf16[16,4608]{1,0:T(8,128)(2,1)S(1)} %get-tuple-element.18), channel_id=1, source_target_pairs={{0,8},{1,9},{2,10},{3,11},{4,12},{5,13},{6,14},{7,15},{8,0},{9,1},... | collective-permute-start | bytes 442376 | tf_op jit(solution)/shard_map/ppermute | solution.py:178
  9.5 4.5 %collective-permute-start.5 = (bf16[16,4608]{1,0:T(8,128)(2,1)S(1)}, bf16[16,4608]{1,0:T(8,128)(2,1)S(1)}, u32[]{:S(2)}, u32[]{:S(2)}) collective-permute-start(bf16[16,4608]{1,0:T(8,128)(2,1)S(1)} %collective-permute-done.3.refs_4_), channel_id=1, source_target_pairs={{0,2},{1,3},{2,0},{3,1},{4,6},{5,7},{6,4},{7,5},{8,10},{9,11},{10,... | collective-permute-start | bytes 442376 | tf_op jit(solution)/shard_map/ppermute | solution.py:178
  14.0 2.3 %collective-permute-done.7.refs_8_ = bf16[16,4608]{1,0:T(8,128)(2,1)S(1)} collective-permute-done((bf16[16,4608]{1,0:T(8,128)(2,1)S(1)}, bf16[16,4608]{1,0:T(8,128)(2,1)S(1)}, u32[]{:S(2)}, u32[]{:S(2)}) %collective-permute-start.7) | collective-permute-done | bytes 147488 | tf_op jit(solution)/shard_map/ppermute | solution.py:178
  16.8 2.5 %collective-permute-start.11 = (bf16[16,4608]{1,0:T(8,128)(2,1)S(1)}, bf16[16,4608]{1,0:T(8,128)(2,1)S(1)}, u32[]{:S(2)}, u32[]{:S(2)}) collective-permute-start(bf16[16,4608]{1,0:T(8,128)(2,1)S(1)} %get-tuple-element.18), channel_id=1, source_target_pairs={{0,12},{1,13},{2,14},{3,15},{4,8},{5,9},{6,10},{7,11},{8,4},{9,5},... | collective-permute-start | bytes 442376 | tf_op jit(solution)/shard_map/ppermute | solution.py:178
  19.3 1.5 %collective-permute-start.15 = (bf16[16,4608]{1,0:T(8,128)(2,1)S(1)}, bf16[16,4608]{1,0:T(8,128)(2,1)S(1)}, u32[]{:S(2)}, u32[]{:S(2)}) collective-permute-start(bf16[16,4608]{1,0:T(8,128)(2,1)S(1)} %collective-permute-done.3.refs_4_), channel_id=1, source_target_pairs={{0,16},{16,0},{1,17},{17,1},{2,18},{18,2},{3,19},{19,3},{4,20},{20... | collective-permute-start | bytes 442376 | tf_op jit(solution)/shard_map/ppermute | solution.py:181
  21.3 1.2 %collective-permute-done.9.refs_10_ = bf16[16,4608]{1,0:T(8,128)(2,1)S(1)} collective-permute-done((bf16[16,4608]{1,0:T(8,128)(2,1)S(1)}, bf16[16,4608]{1,0:T(8,128)(2,1)S(1)}, u32[]{:S(2)}, u32[]{:S(2)}) %collective-permute-start.9) | collective-permute-done | bytes 147488 | tf_op jit(solution)/shard_map/ppermute | solution.py:178
  22.5 2.2 %collective-permute-done.11.refs_12_ = bf16[16,4608]{1,0:T(8,128)(2,1)S(1)} collective-permute-done((bf16[16,4608]{1,0:T(8,128)(2,1)S(1)}, bf16[16,4608]{1,0:T(8,128)(2,1)S(1)}, u32[]{:S(2)}, u32[]{:S(2)}) %collective-permute-start.11) | collective-permute-done | bytes 147488 | tf_op jit(solution)/shard_map/ppermute | solution.py:178
  24.7 1.3 %collective-permute-done.15.refs_4_ = bf16[16,4608]{1,0:T(8,128)(2,1)S(1)} collective-permute-done((bf16[16,4608]{1,0:T(8,128)(2,1)S(1)}, bf16[16,4608]{1,0:T(8,128)(2,1)S(1)}, u32[]{:S(2)}, u32[]{:S(2)}) %collective-permute-start.15) | collective-permute-done | bytes 147488 | tf_op jit(solution)/shard_map/ppermute | solution.py:181
  26.0 1.5 %collective-permute-start.13 = (bf16[16,4608]{1,0:T(8,128)(2,1)S(1)}, bf16[16,4608]{1,0:T(8,128)(2,1)S(1)}, u32[]{:S(2)}, u32[]{:S(2)}) collective-permute-start(bf16[16,4608]{1,0:T(8,128)(2,1)S(1)} %collective-permute-done.11.refs_12_), channel_id=1, source_target_pairs={{0,2},{1,3},{2,0},{3,1},{4,6},{5,7},{6,4},{7,5},{8,10},{9,11},{10,... | collective-permute-start | bytes 442376 | tf_op jit(solution)/shard_map/ppermute | solution.py:178
  28.7 1.5 %collective-permute-start.17 = (bf16[16,4608]{1,0:T(8,128)(2,1)S(1)}, bf16[16,4608]{1,0:T(8,128)(2,1)S(1)}, u32[]{:S(2)}, u32[]{:S(2)}) collective-permute-start(bf16[16,4608]{1,0:T(8,128)(2,1)S(1)} %collective-permute-done.5.refs_6_), channel_id=1, source_target_pairs={{0,16},{16,0},{1,17},{17,1},{2,18},{18,2},{3,19},{19,3},{4,20},{20... | collective-permute-start | bytes 442376 | tf_op jit(solution)/shard_map/ppermute | solution.py:181
  31.1 1.5 %collective-permute-start.23 = (bf16[16,4608]{1,0:T(8,128)(2,1)S(1)}, bf16[16,4608]{1,0:T(8,128)(2,1)S(1)}, u32[]{:S(2)}, u32[]{:S(2)}) collective-permute-start(bf16[16,4608]{1,0:T(8,128)(2,1)S(1)} %collective-permute-done.11.refs_12_), channel_id=1, source_target_pairs={{0,16},{16,0},{1,17},{17,1},{2,18},{18,2},{3,19},{19,3},{4,20},{20... | collective-permute-start | bytes 442376 | tf_op jit(solution)/shard_map/ppermute | solution.py:181
  32.6 2.7 %collective-permute-done.17.refs_6_ = bf16[16,4608]{1,0:T(8,128)(2,1)S(1)} collective-permute-done((bf16[16,4608]{1,0:T(8,128)(2,1)S(1)}, bf16[16,4608]{1,0:T(8,128)(2,1)S(1)}, u32[]{:S(2)}, u32[]{:S(2)}) %collective-permute-start.17) | collective-permute-done | bytes 147488 | tf_op jit(solution)/shard_map/ppermute | solution.py:181
  35.4 1.5 %collective-permute-start.25 = (bf16[16,4608]{1,0:T(8,128)(2,1)S(1)}, bf16[16,4608]{1,0:T(8,128)(2,1)S(1)}, u32[]{:S(2)}, u32[]{:S(2)}) collective-permute-start(bf16[16,4608]{1,0:T(8,128)(2,1)S(1)} %collective-permute-done.13.refs_14_), channel_id=1, source_target_pairs={{0,16},{16,0},{1,17},{17,1},{2,18},{18,2},{3,19},{19,3},{4,20},{20... | collective-permute-start | bytes 442376 | tf_op jit(solution)/shard_map/ppermute | solution.py:181
  36.9 1.7 %collective-permute-done.21.refs_10_ = bf16[16,4608]{1,0:T(8,128)(2,1)S(1)} collective-permute-done((bf16[16,4608]{1,0:T(8,128)(2,1)S(1)}, bf16[16,4608]{1,0:T(8,128)(2,1)S(1)}, u32[]{:S(2)}, u32[]{:S(2)}) %collective-permute-start.21) | collective-permute-done | bytes 147488 | tf_op jit(solution)/shard_map/ppermute | solution.py:181
  38.5 3.2 %collective-permute-done.23.refs_12_ = bf16[16,4608]{1,0:T(8,128)(2,1)S(1)} collective-permute-done((bf16[16,4608]{1,0:T(8,128)(2,1)S(1)}, bf16[16,4608]{1,0:T(8,128)(2,1)S(1)}, u32[]{:S(2)}, u32[]{:S(2)}) %collective-permute-start.23) | collective-permute-done | bytes 147488 | tf_op jit(solution)/shard_map/ppermute | solution.py:181
  42.3 1.7 %collective-permute-done.25.refs_14_ = bf16[16,4608]{1,0:T(8,128)(2,1)S(1)} collective-permute-done((bf16[16,4608]{1,0:T(8,128)(2,1)S(1)}, bf16[16,4608]{1,0:T(8,128)(2,1)S(1)}, u32[]{:S(2)}, u32[]{:S(2)}) %collective-permute-start.25) | collective-permute-done | bytes 147488 | tf_op jit(solution)/shard_map/ppermute | solution.py:181
  44.0 3.1 %copy-done = bf16[128,28672]{1,0:T(8,128)(2,1)S(1)} copy-done((bf16[128,28672]{1,0:T(8,128)(2,1)S(1)}, bf16[128,28672]{1,0:T(8,128)(2,1)}, u32[]{:S(2)}) %copy-start) | copy-done | bytes 7340056
  47.1 1.6 %copy-done.1 = bf16[128,8192]{1,0:T(8,128)(2,1)S(1)} copy-done((bf16[128,8192]{1,0:T(8,128)(2,1)S(1)}, bf16[128,8192]{1,0:T(8,128)(2,1)}, u32[]{:S(2)}) %copy-start.1) | copy-done | bytes 2097176
  49.3 7.2 %shard_map.55 = (f32[8,128]{1,0:T(8,128)S(1)}, bf16[128,8192]{1,0:T(8,128)(2,1)S(1)}, bf16[128,28672]{1,0:T(8,128)(2,1)S(1)}) custom-call(s32[64]{0:T(128)S(1)} %copy-done.4, bf16[128,8192]{1,0:T(8,128)(2,1)S(1)} %copy-done.1, bf16[128,28672]{1,0:T(8,128)(2,1)S(1)} %copy-done), custom_call_target="tpu_custom_call" | custom-call | flops 1207959552 | bytes 9437184 | tf_op jit(solution)/shard_map/pallas_call | solution.py:235
  56.5 1.9 %shard_map.57.held_ref = f32[2,128,64]{2,1,0:T(8,128)S(1)} custom-call(bf16[128,8192]{1,0:T(8,128)(2,1)S(1)} %get-tuple-element.13.out_ref, bf16[128,28672]{1,0:T(8,128)(2,1)S(1)} %get-tuple-element.14.in_ref, bf16[32,4608]{1,0:T(8,128)(2,1)S(1)} %get-tuple-element.15.refs_0_, bf16[32,4608]{1,0:T(8,128)(2,1)S(1)} %collective-permute-done.refs_1_, ...), custom_call_target="tpu_custom_call" | custom-call | flops 301989888 | bytes 7077888 | tf_op jit(solution)/shard_map/pallas_call | solution.py:260
  58.5 3.1 %shard_map.58 = f32[2,4]{1,0:T(2,128)} custom-call(s32[64]{0:T(128)S(1)} %copy-done.4, f32[8,128]{1,0:T(8,128)S(1)} %get-tuple-element.12.norm_ref, f32[2,128,64]{2,1,0:T(8,128)S(1)} %shard_map.57.held_ref, bf16[128,8192]{1,0:T(8,128)(2,1)S(1)} %get-tuple-element.13.out_ref, bf16[128,28672]{1,0:T(8,128)(2,1)S(1)} %get-tuple-element.14.in_ref, ...), custom_call_target="tpu_custom_call" | custom-call | flops 301989888 | bytes 7077888 | tf_op jit(solution)/shard_map/pallas_call | solution.py:269
  (44 shorter events, 6.3 us)
Async XLA Ops:
  1.9 14.4 %collective-permute-start = (bf16[32,4608]{1,0:T(8,128)(2,1)S(1)}, bf16[32,4608]{1,0:T(8,128)(2,1)S(1)}, u32[]{:S(2)}, u32[]{:S(2)}) collective-permute-start(bf16[32,4608]{1,0:T(8,128)(2,1)S(1)} %get-tuple-element.15.refs_0_), channel_id=1, source_target_pairs={{0,1},{1,0},{2,3},{3,2},{4,5},{5,4},{6,7},{7,6},{8,9},{9,8},{10,11... | collective-permute-start | bytes 884744 | tf_op jit(solution)/shard_map/ppermute | solution.py:178
  2.4 7.1 %collective-permute-start.3 = (bf16[16,4608]{1,0:T(8,128)(2,1)S(1)}, bf16[16,4608]{1,0:T(8,128)(2,1)S(1)}, u32[]{:S(2)}, u32[]{:S(2)}) collective-permute-start(bf16[16,4608]{1,0:T(8,128)(2,1)S(1)} %get-tuple-element.18), channel_id=1, source_target_pairs={{0,4},{1,5},{2,6},{3,7},{4,0},{5,1},{6,2},{7,3},{8,12},{9,13},{10,... | collective-permute-start | bytes 442376 | tf_op jit(solution)/shard_map/ppermute | solution.py:178
  5.0 11.8 %collective-permute-start.1 = (bf16[32,4608]{1,0:T(8,128)(2,1)S(1)}, bf16[32,4608]{1,0:T(8,128)(2,1)S(1)}, u32[]{:S(2)}, u32[]{:S(2)}) collective-permute-start(bf16[32,4608]{1,0:T(8,128)(2,1)S(1)} %get-tuple-element.15.refs_0_), channel_id=1, source_target_pairs={{0,2},{1,3},{2,0},{3,1},{4,6},{5,7},{6,4},{7,5},{8,10},{9,11},{10,... | collective-permute-start | bytes 884744 | tf_op jit(solution)/shard_map/ppermute | solution.py:178
  6.5 9.7 %collective-permute-start.7 = (bf16[16,4608]{1,0:T(8,128)(2,1)S(1)}, bf16[16,4608]{1,0:T(8,128)(2,1)S(1)}, u32[]{:S(2)}, u32[]{:S(2)}) collective-permute-start(bf16[16,4608]{1,0:T(8,128)(2,1)S(1)} %get-tuple-element.18), channel_id=1, source_target_pairs={{0,8},{1,9},{2,10},{3,11},{4,12},{5,13},{6,14},{7,15},{8,0},{9,1},... | collective-permute-start | bytes 442376 | tf_op jit(solution)/shard_map/ppermute | solution.py:178
  9.5 9.8 %collective-permute-start.4 = (bf16[16,4608]{1,0:T(8,128)(2,1)S(1)}, bf16[16,4608]{1,0:T(8,128)(2,1)S(1)}, u32[]{:S(2)}, u32[]{:S(2)}) collective-permute-start(bf16[16,4608]{1,0:T(8,128)(2,1)S(1)} %collective-permute-done.3.refs_4_), channel_id=1, source_target_pairs={{0,1},{1,0},{2,3},{3,2},{4,5},{5,4},{6,7},{7,6},{8,9},{9,8},{10,11... | collective-permute-start | bytes 442376 | tf_op jit(solution)/shard_map/ppermute | solution.py:178
  9.5 11.3 %collective-permute-start.5 = (bf16[16,4608]{1,0:T(8,128)(2,1)S(1)}, bf16[16,4608]{1,0:T(8,128)(2,1)S(1)}, u32[]{:S(2)}, u32[]{:S(2)}) collective-permute-start(bf16[16,4608]{1,0:T(8,128)(2,1)S(1)} %collective-permute-done.3.refs_4_), channel_id=1, source_target_pairs={{0,2},{1,3},{2,0},{3,1},{4,6},{5,7},{6,4},{7,5},{8,10},{9,11},{10,... | collective-permute-start | bytes 442376 | tf_op jit(solution)/shard_map/ppermute | solution.py:178
  16.2 6.3 %collective-permute-start.9 = (bf16[16,4608]{1,0:T(8,128)(2,1)S(1)}, bf16[16,4608]{1,0:T(8,128)(2,1)S(1)}, u32[]{:S(2)}, u32[]{:S(2)}) collective-permute-start(bf16[16,4608]{1,0:T(8,128)(2,1)S(1)} %collective-permute-done.7.refs_8_), channel_id=1, source_target_pairs={{0,2},{1,3},{2,0},{3,1},{4,6},{5,7},{6,4},{7,5},{8,10},{9,11},{10,... | collective-permute-start | bytes 442376 | tf_op jit(solution)/shard_map/ppermute | solution.py:178
  16.8 7.9 %collective-permute-start.11 = (bf16[16,4608]{1,0:T(8,128)(2,1)S(1)}, bf16[16,4608]{1,0:T(8,128)(2,1)S(1)}, u32[]{:S(2)}, u32[]{:S(2)}) collective-permute-start(bf16[16,4608]{1,0:T(8,128)(2,1)S(1)} %get-tuple-element.18), channel_id=1, source_target_pairs={{0,12},{1,13},{2,14},{3,15},{4,8},{5,9},{6,10},{7,11},{8,4},{9,5},... | collective-permute-start | bytes 442376 | tf_op jit(solution)/shard_map/ppermute | solution.py:178
  19.3 6.7 %collective-permute-start.15 = (bf16[16,4608]{1,0:T(8,128)(2,1)S(1)}, bf16[16,4608]{1,0:T(8,128)(2,1)S(1)}, u32[]{:S(2)}, u32[]{:S(2)}) collective-permute-start(bf16[16,4608]{1,0:T(8,128)(2,1)S(1)} %collective-permute-done.3.refs_4_), channel_id=1, source_target_pairs={{0,16},{16,0},{1,17},{17,1},{2,18},{18,2},{3,19},{19,3},{4,20},{20... | collective-permute-start | bytes 442376 | tf_op jit(solution)/shard_map/ppermute | solution.py:181
  20.8 7.4 %collective-permute-start.19 = (bf16[16,4608]{1,0:T(8,128)(2,1)S(1)}, bf16[16,4608]{1,0:T(8,128)(2,1)S(1)}, u32[]{:S(2)}, u32[]{:S(2)}) collective-permute-start(bf16[16,4608]{1,0:T(8,128)(2,1)S(1)} %collective-permute-done.7.refs_8_), channel_id=1, source_target_pairs={{0,16},{16,0},{1,17},{17,1},{2,18},{18,2},{3,19},{19,3},{4,20},{20... | collective-permute-start | bytes 442376 | tf_op jit(solution)/shard_map/ppermute | solution.py:181
  21.3 6.8 %collective-permute-start.6 = (bf16[16,4608]{1,0:T(8,128)(2,1)S(1)}, bf16[16,4608]{1,0:T(8,128)(2,1)S(1)}, u32[]{:S(2)}, u32[]{:S(2)}) collective-permute-start(bf16[16,4608]{1,0:T(8,128)(2,1)S(1)} %collective-permute-done.5.refs_6_), channel_id=1, source_target_pairs={{0,1},{1,0},{2,3},{3,2},{4,5},{5,4},{6,7},{7,6},{8,9},{9,8},{10,11... | collective-permute-start | bytes 442376 | tf_op jit(solution)/shard_map/ppermute | solution.py:178
  22.5 6.2 %collective-permute-start.10 = (bf16[16,4608]{1,0:T(8,128)(2,1)S(1)}, bf16[16,4608]{1,0:T(8,128)(2,1)S(1)}, u32[]{:S(2)}, u32[]{:S(2)}) collective-permute-start(bf16[16,4608]{1,0:T(8,128)(2,1)S(1)} %collective-permute-done.9.refs_10_), channel_id=1, source_target_pairs={{0,1},{1,0},{2,3},{3,2},{4,5},{5,4},{6,7},{7,6},{8,9},{9,8},{10,11... | collective-permute-start | bytes 442376 | tf_op jit(solution)/shard_map/ppermute | solution.py:178
  24.7 5.5 %collective-permute-start.12 = (bf16[16,4608]{1,0:T(8,128)(2,1)S(1)}, bf16[16,4608]{1,0:T(8,128)(2,1)S(1)}, u32[]{:S(2)}, u32[]{:S(2)}) collective-permute-start(bf16[16,4608]{1,0:T(8,128)(2,1)S(1)} %collective-permute-done.11.refs_12_), channel_id=1, source_target_pairs={{0,1},{1,0},{2,3},{3,2},{4,5},{5,4},{6,7},{7,6},{8,9},{9,8},{10,11... | collective-permute-start | bytes 442376 | tf_op jit(solution)/shard_map/ppermute | solution.py:178
  28.1 13.6 %collective-permute-start.2 = (bf16[32,4608]{1,0:T(8,128)(2,1)S(1)}, bf16[32,4608]{1,0:T(8,128)(2,1)S(1)}, u32[]{:S(2)}, u32[]{:S(2)}) collective-permute-start(bf16[32,4608]{1,0:T(8,128)(2,1)S(1)} %collective-permute-done.1.refs_2_), channel_id=1, source_target_pairs={{0,1},{1,0},{2,3},{3,2},{4,5},{5,4},{6,7},{7,6},{8,9},{9,8},{10,11... | collective-permute-start | bytes 884744 | tf_op jit(solution)/shard_map/ppermute | solution.py:178
  28.7 6.7 %collective-permute-start.17 = (bf16[16,4608]{1,0:T(8,128)(2,1)S(1)}, bf16[16,4608]{1,0:T(8,128)(2,1)S(1)}, u32[]{:S(2)}, u32[]{:S(2)}) collective-permute-start(bf16[16,4608]{1,0:T(8,128)(2,1)S(1)} %collective-permute-done.5.refs_6_), channel_id=1, source_target_pairs={{0,16},{16,0},{1,17},{17,1},{2,18},{18,2},{3,19},{19,3},{4,20},{20... | collective-permute-start | bytes 442376 | tf_op jit(solution)/shard_map/ppermute | solution.py:181
  30.2 8.4 %collective-permute-start.21 = (bf16[16,4608]{1,0:T(8,128)(2,1)S(1)}, bf16[16,4608]{1,0:T(8,128)(2,1)S(1)}, u32[]{:S(2)}, u32[]{:S(2)}) collective-permute-start(bf16[16,4608]{1,0:T(8,128)(2,1)S(1)} %collective-permute-done.9.refs_10_), channel_id=1, source_target_pairs={{0,16},{16,0},{1,17},{17,1},{2,18},{18,2},{3,19},{19,3},{4,20},{20... | collective-permute-start | bytes 442376 | tf_op jit(solution)/shard_map/ppermute | solution.py:181
  31.1 10.5 %collective-permute-start.23 = (bf16[16,4608]{1,0:T(8,128)(2,1)S(1)}, bf16[16,4608]{1,0:T(8,128)(2,1)S(1)}, u32[]{:S(2)}, u32[]{:S(2)}) collective-permute-start(bf16[16,4608]{1,0:T(8,128)(2,1)S(1)} %collective-permute-done.11.refs_12_), channel_id=1, source_target_pairs={{0,16},{16,0},{1,17},{17,1},{2,18},{18,2},{3,19},{19,3},{4,20},{20... | collective-permute-start | bytes 442376 | tf_op jit(solution)/shard_map/ppermute | solution.py:181
  32.6 9.6 %collective-permute-start.14 = (bf16[16,4608]{1,0:T(8,128)(2,1)S(1)}, bf16[16,4608]{1,0:T(8,128)(2,1)S(1)}, u32[]{:S(2)}, u32[]{:S(2)}) collective-permute-start(bf16[16,4608]{1,0:T(8,128)(2,1)S(1)} %collective-permute-done.13.refs_14_), channel_id=1, source_target_pairs={{0,1},{1,0},{2,3},{3,2},{4,5},{5,4},{6,7},{7,6},{8,9},{9,8},{10,11... | collective-permute-start | bytes 442376 | tf_op jit(solution)/shard_map/ppermute | solution.py:178
  35.4 8.6 %collective-permute-start.25 = (bf16[16,4608]{1,0:T(8,128)(2,1)S(1)}, bf16[16,4608]{1,0:T(8,128)(2,1)S(1)}, u32[]{:S(2)}, u32[]{:S(2)}) collective-permute-start(bf16[16,4608]{1,0:T(8,128)(2,1)S(1)} %collective-permute-done.13.refs_14_), channel_id=1, source_target_pairs={{0,16},{16,0},{1,17},{17,1},{2,18},{18,2},{3,19},{19,3},{4,20},{20... | collective-permute-start | bytes 442376 | tf_op jit(solution)/shard_map/ppermute | solution.py:181
  38.5 19.9 %collective-permute-start.20 = (bf16[16,4608]{1,0:T(8,128)(2,1)S(1)}, bf16[16,4608]{1,0:T(8,128)(2,1)S(1)}, u32[]{:S(2)}, u32[]{:S(2)}) collective-permute-start(bf16[16,4608]{1,0:T(8,128)(2,1)S(1)} %collective-permute-done.19.refs_8_), channel_id=1, source_target_pairs={{0,1},{1,0},{2,3},{3,2},{4,5},{5,4},{6,7},{7,6},{8,9},{9,8},{10,11... | collective-permute-start | bytes 442376 | tf_op jit(solution)/shard_map/ppermute | solution.py:178
  41.7 16.7 %collective-permute-start.18 = (bf16[16,4608]{1,0:T(8,128)(2,1)S(1)}, bf16[16,4608]{1,0:T(8,128)(2,1)S(1)}, u32[]{:S(2)}, u32[]{:S(2)}) collective-permute-start(bf16[16,4608]{1,0:T(8,128)(2,1)S(1)} %collective-permute-done.17.refs_6_), channel_id=1, source_target_pairs={{0,1},{1,0},{2,3},{3,2},{4,5},{5,4},{6,7},{7,6},{8,9},{9,8},{10,11... | collective-permute-start | bytes 442376 | tf_op jit(solution)/shard_map/ppermute | solution.py:178
  41.7 16.7 %collective-permute-start.22 = (bf16[16,4608]{1,0:T(8,128)(2,1)S(1)}, bf16[16,4608]{1,0:T(8,128)(2,1)S(1)}, u32[]{:S(2)}, u32[]{:S(2)}) collective-permute-start(bf16[16,4608]{1,0:T(8,128)(2,1)S(1)} %collective-permute-done.21.refs_10_), channel_id=1, source_target_pairs={{0,1},{1,0},{2,3},{3,2},{4,5},{5,4},{6,7},{7,6},{8,9},{9,8},{10,11... | collective-permute-start | bytes 442376 | tf_op jit(solution)/shard_map/ppermute | solution.py:178
  42.2 16.2 %collective-permute-start.24 = (bf16[16,4608]{1,0:T(8,128)(2,1)S(1)}, bf16[16,4608]{1,0:T(8,128)(2,1)S(1)}, u32[]{:S(2)}, u32[]{:S(2)}) collective-permute-start(bf16[16,4608]{1,0:T(8,128)(2,1)S(1)} %collective-permute-done.23.refs_12_), channel_id=1, source_target_pairs={{0,1},{1,0},{2,3},{3,2},{4,5},{5,4},{6,7},{7,6},{8,9},{9,8},{10,11... | collective-permute-start | bytes 442376 | tf_op jit(solution)/shard_map/ppermute | solution.py:178
  44.0 14.5 %collective-permute-start.26 = (bf16[16,4608]{1,0:T(8,128)(2,1)S(1)}, bf16[16,4608]{1,0:T(8,128)(2,1)S(1)}, u32[]{:S(2)}, u32[]{:S(2)}) collective-permute-start(bf16[16,4608]{1,0:T(8,128)(2,1)S(1)} %collective-permute-done.25.refs_14_), channel_id=1, source_target_pairs={{0,1},{1,0},{2,3},{3,2},{4,5},{5,4},{6,7},{7,6},{8,9},{9,8},{10,11... | collective-permute-start | bytes 442376 | tf_op jit(solution)/shard_map/ppermute | solution.py:178
  (8 other events, 21.8 us)

commit v3 on v2

v3 whole, which is shorter than its diff:
```python
import functools

import jax
import jax.numpy as jnp
from jax import lax
from jax.experimental import pallas as pl
from jax.experimental.pallas import tpu as pltpu
from jax.sharding import PartitionSpec as P

RANK = 32
EPSILON = 1e-06
PACK = 16
SCORE_VMEM = 24 * 1024 * 1024
PACK_VMEM = 58 * 1024 * 1024

NT = (((1,), (1,)), ((), ()))


def inner_rows(left, right):
    return lax.dot_general(left, right, NT, preferred_element_type=jnp.float32)


def sequence_ends(lengths_ref, block, seq_dev):
    ends, total = [], 0
    for k in range(seq_dev):
        total = total + lengths_ref[block * seq_dev + k]
        ends.append(total)
    return ends


def in_sequence(positions, ends, k):
    low = 0 if k == 0 else ends[k - 1]
    return ((positions >= low) & (positions < ends[k])).astype(jnp.float32)


def first_half(paired):
    return lax.axis_index("grp") % 2 if paired else 0


def turn(paired, chunks):
    return lax.axis_index("seq") % chunks if paired else 0


def pack_kernel(chunks, paired, u_hbm, v_hbm, both_ref, *refs):
    *own_refs, u_ref, v_ref, sems = refs
    copies = [
        pltpu.make_async_copy(u_hbm, u_ref, sems.at[0]),
        pltpu.make_async_copy(v_hbm, v_ref, sems.at[1]),
    ]
    for copy in copies:
        copy.start()
    for copy in copies:
        copy.wait()
    rank_rows = u_ref.shape[0]
    member = lax.axis_index("seq") % chunks
    wide_u, wide_v = u_ref.shape[1] // (2 * chunks), v_ref.shape[1] // (2 * chunks)
    for side in range(2):
        half = first_half(paired) ^ side
        place = 0
        for ref, wide in ((u_ref, wide_u), (v_ref, wide_v)):
            rows = []
            for g in range(chunks):
                start = pl.multiple_of(((g ^ member) * 2 + half) * wide, 128)
                rows.append(ref[:, pl.ds(start, wide)].astype(jnp.float32))
            piece = jnp.concatenate(rows, axis=0).astype(both_ref.dtype)
            both_ref[side * PACK : (side + 1) * PACK, place : place + wide] = piece
            if side == 0:
                for own_ref in own_refs:
                    own_ref[:, place : place + wide] = piece
            place += wide


def norm_kernel(seq_dev, lengths_ref, out_ref, in_ref, norm_ref):
    tok_cap = out_ref.shape[0]
    gram_out = inner_rows(out_ref[...], out_ref[...])
    paired = gram_out * inner_rows(in_ref[...], in_ref[...])
    ends = sequence_ends(lengths_ref, lax.axis_index("seq"), seq_dev)
    rows = lax.broadcasted_iota(jnp.int32, (tok_cap, 1), 0)
    cols = lax.broadcasted_iota(jnp.int32, (1, tok_cap), 1)
    lanes = lax.broadcasted_iota(jnp.int32, norm_ref.shape, 1)
    norms = jnp.zeros(norm_ref.shape, jnp.float32)
    for k in range(seq_dev):
        by_col = jnp.sum(paired * in_sequence(rows, ends, k), axis=0, keepdims=True)
        value = jnp.sum(by_col * in_sequence(cols, ends, k), axis=1, keepdims=True)
        norms = jnp.where(lanes == k, value / (out_ref.shape[1] * in_ref.shape[1]), norms)
    norm_ref[...] = norms


def swap_groups(value, bit, rank_rows):
    lanes = lax.broadcasted_iota(jnp.int32, (1, value.shape[1]), 1)
    shift = bit * rank_rows
    up = pltpu.roll(value, shift, 1)
    down = pltpu.roll(value, value.shape[1] - shift, 1)
    return jnp.where((lanes // shift) % 2 == 0, down, up)


def merged_rows(blocks, offset, wide, j, chunks, rank_rows):
    group = lax.broadcasted_iota(jnp.int32, (PACK, wide), 0) // rank_rows
    rows = []
    for first in range(0, len(blocks), chunks):
        merged = None
        for g in range(chunks):
            ref, row = blocks[first + (g ^ j)]
            piece = ref[row : row + PACK, offset : offset + wide]
            merged = piece if merged is None else jnp.where(group == g, piece, merged)
        rows.append(merged)
    return jnp.concatenate(rows, axis=0)


def both_projections(out_ref, in_ref, half, blocks, rank_rows, paired):
    chunks = PACK // rank_rows
    results, offset = [], 0
    for ref in (out_ref, in_ref):
        wide = ref.shape[1] // (2 * chunks)
        result = None
        for j in range(chunks):
            rows = merged_rows(blocks, offset, wide, j, chunks, rank_rows)
            start = pl.multiple_of(((j ^ turn(paired, chunks)) * 2 + half) * wide, 128)
            part = inner_rows(ref[:, pl.ds(start, wide)], rows)
            bit = 1
            while bit < chunks:
                if j & bit:
                    part = swap_groups(part, bit, rank_rows)
                bit *= 2
            result = part if result is None else result + part
        results.append(result)
        offset += wide
    return results


def partial_kernel(rank_rows, paired, places, out_ref, in_ref, *refs):
    *array_refs, held_ref = refs
    blocks = [(array_refs[i], row) for i, row in places]
    half = first_half(paired)
    held_out, held_in = both_projections(
        out_ref, in_ref, half, blocks, rank_rows, paired
    )
    held_ref[0] = held_out
    held_ref[1] = held_in


def score_kernel(seq_dev, rank_rows, paired, places, lengths_ref, norm_ref, held_ref, out_ref, in_ref, *refs):
    *array_refs, score_ref = refs
    blocks = [(array_refs[i], row) for i, row in places]
    tok_cap = out_ref.shape[0]
    half = 1 - first_half(paired)
    held_out, held_in = both_projections(
        out_ref, in_ref, half, blocks, rank_rows, paired
    )
    product = (held_ref[0] + held_out) * (held_ref[1] + held_in)
    me = lax.axis_index("seq")
    lanes = lax.broadcasted_iota(jnp.int32, (1, product.shape[1]), 1)
    source = lanes // rank_rows
    if paired:
        source = source ^ me
    query = (source * rank_rows) // RANK
    ends = sequence_ends(lengths_ref, me, seq_dev)
    positions = lax.broadcasted_iota(jnp.int32, (tok_cap, 1), 0)
    at_query = lax.broadcasted_iota(jnp.int32, score_ref.shape, 0)
    at_seq = lax.broadcasted_iota(jnp.int32, score_ref.shape, 1)
    numerator = jnp.zeros(score_ref.shape, jnp.float32)
    for k in range(seq_dev):
        by_row = jnp.sum(product * in_sequence(positions, ends, k), axis=0, keepdims=True)
        for q in range(score_ref.shape[0]):
            value = jnp.sum(jnp.where(query == q, by_row, 0.0), axis=1, keepdims=True)
            numerator = jnp.where((at_query == q) & (at_seq == k), value, numerator)
    score_ref[...] = numerator / jnp.sqrt(norm_ref[0:1, 0:seq_dev] + EPSILON)


def after(value, *others):
    return lax.optimization_barrier((value, *others))[0]


def gather_blocks(both, own, devices, norm_step, lengths):
    def swap(value, mask):
        return lax.ppermute(value, "seq", [(i, i ^ mask) for i in range(devices)])

    def across(value):
        return lax.ppermute(value, "grp", [(0, 1), (1, 0)])

    def swap_core(values):
        group = jnp.concatenate(values, axis=0) if len(values) > 1 else values[0]
        return group, swap(group, 1)

    z1, z2, y0 = swap(own, 4), swap(own, 8), swap(both, 2)
    x1, y1, z3 = across(z1), swap(z1, 2), swap(after(own, z1), 12)
    z2 = after(z2, x1, y0)
    x2, y2 = across(z2), swap(z2, 2)
    xy1 = across(y1)
    first, first_core = swap_core([both, y0, z1, x1, y1, z2])
    z3 = after(z3, x2, first_core)
    x3, y3 = across(z3), swap(z3, 2)
    y2 = after(y2, xy1)
    xy2 = across(y2)
    second, second_core = swap_core([x2, y2, xy1, z3])
    y3 = after(y3, second_core)
    xy3 = across(y3)
    normed = norm_step(after(lengths, y3))
    third, third_core = swap_core([x3, y3, xy2])
    xy3 = after(xy3, normed)
    last, last_core = swap_core([xy3])
    mine, other = {}, {}
    spots = (
        (first, first_core, ((mine, 0), (other, 0), (mine, 2), (other, 2), (mine, 4), (other, 4), (mine, 6), (mine, 8))),
        (second, second_core, ((other, 8), (mine, 10), (other, 6), (mine, 12))),
        (third, third_core, ((other, 12), (mine, 14), (other, 10))),
        (last, last_core, ((other, 14),)),
    )
    for here, core, places in spots:
        for i, (held, b) in enumerate(places):
            held[b], held[b + 1] = (here, i * PACK), (core, i * PACK)
    return [mine[b] for b in range(devices)], [other[b] for b in range(devices)], normed


def refs_of(blocks):
    arrays, places = [], []
    for value, row in blocks:
        seen = [i for i, array in enumerate(arrays) if array is value]
        if not seen:
            arrays.append(value)
        places.append((seen[0] if seen else len(arrays) - 1, row))
    return arrays, tuple(places)


def local(out_grads, layer_inputs, factor_u, factor_v, seq_lengths):
    devices = lax.axis_size("seq")
    paired = devices == 16 and lax.axis_size("grp") == 2
    seq_dev = seq_lengths.shape[0] // devices
    rank_rows = factor_u.shape[0]
    chunks = PACK // rank_rows
    queries = rank_rows * devices // RANK
    tok_cap, width_out = out_grads.shape
    width_in = layer_inputs.shape[1]
    width = width_out + width_in
    smem = pl.BlockSpec(memory_space=pltpu.SMEM)
    vmem = pl.BlockSpec(memory_space=pltpu.VMEM)
    hbm = pl.BlockSpec(memory_space=pltpu.HBM)

    score_params = pltpu.CompilerParams(vmem_limit_bytes=SCORE_VMEM)
    half_width = width // (2 * chunks)
    packed = pl.pallas_call(
        functools.partial(pack_kernel, chunks, paired),
        out_shape=[jax.ShapeDtypeStruct((2 * PACK, half_width), factor_u.dtype)]
        + [jax.ShapeDtypeStruct((PACK, half_width), factor_u.dtype)] * paired,
        in_specs=[hbm, hbm],
        out_specs=[vmem] * (1 + paired),
        scratch_shapes=[
            pltpu.VMEM(factor_u.shape, factor_u.dtype),
            pltpu.VMEM(factor_v.shape, factor_v.dtype),
            pltpu.SemaphoreType.DMA((2,)),
        ],
        compiler_params=pltpu.CompilerParams(vmem_limit_bytes=PACK_VMEM),
    )(factor_u, factor_v)
    def norm_step(lengths):
        return pl.pallas_call(
            functools.partial(norm_kernel, seq_dev),
            out_shape=jax.ShapeDtypeStruct((8, 128), jnp.float32),
            in_specs=[smem, vmem, vmem],
            out_specs=vmem,
            compiler_params=score_params,
            cost_estimate=pl.CostEstimate(
                flops=2 * tok_cap * tok_cap * width,
                bytes_accessed=2 * tok_cap * width,
                transcendentals=0,
            ),
        )(lengths, out_grads, layer_inputs)

    if paired:
        mine, other, normed = gather_blocks(packed[0], packed[1], devices, norm_step, seq_lengths)
    else:
        normed = norm_step(seq_lengths)
        gathered = lax.all_gather(packed[0], "seq", axis=0, tiled=True)
        mine = [(gathered, 2 * PACK * b) for b in range(devices)]
        other = [(gathered, 2 * PACK * b + PACK) for b in range(devices)]

    frows = devices * rank_rows
    cost = pl.CostEstimate(
        flops=tok_cap * frows * width, bytes_accessed=(tok_cap + frows) * width, transcendentals=0
    )

    arrays, places = refs_of(mine)
    held = pl.pallas_call(
        functools.partial(partial_kernel, rank_rows, paired, places),
        out_shape=jax.ShapeDtypeStruct((2, tok_cap, frows), jnp.float32),
        in_specs=[vmem, vmem] + [vmem] * len(arrays),
        out_specs=vmem,
        compiler_params=score_params,
        cost_estimate=cost,
    )(out_grads, layer_inputs, *arrays)
    arrays, places = refs_of(other)
    return pl.pallas_call(
        functools.partial(score_kernel, seq_dev, rank_rows, paired, places),
        out_shape=jax.ShapeDtypeStruct((queries, seq_dev), jnp.float32),
        in_specs=[smem, vmem, vmem, vmem, vmem] + [vmem] * len(arrays),
        out_specs=vmem,
        compiler_params=score_params,
        cost_estimate=cost,
    )(seq_lengths, normed, held, out_grads, layer_inputs, *arrays)


def solution(mesh):
    in_specs = (
        P(("grp", "seq"), None),
        P(("grp", "seq"), None),
        P("seq", None),
        P("seq", None),
        P("grp"),
    )
    out_specs = P(None, ("grp", "seq"))
    return jax.shard_map(local, mesh=mesh, in_specs=in_specs, out_specs=out_specs, check_vma=False)
```

time: 61.9 us -> 50.4 us (0.81)
  starting transfers between devices: 24.5 us -> 20 us
  local copies, waits for them, and re-layouts: 7.11 us -> 4.22 us
  Pallas kernels: 12.3 us -> 9.98 us
  waiting for transfers between devices: 17.6 us -> 15.9 us
    pallas_call x2, Pallas kernels: 9.1 us -> 5.13 us  [the longest x1 3.22 us: norm_step(): pl.pallas_call(functools.partial(norm_kernel, seq_dev), out_shape=jax.Sha...]
    ppermute x21 -> x11, starting transfers between devices: 17.5 us -> 14.1 us  [swap(): return lax.ppermute(value, 'seq', [(i, i ^ mask) for i in range(devices)])]
    unnamed x10 -> x18, local copies, waits for them, and re-layouts: 7.11 us -> 4.19 us
    ppermute x6, waiting for transfers between devices: 11.2 us -> 9.15 us  [across(): return lax.ppermute(value, 'grp', [(0, 1), (1, 0)])]
    pallas_call x1, Pallas kernels: 0.07 us -> 1.79 us  [local(): pl.pallas_call(functools.partial(pack_kernel, chunks, paired), out_shape=...]
    ppermute x6, starting transfers between devices: 7.04 us -> 5.85 us  [across(): return lax.ppermute(value, 'grp', [(0, 1), (1, 0)])]
    ppermute x21 -> x11, waiting for transfers between devices: 6.44 us -> 6.72 us  [swap(): return lax.ppermute(value, 'seq', [(i, i ^ mask) for i in range(devices)])]
  transfers between devices with their start and end apart: 27 -> 17, of which waited for: 11 -> 7; matrix products, arithmetic and copies ran while one was open for 0% -> 2% of each run, Pallas kernels for 15% -> 10%
where the time goes in v3:
time: 50.4 us; the launch traced here: 50.2 us
  starting transfers between devices  20 us (40%)
  waiting for transfers between devices  15.9 us (32%)
  Pallas kernels  9.98 us (20%)
  local copies, waits for them, and re-layouts  4.22 us (8%)
    ppermute x11, starting transfers between devices, swap(): return lax.ppermute(value, 'seq', [(i, i ^ mask) for i in range(devices)])  14.1 us
    ppermute x6, waiting for transfers between devices, across(): return lax.ppermute(value, 'grp', [(0, 1), (1, 0)])  9.15 us
    ppermute x11, waiting for transfers between devices, swap(): return lax.ppermute(value, 'seq', [(i, i ^ mask) for i in range(devices)])  6.72 us
    ppermute x6, starting transfers between devices, across(): return lax.ppermute(value, 'grp', [(0, 1), (1, 0)])  5.85 us
    unnamed x18, local copies, waits for them, and re-layouts  4.19 us
    pallas_call x1, Pallas kernels, norm_step(): pl.pallas_call(functools.partial(norm_kernel, seq_dev), out_shape=jax.Sha...  3.22 us
    pallas_call x1, Pallas kernels, local(): pl.pallas_call(functools.partial(score_kernel, seq_dev, rank_rows, paired...  3.06 us
    pallas_call x1, Pallas kernels, local(): pl.pallas_call(functools.partial(partial_kernel, rank_rows, paired, place...  1.9 us
  transfers between devices with their start and end apart: 17, of which 7 were waited for; matrix products, arithmetic and copies ran while one was open for 2% of the time, Pallas kernels for 10%

profile of v3, /device:TPU:0, one launch (start us, length us, event | category | flops | bytes accessed | tf_op | source)
XLA Modules:
  0.0 50.2 jit_solution(12303799131413059568)
XLA Ops:
  0.0 1.8 %shard_map.55 = (bf16[32,4608]{1,0:T(8,128)(2,1)}, bf16[16,4608]{1,0:T(8,128)(2,1)}) custom-call(bf16[4,8192]{1,0:T(4,128)(2,1)} %u_hbm.1, bf16[4,28672]{1,0:T(4,128)(2,1)} %v_hbm.1), custom_call_target="tpu_custom_call" | custom-call | tf_op jit(solution)/shard_map/pallas_call | solution.py:241
  1.8 3.1 %collective-permute-start = (bf16[16,4608]{1,0:T(8,128)(2,1)}, bf16[16,4608]{1,0:T(8,128)(2,1)S(1)}, u32[]{:S(2)}, u32[]{:S(2)}) collective-permute-start(bf16[16,4608]{1,0:T(8,128)(2,1)} %get-tuple-element.15), channel_id=1, source_target_pairs={{0,4},{1,5},{2,6},{3,7},{4,0},{5,1},{6,2},{7,3},{8,12},{9,13},{10,... | collective-permute-start | bytes 442376 | tf_op jit(solution)/shard_map/ppermute | solution.py:176
  4.9 2.6 %collective-permute-start.2 = (bf16[16,4608]{1,0:T(8,128)(2,1)}, bf16[16,4608]{1,0:T(8,128)(2,1)S(1)}, u32[]{:S(2)}, u32[]{:S(2)}) collective-permute-start(bf16[16,4608]{1,0:T(8,128)(2,1)} %get-tuple-element.15), channel_id=1, source_target_pairs={{0,8},{1,9},{2,10},{3,11},{4,12},{5,13},{6,14},{7,15},{8,0},{9,1},... | collective-permute-start | bytes 442376 | tf_op jit(solution)/shard_map/ppermute | solution.py:176
  7.5 1.5 %collective-permute-start.4 = (bf16[32,4608]{1,0:T(8,128)(2,1)}, bf16[32,4608]{1,0:T(8,128)(2,1)S(1)}, u32[]{:S(2)}, u32[]{:S(2)}) collective-permute-start(bf16[32,4608]{1,0:T(8,128)(2,1)} %get-tuple-element.16), channel_id=1, source_target_pairs={{0,2},{1,3},{2,0},{3,1},{4,6},{5,7},{6,4},{7,5},{8,10},{9,11},{10,... | collective-permute-start | bytes 884744 | tf_op jit(solution)/shard_map/ppermute | solution.py:176
  9.0 2.5 %collective-permute-done = bf16[16,4608]{1,0:T(8,128)(2,1)S(1)} collective-permute-done((bf16[16,4608]{1,0:T(8,128)(2,1)}, bf16[16,4608]{1,0:T(8,128)(2,1)S(1)}, u32[]{:S(2)}, u32[]{:S(2)}) %collective-permute-start) | collective-permute-done | bytes 147488 | tf_op jit(solution)/shard_map/ppermute | solution.py:176
  11.5 1.8 %collective-permute-start.3 = (bf16[16,4608]{1,0:T(8,128)(2,1)S(1)}, bf16[16,4608]{1,0:T(8,128)(2,1)S(1)}, u32[]{:S(2)}, u32[]{:S(2)}) collective-permute-start(bf16[16,4608]{1,0:T(8,128)(2,1)S(1)} %collective-permute-done), channel_id=1, source_target_pairs={{0,16},{16,0},{1,17},{17,1},{2,18},{18,2},{3,19},{19,3},{4,20},{20... | collective-permute-start | bytes 442376 | tf_op jit(solution)/shard_map/ppermute | solution.py:179
  13.3 1.0 %constant_dynamic-update-slice_fusion.5 = bf16[128,4608]{1,0:T(8,128)(2,1)S(1)} fusion(bf16[32,4608]{1,0:T(8,128)(2,1)} %get-tuple-element.16), kind=kLoop, calls=%fused_computation.5 | loop fusion | bytes 589824
  14.3 2.9 %collective-permute-start.1 = (bf16[16,4608]{1,0:T(8,128)(2,1)}, bf16[16,4608]{1,0:T(8,128)(2,1)S(1)}, u32[]{:S(2)}, u32[]{:S(2)}) collective-permute-start(bf16[16,4608]{1,0:T(8,128)(2,1)} %get-tuple-element.15), channel_id=1, source_target_pairs={{0,12},{1,13},{2,14},{3,15},{4,8},{5,9},{6,10},{7,11},{8,4},{9,5},... | collective-permute-start | bytes 442376 | tf_op jit(solution)/shard_map/ppermute | solution.py:176
  17.2 1.5 %collective-permute-start.6 = (bf16[16,4608]{1,0:T(8,128)(2,1)S(1)}, bf16[16,4608]{1,0:T(8,128)(2,1)S(1)}, u32[]{:S(2)}, u32[]{:S(2)}) collective-permute-start(bf16[16,4608]{1,0:T(8,128)(2,1)S(1)} %collective-permute-done), channel_id=1, source_target_pairs={{0,2},{1,3},{2,0},{3,1},{4,6},{5,7},{6,4},{7,5},{8,10},{9,11},{10,... | collective-permute-start | bytes 442376 | tf_op jit(solution)/shard_map/ppermute | solution.py:176
  19.3 0.7 %collective-permute-start.5 = (bf16[16,4608]{1,0:T(8,128)(2,1)S(1)}, bf16[16,4608]{1,0:T(8,128)(2,1)S(1)}, u32[]{:S(2)}, u32[]{:S(2)}) collective-permute-start(bf16[16,4608]{1,0:T(8,128)(2,1)S(1)} %collective-permute-done.2), channel_id=1, source_target_pairs={{0,16},{16,0},{1,17},{17,1},{2,18},{18,2},{3,19},{19,3},{4,20},{20... | collective-permute-start | bytes 442376 | tf_op jit(solution)/shard_map/ppermute | solution.py:179
  20.0 2.9 %collective-permute-done.6 = bf16[16,4608]{1,0:T(8,128)(2,1)S(1)} collective-permute-done((bf16[16,4608]{1,0:T(8,128)(2,1)S(1)}, bf16[16,4608]{1,0:T(8,128)(2,1)S(1)}, u32[]{:S(2)}, u32[]{:S(2)}) %collective-permute-start.6) | collective-permute-done | bytes 147488 | tf_op jit(solution)/shard_map/ppermute | solution.py:176
  23.1 0.6 %collective-permute-start.10 = (bf16[16,4608]{1,0:T(8,128)(2,1)S(1)}, bf16[16,4608]{1,0:T(8,128)(2,1)S(1)}, u32[]{:S(2)}, u32[]{:S(2)}) collective-permute-start(bf16[16,4608]{1,0:T(8,128)(2,1)S(1)} %collective-permute-done.6), channel_id=1, source_target_pairs={{0,16},{16,0},{1,17},{17,1},{2,18},{18,2},{3,19},{19,3},{4,20},{20... | collective-permute-start | bytes 442376 | tf_op jit(solution)/shard_map/ppermute | solution.py:179
  23.7 0.8 %collective-permute-done.5 = bf16[16,4608]{1,0:T(8,128)(2,1)S(1)} collective-permute-done((bf16[16,4608]{1,0:T(8,128)(2,1)S(1)}, bf16[16,4608]{1,0:T(8,128)(2,1)S(1)}, u32[]{:S(2)}, u32[]{:S(2)}) %collective-permute-start.5) | collective-permute-done | bytes 147488 | tf_op jit(solution)/shard_map/ppermute | solution.py:179
  24.4 4.9 %collective-permute-done.10 = bf16[16,4608]{1,0:T(8,128)(2,1)S(1)} collective-permute-done((bf16[16,4608]{1,0:T(8,128)(2,1)S(1)}, bf16[16,4608]{1,0:T(8,128)(2,1)S(1)}, u32[]{:S(2)}, u32[]{:S(2)}) %collective-permute-start.10) | collective-permute-done | bytes 147488 | tf_op jit(solution)/shard_map/ppermute | solution.py:179
  29.4 0.6 %collective-permute-start.12 = (bf16[16,4608]{1,0:T(8,128)(2,1)S(1)}, bf16[16,4608]{1,0:T(8,128)(2,1)S(1)}, u32[]{:S(2)}, u32[]{:S(2)}) collective-permute-start(bf16[16,4608]{1,0:T(8,128)(2,1)S(1)} %collective-permute-done.1), channel_id=1, source_target_pairs={{0,16},{16,0},{1,17},{17,1},{2,18},{18,2},{3,19},{19,3},{4,20},{20... | collective-permute-start | bytes 442376 | tf_op jit(solution)/shard_map/ppermute | solution.py:179
  30.1 1.6 %collective-permute-start.13 = (bf16[16,4608]{1,0:T(8,128)(2,1)S(1)}, bf16[16,4608]{1,0:T(8,128)(2,1)S(1)}, u32[]{:S(2)}, u32[]{:S(2)}) collective-permute-start(bf16[16,4608]{1,0:T(8,128)(2,1)S(1)} %collective-permute-done.9), channel_id=1, source_target_pairs={{0,16},{16,0},{1,17},{17,1},{2,18},{18,2},{3,19},{19,3},{4,20},{20... | collective-permute-start | bytes 442376 | tf_op jit(solution)/shard_map/ppermute | solution.py:179
  31.6 1.5 %collective-permute-start.8 = (bf16[16,4608]{1,0:T(8,128)(2,1)S(1)}, bf16[16,4608]{1,0:T(8,128)(2,1)S(1)}, u32[]{:S(2)}, u32[]{:S(2)}) collective-permute-start(bf16[16,4608]{1,0:T(8,128)(2,1)S(1)} %collective-permute-done.1), channel_id=1, source_target_pairs={{0,2},{1,3},{2,0},{3,1},{4,6},{5,7},{6,4},{7,5},{8,10},{9,11},{10,... | collective-permute-start | bytes 442376 | tf_op jit(solution)/shard_map/ppermute | solution.py:176
  33.1 3.1 %collective-permute-done.12 = bf16[16,4608]{1,0:T(8,128)(2,1)S(1)} collective-permute-done((bf16[16,4608]{1,0:T(8,128)(2,1)S(1)}, bf16[16,4608]{1,0:T(8,128)(2,1)S(1)}, u32[]{:S(2)}, u32[]{:S(2)}) %collective-permute-start.12) | collective-permute-done | bytes 147488 | tf_op jit(solution)/shard_map/ppermute | solution.py:179
  36.2 1.3 %collective-permute-done.8 = bf16[16,4608]{1,0:T(8,128)(2,1)S(1)} collective-permute-done((bf16[16,4608]{1,0:T(8,128)(2,1)S(1)}, bf16[16,4608]{1,0:T(8,128)(2,1)S(1)}, u32[]{:S(2)}, u32[]{:S(2)}) %collective-permute-start.8) | collective-permute-done | bytes 147488 | tf_op jit(solution)/shard_map/ppermute | solution.py:176
  38.1 0.6 %collective-permute-start.15 = (bf16[16,4608]{1,0:T(8,128)(2,1)S(1)}, bf16[16,4608]{1,0:T(8,128)(2,1)S(1)}, u32[]{:S(2)}, u32[]{:S(2)}) collective-permute-start(bf16[16,4608]{1,0:T(8,128)(2,1)S(1)} %collective-permute-done.8), channel_id=1, source_target_pairs={{0,16},{16,0},{1,17},{17,1},{2,18},{18,2},{3,19},{19,3},{4,20},{20... | collective-permute-start | bytes 442376 | tf_op jit(solution)/shard_map/ppermute | solution.py:179
  38.7 3.1 %copy-done = bf16[128,28672]{1,0:T(8,128)(2,1)S(1)} copy-done((bf16[128,28672]{1,0:T(8,128)(2,1)S(1)}, bf16[128,28672]{1,0:T(8,128)(2,1)}, u32[]{:S(2)}) %copy-start) | copy-done | bytes 7340056
  41.8 3.2 %shard_map.56.norm_ref = f32[8,128]{1,0:T(8,128)S(1)} custom-call(s32[64]{0:T(128)S(1)} %copy-done.3, bf16[128,8192]{1,0:T(8,128)(2,1)S(1)} %copy-done.2, bf16[128,28672]{1,0:T(8,128)(2,1)S(1)} %copy-done), custom_call_target="tpu_custom_call" | custom-call | flops 1207959552 | bytes 9437184 | tf_op jit(solution)/shard_map/pallas_call | solution.py:255
  45.2 1.9 %shard_map.57.held_ref = f32[2,128,64]{2,1,0:T(8,128)S(1)} custom-call(bf16[128,8192]{1,0:T(8,128)(2,1)S(1)} %copy-done.2, bf16[128,28672]{1,0:T(8,128)(2,1)S(1)} %copy-done.1, bf16[128,4608]{1,0:T(8,128)(2,1)S(1)} %constant_dynamic-update-slice_fusion.refs_0_, bf16[128,4608]{1,0:T(8,128)(2,1)S(1)} %collective-permute-done.7.refs_1_, ...), custom_call_target="tpu_custom_call" | custom-call | flops 301989888 | bytes 7077888 | tf_op jit(solution)/shard_map/pallas_call | solution.py:282
  47.2 3.1 %shard_map.58 = f32[2,4]{1,0:T(2,128)} custom-call(s32[64]{0:T(128)S(1)} %copy-done.3, f32[8,128]{1,0:T(8,128)S(1)} %shard_map.56.norm_ref, f32[2,128,64]{2,1,0:T(8,128)S(1)} %shard_map.57.held_ref, bf16[128,8192]{1,0:T(8,128)(2,1)S(1)} %copy-done.2, bf16[128,28672]{1,0:T(8,128)(2,1)S(1)} %copy-done.1, ...), custom_call_target="tpu_custom_call" | custom-call | flops 301989888 | bytes 7077888 | tf_op jit(solution)/shard_map/pallas_call | solution.py:291
  (35 shorter events, 1.6 us)
Async XLA Ops:
  1.8 9.7 %collective-permute-start = (bf16[16,4608]{1,0:T(8,128)(2,1)}, bf16[16,4608]{1,0:T(8,128)(2,1)S(1)}, u32[]{:S(2)}, u32[]{:S(2)}) collective-permute-start(bf16[16,4608]{1,0:T(8,128)(2,1)} %get-tuple-element.15), channel_id=1, source_target_pairs={{0,4},{1,5},{2,6},{3,7},{4,0},{5,1},{6,2},{7,3},{8,12},{9,13},{10,... | collective-permute-start | bytes 442376 | tf_op jit(solution)/shard_map/ppermute | solution.py:176
  4.9 13.8 %collective-permute-start.2 = (bf16[16,4608]{1,0:T(8,128)(2,1)}, bf16[16,4608]{1,0:T(8,128)(2,1)S(1)}, u32[]{:S(2)}, u32[]{:S(2)}) collective-permute-start(bf16[16,4608]{1,0:T(8,128)(2,1)} %get-tuple-element.15), channel_id=1, source_target_pairs={{0,8},{1,9},{2,10},{3,11},{4,12},{5,13},{6,14},{7,15},{8,0},{9,1},... | collective-permute-start | bytes 442376 | tf_op jit(solution)/shard_map/ppermute | solution.py:176
  7.5 11.2 %collective-permute-start.4 = (bf16[32,4608]{1,0:T(8,128)(2,1)}, bf16[32,4608]{1,0:T(8,128)(2,1)S(1)}, u32[]{:S(2)}, u32[]{:S(2)}) collective-permute-start(bf16[32,4608]{1,0:T(8,128)(2,1)} %get-tuple-element.16), channel_id=1, source_target_pairs={{0,2},{1,3},{2,0},{3,1},{4,6},{5,7},{6,4},{7,5},{8,10},{9,11},{10,... | collective-permute-start | bytes 884744 | tf_op jit(solution)/shard_map/ppermute | solution.py:176
  11.5 7.2 %collective-permute-start.3 = (bf16[16,4608]{1,0:T(8,128)(2,1)S(1)}, bf16[16,4608]{1,0:T(8,128)(2,1)S(1)}, u32[]{:S(2)}, u32[]{:S(2)}) collective-permute-start(bf16[16,4608]{1,0:T(8,128)(2,1)S(1)} %collective-permute-done), channel_id=1, source_target_pairs={{0,16},{16,0},{1,17},{17,1},{2,18},{18,2},{3,19},{19,3},{4,20},{20... | collective-permute-start | bytes 442376 | tf_op jit(solution)/shard_map/ppermute | solution.py:179
  14.3 15.1 %collective-permute-start.1 = (bf16[16,4608]{1,0:T(8,128)(2,1)}, bf16[16,4608]{1,0:T(8,128)(2,1)S(1)}, u32[]{:S(2)}, u32[]{:S(2)}) collective-permute-start(bf16[16,4608]{1,0:T(8,128)(2,1)} %get-tuple-element.15), channel_id=1, source_target_pairs={{0,12},{1,13},{2,14},{3,15},{4,8},{5,9},{6,10},{7,11},{8,4},{9,5},... | collective-permute-start | bytes 442376 | tf_op jit(solution)/shard_map/ppermute | solution.py:176
  17.2 5.7 %collective-permute-start.6 = (bf16[16,4608]{1,0:T(8,128)(2,1)S(1)}, bf16[16,4608]{1,0:T(8,128)(2,1)S(1)}, u32[]{:S(2)}, u32[]{:S(2)}) collective-permute-start(bf16[16,4608]{1,0:T(8,128)(2,1)S(1)} %collective-permute-done), channel_id=1, source_target_pairs={{0,2},{1,3},{2,0},{3,1},{4,6},{5,7},{6,4},{7,5},{8,10},{9,11},{10,... | collective-permute-start | bytes 442376 | tf_op jit(solution)/shard_map/ppermute | solution.py:176
  18.7 10.6 %collective-permute-start.9 = (bf16[16,4608]{1,0:T(8,128)(2,1)S(1)}, bf16[16,4608]{1,0:T(8,128)(2,1)S(1)}, u32[]{:S(2)}, u32[]{:S(2)}) collective-permute-start(bf16[16,4608]{1,0:T(8,128)(2,1)S(1)} %collective-permute-done.2), channel_id=1, source_target_pairs={{0,2},{1,3},{2,0},{3,1},{4,6},{5,7},{6,4},{7,5},{8,10},{9,11},{10,... | collective-permute-start | bytes 442376 | tf_op jit(solution)/shard_map/ppermute | solution.py:176
  19.3 5.1 %collective-permute-start.5 = (bf16[16,4608]{1,0:T(8,128)(2,1)S(1)}, bf16[16,4608]{1,0:T(8,128)(2,1)S(1)}, u32[]{:S(2)}, u32[]{:S(2)}) collective-permute-start(bf16[16,4608]{1,0:T(8,128)(2,1)S(1)} %collective-permute-done.2), channel_id=1, source_target_pairs={{0,16},{16,0},{1,17},{17,1},{2,18},{18,2},{3,19},{19,3},{4,20},{20... | collective-permute-start | bytes 442376 | tf_op jit(solution)/shard_map/ppermute | solution.py:179
  22.9 15.8 %copy-start.2 = (bf16[128,8192]{1,0:T(8,128)(2,1)S(1)}, bf16[128,8192]{1,0:T(8,128)(2,1)}, u32[]{:S(2)}) copy-start(bf16[128,8192]{1,0:T(8,128)(2,1)} %out_ref.5) | copy-start | bytes 6291460
  22.9 15.8 %copy-start.3 = (s32[64]{0:T(128)S(1)}, s32[64]{0:T(128)}, u32[]{:S(2)}) copy-start(s32[64]{0:T(128)} %lengths_ref.2) | copy-start | bytes 772
  23.0 6.4 %collective-permute-start.7 = (bf16[128,4608]{1,0:T(8,128)(2,1)S(1)}, bf16[128,4608]{1,0:T(8,128)(2,1)S(1)}, u32[]{:S(2)}, u32[]{:S(2)}) collective-permute-start(bf16[128,4608]{1,0:T(8,128)(2,1)S(1)} %constant_dynamic-update-slice_fusion.refs_0_), channel_id=1, source_target_pairs={{0,1},{1,0},{2,3},{3,2},{4,5},{5,4},{6,7},{7,6},{8,9},{9,8},{10,11... | collective-permute-start | bytes 3538952 | tf_op jit(solution)/shard_map/ppermute | solution.py:176
  23.1 6.3 %collective-permute-start.10 = (bf16[16,4608]{1,0:T(8,128)(2,1)S(1)}, bf16[16,4608]{1,0:T(8,128)(2,1)S(1)}, u32[]{:S(2)}, u32[]{:S(2)}) collective-permute-start(bf16[16,4608]{1,0:T(8,128)(2,1)S(1)} %collective-permute-done.6), channel_id=1, source_target_pairs={{0,16},{16,0},{1,17},{17,1},{2,18},{18,2},{3,19},{19,3},{4,20},{20... | collective-permute-start | bytes 442376 | tf_op jit(solution)/shard_map/ppermute | solution.py:179
  29.4 6.8 %collective-permute-start.12 = (bf16[16,4608]{1,0:T(8,128)(2,1)S(1)}, bf16[16,4608]{1,0:T(8,128)(2,1)S(1)}, u32[]{:S(2)}, u32[]{:S(2)}) collective-permute-start(bf16[16,4608]{1,0:T(8,128)(2,1)S(1)} %collective-permute-done.1), channel_id=1, source_target_pairs={{0,16},{16,0},{1,17},{17,1},{2,18},{18,2},{3,19},{19,3},{4,20},{20... | collective-permute-start | bytes 442376 | tf_op jit(solution)/shard_map/ppermute | solution.py:179
  30.0 7.6 %collective-permute-start.11 = (bf16[64,4608]{1,0:T(8,128)(2,1)S(1)}, bf16[64,4608]{1,0:T(8,128)(2,1)S(1)}, u32[]{:S(2)}, u32[]{:S(2)}) collective-permute-start(bf16[64,4608]{1,0:T(8,128)(2,1)S(1)} %constant_dynamic-update-slice_fusion.6.refs_2_), channel_id=1, source_target_pairs={{0,1},{1,0},{2,3},{3,2},{4,5},{5,4},{6,7},{7,6},{8,9},{9,8},{10,11... | collective-permute-start | bytes 1769480 | tf_op jit(solution)/shard_map/ppermute | solution.py:176
  30.1 7.9 %collective-permute-start.13 = (bf16[16,4608]{1,0:T(8,128)(2,1)S(1)}, bf16[16,4608]{1,0:T(8,128)(2,1)S(1)}, u32[]{:S(2)}, u32[]{:S(2)}) collective-permute-start(bf16[16,4608]{1,0:T(8,128)(2,1)S(1)} %collective-permute-done.9), channel_id=1, source_target_pairs={{0,16},{16,0},{1,17},{17,1},{2,18},{18,2},{3,19},{19,3},{4,20},{20... | collective-permute-start | bytes 442376 | tf_op jit(solution)/shard_map/ppermute | solution.py:179
  31.6 5.9 %collective-permute-start.8 = (bf16[16,4608]{1,0:T(8,128)(2,1)S(1)}, bf16[16,4608]{1,0:T(8,128)(2,1)S(1)}, u32[]{:S(2)}, u32[]{:S(2)}) collective-permute-start(bf16[16,4608]{1,0:T(8,128)(2,1)S(1)} %collective-permute-done.1), channel_id=1, source_target_pairs={{0,2},{1,3},{2,0},{3,1},{4,6},{5,7},{6,4},{7,5},{8,10},{9,11},{10,... | collective-permute-start | bytes 442376 | tf_op jit(solution)/shard_map/ppermute | solution.py:176
  38.0 7.2 %collective-permute-start.14 = (bf16[48,4608]{1,0:T(8,128)(2,1)S(1)}, bf16[48,4608]{1,0:T(8,128)(2,1)S(1)}, u32[]{:S(2)}, u32[]{:S(2)}) collective-permute-start(bf16[48,4608]{1,0:T(8,128)(2,1)S(1)} %constant_dynamic-update-slice_fusion.10.refs_4_), channel_id=1, source_target_pairs={{0,1},{1,0},{2,3},{3,2},{4,5},{5,4},{6,7},{7,6},{8,9},{9,8},{10,11... | collective-permute-start | bytes 1327112 | tf_op jit(solution)/shard_map/ppermute | solution.py:176
  38.1 6.9 %collective-permute-start.15 = (bf16[16,4608]{1,0:T(8,128)(2,1)S(1)}, bf16[16,4608]{1,0:T(8,128)(2,1)S(1)}, u32[]{:S(2)}, u32[]{:S(2)}) collective-permute-start(bf16[16,4608]{1,0:T(8,128)(2,1)S(1)} %collective-permute-done.8), channel_id=1, source_target_pairs={{0,16},{16,0},{1,17},{17,1},{2,18},{18,2},{3,19},{19,3},{4,20},{20... | collective-permute-start | bytes 442376 | tf_op jit(solution)/shard_map/ppermute | solution.py:179
  38.7 3.1 %copy-start = (bf16[128,28672]{1,0:T(8,128)(2,1)S(1)}, bf16[128,28672]{1,0:T(8,128)(2,1)}, u32[]{:S(2)}) copy-start(bf16[128,28672]{1,0:T(8,128)(2,1)} %in_ref.5) | copy-start | bytes 22020100
  41.8 3.4 %copy-start.1 = (bf16[128,28672]{1,0:T(8,128)(2,1)S(1)}, bf16[128,28672]{1,0:T(8,128)(2,1)}, u32[]{:S(2)}) copy-start(bf16[128,28672]{1,0:T(8,128)(2,1)} %in_ref.5) | copy-start | bytes 22020100
  45.0 2.1 %collective-permute-start.16 = (bf16[16,4608]{1,0:T(8,128)(2,1)S(1)}, bf16[16,4608]{1,0:T(8,128)(2,1)S(1)}, u32[]{:S(2)}, u32[]{:S(2)}) collective-permute-start(bf16[16,4608]{1,0:T(8,128)(2,1)S(1)} %collective-permute-done.15.refs_6_), channel_id=1, source_target_pairs={{0,1},{1,0},{2,3},{3,2},{4,5},{5,4},{6,7},{7,6},{8,9},{9,8},{10,11... | collective-permute-start | bytes 442376 | tf_op jit(solution)/shard_map/ppermute | solution.py:176

commit v4 on v3

v4 whole, which is shorter than its diff:
```python
import functools

import jax
import jax.numpy as jnp
from jax import lax
from jax.experimental import pallas as pl
from jax.experimental.pallas import tpu as pltpu
from jax.sharding import PartitionSpec as P

RANK = 32
EPSILON = 1e-06
PACK = 16
HEAD = 8192
SCORE_VMEM = 24 * 1024 * 1024
PACK_VMEM = 58 * 1024 * 1024

NT = (((1,), (1,)), ((), ()))


def inner_rows(left, right):
    return lax.dot_general(left, right, NT, preferred_element_type=jnp.float32)


def first_half(paired):
    return lax.axis_index("grp") % 2 if paired else 0


def turn(paired, chunks):
    return lax.axis_index("seq") % chunks if paired else 0


def pack_kernel(chunks, paired, u_hbm, v_hbm, both_ref, *refs):
    *own_refs, u_ref, v_ref, sems = refs
    copies = []
    for i, (hbm, ref) in enumerate(((u_hbm, u_ref), (v_hbm, v_ref))):
        wide = ref.shape[1] // chunks
        for j in range(chunks):
            cols = pl.ds(j * wide, wide)
            copies.append(pltpu.make_async_copy(hbm.at[:, cols], ref.at[:, cols], sems.at[i, j]))
    for copy in copies:
        copy.start()
    for copy in copies:
        copy.wait()
    rank_rows = u_ref.shape[0]
    member = lax.axis_index("seq") % chunks
    wide_u, wide_v = u_ref.shape[1] // (2 * chunks), v_ref.shape[1] // (2 * chunks)
    for side in range(2):
        half = first_half(paired) ^ side
        place = 0
        for ref, wide in ((u_ref, wide_u), (v_ref, wide_v)):
            rows = []
            for g in range(chunks):
                start = pl.multiple_of(((g ^ member) * 2 + half) * wide, 128)
                rows.append(ref[:, pl.ds(start, wide)].astype(jnp.float32))
            piece = jnp.concatenate(rows, axis=0).astype(both_ref.dtype)
            both_ref[side * PACK : (side + 1) * PACK, place : place + wide] = piece
            if side == 0:
                for own_ref in own_refs:
                    own_ref[:, place : place + wide] = piece
            place += wide


def head_kernel(after_ref, in_ref, gram_ref):
    head = in_ref[:, :HEAD]
    gram_ref[...] = inner_rows(head, head)


def norm_kernel(seq_dev, lengths_hbm, head_ref, out_ref, in_ref, norm_ref, member_ref, lengths_ref, sem):
    copy = pltpu.make_async_copy(lengths_hbm, lengths_ref, sem)
    copy.start()
    gram_out = inner_rows(out_ref[...], out_ref[...])
    tail = in_ref[:, HEAD:]
    paired = gram_out * (head_ref[...] + inner_rows(tail, tail))
    copy.wait()
    seqs, tok_cap = member_ref.shape
    which = lax.broadcasted_iota(jnp.int32, (seqs, tok_cap), 0)
    position = lax.broadcasted_iota(jnp.int32, (seqs, tok_cap), 1)
    block = lax.axis_index("seq")
    member = jnp.zeros((seqs, tok_cap), jnp.float32)
    low = 0
    for k in range(seq_dev):
        high = low + lengths_ref[block * seq_dev + k]
        inside = (which == k) & (position >= low) & (position < high)
        member = jnp.where(inside, 1.0, member)
        low = high
    member_ref[...] = member
    sums = jnp.dot(
        member, paired, precision=lax.Precision.HIGHEST, preferred_element_type=jnp.float32
    )
    value = jnp.sum(sums * member, axis=1, keepdims=True) / (out_ref.shape[1] * in_ref.shape[1])
    norm_ref[...] = jnp.sum(jnp.where(which == position, value, 0.0), axis=0, keepdims=True)


def swap_groups(value, bit, rank_rows):
    lanes = lax.broadcasted_iota(jnp.int32, (1, value.shape[1]), 1)
    shift = bit * rank_rows
    up = pltpu.roll(value, shift, 1)
    down = pltpu.roll(value, value.shape[1] - shift, 1)
    return jnp.where((lanes // shift) % 2 == 0, down, up)


def merged_rows(blocks, offset, wide, j, chunks, rank_rows):
    group = lax.broadcasted_iota(jnp.int32, (PACK, wide), 0) // rank_rows
    rows = []
    for first in range(0, len(blocks), chunks):
        merged = None
        for g in range(chunks):
            ref, row = blocks[first + (g ^ j)]
            piece = ref[row : row + PACK, offset : offset + wide]
            merged = piece if merged is None else jnp.where(group == g, piece, merged)
        rows.append(merged)
    return jnp.concatenate(rows, axis=0)


def both_projections(out_ref, in_ref, half, blocks, rank_rows, paired):
    chunks = PACK // rank_rows
    results, offset = [], 0
    for ref in (out_ref, in_ref):
        wide = ref.shape[1] // (2 * chunks)
        result = None
        for j in range(chunks):
            rows = merged_rows(blocks, offset, wide, j, chunks, rank_rows)
            start = pl.multiple_of(((j ^ turn(paired, chunks)) * 2 + half) * wide, 128)
            part = inner_rows(ref[:, pl.ds(start, wide)], rows)
            bit = 1
            while bit < chunks:
                if j & bit:
                    part = swap_groups(part, bit, rank_rows)
                bit *= 2
            result = part if result is None else result + part
        results.append(result)
        offset += wide
    return results


def partial_kernel(rank_rows, paired, places, out_ref, in_ref, *refs):
    *array_refs, held_ref = refs
    blocks = [(array_refs[i], row) for i, row in places]
    half = first_half(paired)
    held_out, held_in = both_projections(
        out_ref, in_ref, half, blocks, rank_rows, paired
    )
    held_ref[0] = held_out
    held_ref[1] = held_in


def score_kernel(rank_rows, paired, places, norm_ref, member_ref, held_ref, out_ref, in_ref, *refs):
    *array_refs, score_ref = refs
    blocks = [(array_refs[i], row) for i, row in places]
    half = 1 - first_half(paired)
    held_out, held_in = both_projections(
        out_ref, in_ref, half, blocks, rank_rows, paired
    )
    product = (held_ref[0] + held_out) * (held_ref[1] + held_in)
    me = lax.axis_index("seq")
    lanes = lax.broadcasted_iota(jnp.int32, (1, product.shape[1]), 1)
    source = lanes // rank_rows
    if paired:
        source = source ^ me
    query = (source * rank_rows) // RANK
    sums = jnp.dot(
        member_ref[...], product, precision=lax.Precision.HIGHEST, preferred_element_type=jnp.float32
    )
    seqs, tok_cap = member_ref.shape
    diagonal = lax.broadcasted_iota(jnp.int32, (seqs, tok_cap), 0) == lax.broadcasted_iota(
        jnp.int32, (seqs, tok_cap), 1
    )
    scale = jnp.sqrt(norm_ref[...] + EPSILON)
    for q in range(score_ref.shape[0]):
        value = jnp.sum(jnp.where(query == q, sums, 0.0), axis=1, keepdims=True)
        row = jnp.sum(jnp.where(diagonal, value, 0.0), axis=0, keepdims=True) / scale
        score_ref[q : q + 1, :] = row[:, : score_ref.shape[1]]


def gather_blocks(both, own, devices, lengths, head_step, norm_step, partial_step):
    def swap(value, mask):
        return lax.ppermute(value, "seq", [(i, i ^ mask) for i in range(devices)])

    def across(value):
        return lax.ppermute(value, "grp", [(0, 1), (1, 0)])

    gate = lambda *values: lax.optimization_barrier(values)
    stack = lambda *values: jnp.concatenate(values, axis=0)
    z1, z2, y0, both_core = swap(own, 4), swap(own, 8), swap(both, 2), swap(both, 1)
    z1, both_core, own = gate(z1, both_core, own)
    x1, y1, z3 = across(z1), swap(z1, 2), swap(own, 12)
    z2, x1, y1, y0, lengths = gate(z2, x1, y1, y0, lengths)
    x_near, y2 = across(stack(z2, y1)), swap(z2, 2)
    head = head_step(lengths)
    z3, y2, x_near, head, lengths = gate(z3, y2, x_near, head, lengths)
    x_far, y3 = across(stack(z3, y2)), swap(z3, 2)
    early = stack(y0, z1, y1, z2, x1)
    early_core = swap(early, 1)
    normed = norm_step(lengths, head)
    y3, norms = gate(y3, normed[0])
    x_last = across(y3)
    middle = stack(y2, z3, y3, x_near)
    middle_core = swap(middle, 1)
    mine, other = {}, {}

    def place(group, core, places):
        for i, (held, b) in enumerate(places):
            held[b], held[b + 1] = (group, i * PACK), (core, i * PACK)

    place(both, both_core, ((mine, 0), (other, 0)))
    place(early, early_core, ((mine, 2), (other, 2), (mine, 4), (mine, 6), (mine, 8), (other, 4)))
    place(middle, middle_core, ((mine, 10), (mine, 12), (mine, 14), (other, 8), (other, 6)))
    partial = partial_step([mine[b] for b in range(devices)])
    x_far, x_last, partial = gate(x_far, x_last, partial)
    late = stack(x_far, x_last)
    place(late, swap(late, 1), ((other, 12), (other, 10), (other, 14)))
    return [other[b] for b in range(devices)], (norms, normed[1]), partial


def refs_of(blocks):
    arrays, places = [], []
    for value, row in blocks:
        seen = [i for i, array in enumerate(arrays) if array is value]
        if not seen:
            arrays.append(value)
        places.append((seen[0] if seen else len(arrays) - 1, row))
    return arrays, tuple(places)


def local(out_grads, layer_inputs, factor_u, factor_v, seq_lengths):
    devices = lax.axis_size("seq")
    paired = devices == 16 and lax.axis_size("grp") == 2
    seq_dev = seq_lengths.shape[0] // devices
    rank_rows = factor_u.shape[0]
    chunks = PACK // rank_rows
    queries = rank_rows * devices // RANK
    tok_cap, width_out = out_grads.shape
    width_in = layer_inputs.shape[1]
    width = width_out + width_in
    vmem = pl.BlockSpec(memory_space=pltpu.VMEM)
    hbm = pl.BlockSpec(memory_space=pltpu.HBM)

    score_params = pltpu.CompilerParams(vmem_limit_bytes=SCORE_VMEM)
    half_width = width // (2 * chunks)
    packed = pl.pallas_call(
        functools.partial(pack_kernel, chunks, paired),
        out_shape=[jax.ShapeDtypeStruct((2 * PACK, half_width), factor_u.dtype)]
        + [jax.ShapeDtypeStruct((PACK, half_width), factor_u.dtype)] * paired,
        in_specs=[hbm, hbm],
        out_specs=[vmem] * (1 + paired),
        scratch_shapes=[
            pltpu.VMEM(factor_u.shape, factor_u.dtype),
            pltpu.VMEM(factor_v.shape, factor_v.dtype),
            pltpu.SemaphoreType.DMA((2, chunks)),
        ],
        compiler_params=pltpu.CompilerParams(vmem_limit_bytes=PACK_VMEM),
    )(factor_u, factor_v)
    def head_step(lengths):
        return pl.pallas_call(
            head_kernel,
            out_shape=jax.ShapeDtypeStruct((tok_cap, tok_cap), jnp.float32),
            in_specs=[hbm, vmem],
            out_specs=vmem,
            compiler_params=score_params,
            cost_estimate=pl.CostEstimate(
                flops=1, bytes_accessed=1, transcendentals=0
            ),
        )(lengths, layer_inputs)

    def norm_step(lengths, head):
        return pl.pallas_call(
            functools.partial(norm_kernel, seq_dev),
            out_shape=[
                jax.ShapeDtypeStruct((1, tok_cap), jnp.float32),
                jax.ShapeDtypeStruct((8, tok_cap), jnp.float32),
            ],
            in_specs=[hbm, vmem, vmem, vmem],
            out_specs=[vmem, vmem],
            scratch_shapes=[pltpu.SMEM(seq_lengths.shape, seq_lengths.dtype), pltpu.SemaphoreType.DMA],
            compiler_params=score_params,
            cost_estimate=pl.CostEstimate(
                flops=1, bytes_accessed=1,
                transcendentals=0,
            ),
        )(lengths, head, out_grads, layer_inputs)

    frows = devices * rank_rows
    cost = pl.CostEstimate(
        flops=1, bytes_accessed=1, transcendentals=0
    )

    def partial_step(blocks):
        arrays, places = refs_of(blocks)
        return pl.pallas_call(
            functools.partial(partial_kernel, rank_rows, paired, places),
            out_shape=jax.ShapeDtypeStruct((2, tok_cap, frows), jnp.float32),
            in_specs=[vmem] * (2 + len(arrays)),
            out_specs=vmem,
            compiler_params=score_params,
            cost_estimate=cost,
        )(out_grads, layer_inputs, *arrays)

    if paired:
        other, normed, partial = gather_blocks(
            packed[0], packed[1], devices, seq_lengths, head_step, norm_step, partial_step
        )
    else:
        normed = norm_step(seq_lengths, head_step(seq_lengths))
        gathered = lax.all_gather(packed[0], "seq", axis=0, tiled=True)
        partial = partial_step([(gathered, 2 * PACK * b) for b in range(devices)])
        other = [(gathered, 2 * PACK * b + PACK) for b in range(devices)]
    arrays, places = refs_of(other)
    return pl.pallas_call(
        functools.partial(score_kernel, rank_rows, paired, places),
        out_shape=jax.ShapeDtypeStruct((queries, seq_dev), jnp.float32),
        in_specs=[vmem] * (5 + len(arrays)),
        out_specs=vmem,
        compiler_params=score_params,
        cost_estimate=cost,
    )(*normed, partial, out_grads, layer_inputs, *arrays)


def solution(mesh):
    in_specs = (
        P(("grp", "seq"), None),
        P(("grp", "seq"), None),
        P("seq", None),
        P("seq", None),
        P("grp"),
    )
    out_specs = P(None, ("grp", "seq"))
    return jax.shard_map(local, mesh=mesh, in_specs=in_specs, out_specs=out_specs, check_vma=False)
```

time: 50.4 us -> 50 us (level)
  waiting for transfers between devices: 15.9 us -> 14.5 us
  starting transfers between devices: 20 us -> 21.4 us
    ppermute x11, waiting for transfers between devices: 6.72 us -> 3.81 us  [swap(): return lax.ppermute(value, 'seq', [(i, i ^ mask) for i in range(devices)])]
    ppermute x11, starting transfers between devices: 14.1 us -> 16.2 us  [swap(): return lax.ppermute(value, 'seq', [(i, i ^ mask) for i in range(devices)])]
    ppermute x6 -> x4, waiting for transfers between devices: 9.15 us -> 10.7 us  [across(): return lax.ppermute(value, 'grp', [(0, 1), (1, 0)])]
    ppermute x6 -> x4, starting transfers between devices: 5.85 us -> 5.14 us  [across(): return lax.ppermute(value, 'grp', [(0, 1), (1, 0)])]
    pallas_call x3 -> x4, Pallas kernels: 8.19 us -> 7.83 us  [the longest x1 2.79 us: local(): pl.pallas_call(functools.partial(score_kernel, rank_rows, paired, places)...]
    unnamed x18 -> x20, local copies, waits for them, and re-layouts: 4.19 us -> 3.86 us
  transfers between devices with their start and end apart: 17 -> 15, of which waited for: 7 -> 7; matrix products, arithmetic and copies ran while one was open for 2% -> 0% of each run, Pallas kernels for 10% -> 10%
where the time goes in v4:
time: 50 us; the launch traced here: 49.8 us
  starting transfers between devices  21.4 us (43%)
  waiting for transfers between devices  14.5 us (29%)
  Pallas kernels  9.82 us (20%)
  local copies, waits for them, and re-layouts  3.91 us (8%)
    ppermute x11, starting transfers between devices, swap(): return lax.ppermute(value, 'seq', [(i, i ^ mask) for i in range(devices)])  16.2 us
    ppermute x4, waiting for transfers between devices, across(): return lax.ppermute(value, 'grp', [(0, 1), (1, 0)])  10.7 us
    ppermute x4, starting transfers between devices, across(): return lax.ppermute(value, 'grp', [(0, 1), (1, 0)])  5.14 us
    unnamed x20, local copies, waits for them, and re-layouts  3.86 us
    ppermute x11, waiting for transfers between devices, swap(): return lax.ppermute(value, 'seq', [(i, i ^ mask) for i in range(devices)])  3.81 us
    pallas_call x1, Pallas kernels, local(): pl.pallas_call(functools.partial(score_kernel, rank_rows, paired, places)...  2.79 us
    pallas_call x1, Pallas kernels, norm_step(): pl.pallas_call(functools.partial(norm_kernel, seq_dev), out_shape=[jax.Sh...  2.44 us
    pallas_call x1, Pallas kernels, local(): pl.pallas_call(functools.partial(pack_kernel, chunks, paired), out_shape=...  1.99 us
  transfers between devices with their start and end apart: 15, of which 7 were waited for; matrix products, arithmetic and copies ran while one was open for 0% of the time, Pallas kernels for 10%

profile of v4, /device:TPU:0, one launch (start us, length us, event | category | flops | bytes accessed | tf_op | source)
XLA Modules:
  0.0 49.8 jit_solution(13622978739034272398)
XLA Ops:
  0.0 2.0 %shard_map.55 = (bf16[32,4608]{1,0:T(8,128)(2,1)}, bf16[16,4608]{1,0:T(8,128)(2,1)}) custom-call(bf16[4,8192]{1,0:T(4,128)(2,1)} %u_hbm.1, bf16[4,28672]{1,0:T(4,128)(2,1)} %v_hbm.1), custom_call_target="tpu_custom_call" | custom-call | tf_op jit(solution)/shard_map/pallas_call | solution.py:240
  2.0 0.5 %collective-permute-start.1 = (bf16[32,4608]{1,0:T(8,128)(2,1)}, bf16[32,4608]{1,0:T(8,128)(2,1)S(1)}, u32[]{:S(2)}, u32[]{:S(2)}) collective-permute-start(bf16[32,4608]{1,0:T(8,128)(2,1)} %get-tuple-element.28.refs_0_), channel_id=1, source_target_pairs={{0,1},{1,0},{2,3},{3,2},{4,5},{5,4},{6,7},{7,6},{8,9},{9,8},{10,11... | collective-permute-start | bytes 884744 | tf_op jit(solution)/shard_map/ppermute | solution.py:177
  2.5 2.6 %collective-permute-start = (bf16[16,4608]{1,0:T(8,128)(2,1)}, bf16[16,4608]{1,0:T(8,128)(2,1)S(1)}, u32[]{:S(2)}, u32[]{:S(2)}) collective-permute-start(bf16[16,4608]{1,0:T(8,128)(2,1)} %get-tuple-element.29), channel_id=1, source_target_pairs={{0,4},{1,5},{2,6},{3,7},{4,0},{5,1},{6,2},{7,3},{8,12},{9,13},{10,... | collective-permute-start | bytes 442376 | tf_op jit(solution)/shard_map/ppermute | solution.py:177
  5.2 1.5 %collective-permute-start.6 = (bf16[32,4608]{1,0:T(8,128)(2,1)}, bf16[32,4608]{1,0:T(8,128)(2,1)S(1)}, u32[]{:S(2)}, u32[]{:S(2)}) collective-permute-start(bf16[32,4608]{1,0:T(8,128)(2,1)} %get-tuple-element.28.refs_0_), channel_id=1, source_target_pairs={{0,2},{1,3},{2,0},{3,1},{4,6},{5,7},{6,4},{7,5},{8,10},{9,11},{10,... | collective-permute-start | bytes 884744 | tf_op jit(solution)/shard_map/ppermute | solution.py:177
  6.7 2.6 %collective-permute-start.3 = (bf16[16,4608]{1,0:T(8,128)(2,1)}, bf16[16,4608]{1,0:T(8,128)(2,1)S(1)}, u32[]{:S(2)}, u32[]{:S(2)}) collective-permute-start(bf16[16,4608]{1,0:T(8,128)(2,1)} %get-tuple-element.29), channel_id=1, source_target_pairs={{0,8},{1,9},{2,10},{3,11},{4,12},{5,13},{6,14},{7,15},{8,0},{9,1},... | collective-permute-start | bytes 442376 | tf_op jit(solution)/shard_map/ppermute | solution.py:177
  9.3 0.5 %collective-permute-done = bf16[16,4608]{1,0:T(8,128)(2,1)S(1)} collective-permute-done((bf16[16,4608]{1,0:T(8,128)(2,1)}, bf16[16,4608]{1,0:T(8,128)(2,1)S(1)}, u32[]{:S(2)}, u32[]{:S(2)}) %collective-permute-start) | collective-permute-done | bytes 147488 | tf_op jit(solution)/shard_map/ppermute | solution.py:177
  9.8 4.5 %collective-permute-start.5 = (bf16[16,4608]{1,0:T(8,128)(2,1)S(1)}, bf16[16,4608]{1,0:T(8,128)(2,1)S(1)}, u32[]{:S(2)}, u32[]{:S(2)}) collective-permute-start(bf16[16,4608]{1,0:T(8,128)(2,1)S(1)} %collective-permute-done), channel_id=1, source_target_pairs={{0,2},{1,3},{2,0},{3,1},{4,6},{5,7},{6,4},{7,5},{8,10},{9,11},{10,... | collective-permute-start | bytes 442376 | tf_op jit(solution)/shard_map/ppermute | solution.py:177
  14.3 1.5 %collective-permute-start.4 = (bf16[16,4608]{1,0:T(8,128)(2,1)S(1)}, bf16[16,4608]{1,0:T(8,128)(2,1)S(1)}, u32[]{:S(2)}, u32[]{:S(2)}) collective-permute-start(bf16[16,4608]{1,0:T(8,128)(2,1)S(1)} %collective-permute-done), channel_id=1, source_target_pairs={{0,16},{16,0},{1,17},{17,1},{2,18},{18,2},{3,19},{19,3},{4,20},{20... | collective-permute-start | bytes 442376 | tf_op jit(solution)/shard_map/ppermute | solution.py:180
  15.8 2.5 %collective-permute-start.2 = (bf16[16,4608]{1,0:T(8,128)(2,1)}, bf16[16,4608]{1,0:T(8,128)(2,1)S(1)}, u32[]{:S(2)}, u32[]{:S(2)}) collective-permute-start(bf16[16,4608]{1,0:T(8,128)(2,1)} %get-tuple-element.29), channel_id=1, source_target_pairs={{0,12},{1,13},{2,14},{3,15},{4,8},{5,9},{6,10},{7,11},{8,4},{9,5},... | collective-permute-start | bytes 442376 | tf_op jit(solution)/shard_map/ppermute | solution.py:177
  18.3 1.2 %collective-permute-done.4 = bf16[16,4608]{1,0:T(8,128)(2,1)S(1)} collective-permute-done((bf16[16,4608]{1,0:T(8,128)(2,1)S(1)}, bf16[16,4608]{1,0:T(8,128)(2,1)S(1)}, u32[]{:S(2)}, u32[]{:S(2)}) %collective-permute-start.4) | collective-permute-done | bytes 147488 | tf_op jit(solution)/shard_map/ppermute | solution.py:180
  19.5 1.6 %collective-permute-start.8 = (bf16[32,4608]{1,0:T(8,128)(2,1)S(1)}, bf16[32,4608]{1,0:T(8,128)(2,1)S(1)}, u32[]{:S(2)}, u32[]{:S(2)}) collective-permute-start(bf16[32,4608]{1,0:T(8,128)(2,1)S(1)} %pad_maximum_fusion), channel_id=1, source_target_pairs={{0,16},{16,0},{1,17},{17,1},{2,18},{18,2},{3,19},{19,3},{4,20},{20... | collective-permute-start | bytes 884744 | tf_op jit(solution)/shard_map/ppermute | solution.py:180
  21.3 3.1 %copy-done = bf16[128,28672]{1,0:T(8,128)(2,1)S(1)} copy-done((bf16[128,28672]{1,0:T(8,128)(2,1)S(1)}, bf16[128,28672]{1,0:T(8,128)(2,1)}, u32[]{:S(2)}) %copy-start) | copy-done | bytes 7340056
  24.3 0.7 %copy-done.3 = s32[64]{0:T(128)S(1)} copy-done((s32[64]{0:T(128)S(1)}, s32[64]{0:T(128)}, u32[]{:S(2)}) %copy-start.3) | copy-done | bytes 280
  25.0 0.7 %shard_map.56.head_ref = f32[128,128]{1,0:T(8,128)S(1)} custom-call(s32[64]{0:T(128)S(1)} %copy-done.3, bf16[128,28672]{1,0:T(8,128)(2,1)S(1)} %copy-done), custom_call_target="tpu_custom_call" | custom-call | flops 1 | bytes 1 | tf_op jit(solution)/shard_map/pallas_call | solution.py:254
  25.7 1.0 %collective-permute-done.8 = bf16[32,4608]{1,0:T(8,128)(2,1)S(1)} collective-permute-done((bf16[32,4608]{1,0:T(8,128)(2,1)S(1)}, bf16[32,4608]{1,0:T(8,128)(2,1)S(1)}, u32[]{:S(2)}, u32[]{:S(2)}) %collective-permute-start.8) | collective-permute-done | bytes 294944 | tf_op jit(solution)/shard_map/ppermute | solution.py:180
  26.7 1.7 %collective-permute-start.9 = (bf16[16,4608]{1,0:T(8,128)(2,1)S(1)}, bf16[16,4608]{1,0:T(8,128)(2,1)S(1)}, u32[]{:S(2)}, u32[]{:S(2)}) collective-permute-start(bf16[16,4608]{1,0:T(8,128)(2,1)S(1)} %collective-permute-done.2), channel_id=1, source_target_pairs={{0,2},{1,3},{2,0},{3,1},{4,6},{5,7},{6,4},{7,5},{8,10},{9,11},{10,... | collective-permute-start | bytes 442376 | tf_op jit(solution)/shard_map/ppermute | solution.py:177
  28.5 2.4 %shard_map.57 = (f32[1,128]{1,0:T(1,128)S(1)}, f32[8,128]{1,0:T(8,128)S(1)}) custom-call(s32[64]{0:T(128)S(1)} %copy-done.3, f32[128,128]{1,0:T(8,128)S(1)} %shard_map.56.head_ref, bf16[128,8192]{1,0:T(8,128)(2,1)S(1)} %copy-done.1, bf16[128,28672]{1,0:T(8,128)(2,1)S(1)} %copy-done), custom_call_target="tpu_custom_call" | custom-call | flops 1 | bytes 1 | tf_op jit(solution)/shard_map/pallas_call | solution.py:266
  31.0 1.4 %collective-permute-done.9 = bf16[16,4608]{1,0:T(8,128)(2,1)S(1)} collective-permute-done((bf16[16,4608]{1,0:T(8,128)(2,1)S(1)}, bf16[16,4608]{1,0:T(8,128)(2,1)S(1)}, u32[]{:S(2)}, u32[]{:S(2)}) %collective-permute-start.9) | collective-permute-done | bytes 147488 | tf_op jit(solution)/shard_map/ppermute | solution.py:177
  32.5 1.1 %collective-permute-start.10 = (bf16[32,4608]{1,0:T(8,128)(2,1)S(1)}, bf16[32,4608]{1,0:T(8,128)(2,1)S(1)}, u32[]{:S(2)}, u32[]{:S(2)}) collective-permute-start(bf16[32,4608]{1,0:T(8,128)(2,1)S(1)} %pad_maximum_fusion.1), channel_id=1, source_target_pairs={{0,16},{16,0},{1,17},{17,1},{2,18},{18,2},{3,19},{19,3},{4,20},{20... | collective-permute-start | bytes 884744 | tf_op jit(solution)/shard_map/ppermute | solution.py:180
  33.6 1.0 %collective-permute-start.11 = (bf16[16,4608]{1,0:T(8,128)(2,1)S(1)}, bf16[16,4608]{1,0:T(8,128)(2,1)S(1)}, u32[]{:S(2)}, u32[]{:S(2)}) collective-permute-start(bf16[16,4608]{1,0:T(8,128)(2,1)S(1)} %collective-permute-done.9), channel_id=1, source_target_pairs={{0,16},{16,0},{1,17},{17,1},{2,18},{18,2},{3,19},{19,3},{4,20},{20... | collective-permute-start | bytes 442376 | tf_op jit(solution)/shard_map/ppermute | solution.py:180
  34.7 1.9 %shard_map.58.held_ref = f32[2,128,64]{2,1,0:T(8,128)S(1)} custom-call(bf16[128,8192]{1,0:T(8,128)(2,1)S(1)} %copy-done.1, bf16[128,28672]{1,0:T(8,128)(2,1)S(1)} %bitcast.1, bf16[32,4608]{1,0:T(8,128)(2,1)S(1)} %copy-done.2, bf16[32,4608]{1,0:T(8,128)(2,1)S(1)} %collective-permute-done.1.refs_1_, ...), custom_call_target="tpu_custom_call" | custom-call | flops 1 | bytes 1 | tf_op jit(solution)/shard_map/pallas_call | solution.py:289
  36.6 8.5 %collective-permute-done.11 = bf16[16,4608]{1,0:T(8,128)(2,1)S(1)} collective-permute-done((bf16[16,4608]{1,0:T(8,128)(2,1)S(1)}, bf16[16,4608]{1,0:T(8,128)(2,1)S(1)}, u32[]{:S(2)}, u32[]{:S(2)}) %collective-permute-start.11) | collective-permute-done | bytes 147488 | tf_op jit(solution)/shard_map/ppermute | solution.py:180
  45.3 1.8 %collective-permute-done.14.refs_7_ = bf16[48,4608]{1,0:T(8,128)(2,1)S(1)} collective-permute-done((bf16[48,4608]{1,0:T(8,128)(2,1)S(1)}, bf16[48,4608]{1,0:T(8,128)(2,1)S(1)}, u32[]{:S(2)}, u32[]{:S(2)}) %collective-permute-start.14) | collective-permute-done | bytes 442400 | tf_op jit(solution)/shard_map/ppermute | solution.py:177
  47.0 2.8 %shard_map.59 = f32[2,4]{1,0:T(2,128)} custom-call(f32[1,128]{1,0:T(1,128)S(1)} %get-tuple-element.38.norm_ref, f32[8,128]{1,0:T(8,128)S(1)} %get-tuple-element.39.member_ref, f32[2,128,64]{2,1,0:T(8,128)S(1)} %shard_map.58.held_ref, bf16[128,8192]{1,0:T(8,128)(2,1)S(1)} %copy-done.1, bf16[128,28672]{1,0:T(8,128)(2,1)S(1)} %bitcast.1, ...), custom_call_target="tpu_custom_call" | custom-call | flops 1 | bytes 1 | tf_op jit(solution)/shard_map/pallas_call | solution.py:308
  (37 shorter events, 0.5 us)
Async XLA Ops:
  0.0 28.5 %copy-start.1 = (bf16[128,8192]{1,0:T(8,128)(2,1)S(1)}, bf16[128,8192]{1,0:T(8,128)(2,1)}, u32[]{:S(2)}) copy-start(bf16[128,8192]{1,0:T(8,128)(2,1)} %out_ref.5) | copy-start | bytes 6291460
  2.0 7.8 %collective-permute-start.1 = (bf16[32,4608]{1,0:T(8,128)(2,1)}, bf16[32,4608]{1,0:T(8,128)(2,1)S(1)}, u32[]{:S(2)}, u32[]{:S(2)}) collective-permute-start(bf16[32,4608]{1,0:T(8,128)(2,1)} %get-tuple-element.28.refs_0_), channel_id=1, source_target_pairs={{0,1},{1,0},{2,3},{3,2},{4,5},{5,4},{6,7},{7,6},{8,9},{9,8},{10,11... | collective-permute-start | bytes 884744 | tf_op jit(solution)/shard_map/ppermute | solution.py:177
  2.5 7.3 %collective-permute-start = (bf16[16,4608]{1,0:T(8,128)(2,1)}, bf16[16,4608]{1,0:T(8,128)(2,1)S(1)}, u32[]{:S(2)}, u32[]{:S(2)}) collective-permute-start(bf16[16,4608]{1,0:T(8,128)(2,1)} %get-tuple-element.29), channel_id=1, source_target_pairs={{0,4},{1,5},{2,6},{3,7},{4,0},{5,1},{6,2},{7,3},{8,12},{9,13},{10,... | collective-permute-start | bytes 442376 | tf_op jit(solution)/shard_map/ppermute | solution.py:177
  5.2 13.1 %collective-permute-start.6 = (bf16[32,4608]{1,0:T(8,128)(2,1)}, bf16[32,4608]{1,0:T(8,128)(2,1)S(1)}, u32[]{:S(2)}, u32[]{:S(2)}) collective-permute-start(bf16[32,4608]{1,0:T(8,128)(2,1)} %get-tuple-element.28.refs_0_), channel_id=1, source_target_pairs={{0,2},{1,3},{2,0},{3,1},{4,6},{5,7},{6,4},{7,5},{8,10},{9,11},{10,... | collective-permute-start | bytes 884744 | tf_op jit(solution)/shard_map/ppermute | solution.py:177
  6.7 11.6 %collective-permute-start.3 = (bf16[16,4608]{1,0:T(8,128)(2,1)}, bf16[16,4608]{1,0:T(8,128)(2,1)S(1)}, u32[]{:S(2)}, u32[]{:S(2)}) collective-permute-start(bf16[16,4608]{1,0:T(8,128)(2,1)} %get-tuple-element.29), channel_id=1, source_target_pairs={{0,8},{1,9},{2,10},{3,11},{4,12},{5,13},{6,14},{7,15},{8,0},{9,1},... | collective-permute-start | bytes 442376 | tf_op jit(solution)/shard_map/ppermute | solution.py:177
  9.8 8.5 %collective-permute-start.5 = (bf16[16,4608]{1,0:T(8,128)(2,1)S(1)}, bf16[16,4608]{1,0:T(8,128)(2,1)S(1)}, u32[]{:S(2)}, u32[]{:S(2)}) collective-permute-start(bf16[16,4608]{1,0:T(8,128)(2,1)S(1)} %collective-permute-done), channel_id=1, source_target_pairs={{0,2},{1,3},{2,0},{3,1},{4,6},{5,7},{6,4},{7,5},{8,10},{9,11},{10,... | collective-permute-start | bytes 442376 | tf_op jit(solution)/shard_map/ppermute | solution.py:177
  14.3 5.1 %collective-permute-start.4 = (bf16[16,4608]{1,0:T(8,128)(2,1)S(1)}, bf16[16,4608]{1,0:T(8,128)(2,1)S(1)}, u32[]{:S(2)}, u32[]{:S(2)}) collective-permute-start(bf16[16,4608]{1,0:T(8,128)(2,1)S(1)} %collective-permute-done), channel_id=1, source_target_pairs={{0,16},{16,0},{1,17},{17,1},{2,18},{18,2},{3,19},{19,3},{4,20},{20... | collective-permute-start | bytes 442376 | tf_op jit(solution)/shard_map/ppermute | solution.py:180
  15.8 9.9 %collective-permute-start.2 = (bf16[16,4608]{1,0:T(8,128)(2,1)}, bf16[16,4608]{1,0:T(8,128)(2,1)S(1)}, u32[]{:S(2)}, u32[]{:S(2)}) collective-permute-start(bf16[16,4608]{1,0:T(8,128)(2,1)} %get-tuple-element.29), channel_id=1, source_target_pairs={{0,12},{1,13},{2,14},{3,15},{4,8},{5,9},{6,10},{7,11},{8,4},{9,5},... | collective-permute-start | bytes 442376 | tf_op jit(solution)/shard_map/ppermute | solution.py:177
  19.5 6.2 %collective-permute-start.7 = (bf16[16,4608]{1,0:T(8,128)(2,1)S(1)}, bf16[16,4608]{1,0:T(8,128)(2,1)S(1)}, u32[]{:S(2)}, u32[]{:S(2)}) collective-permute-start(bf16[16,4608]{1,0:T(8,128)(2,1)S(1)} %collective-permute-done.3), channel_id=1, source_target_pairs={{0,2},{1,3},{2,0},{3,1},{4,6},{5,7},{6,4},{7,5},{8,10},{9,11},{10,... | collective-permute-start | bytes 442376 | tf_op jit(solution)/shard_map/ppermute | solution.py:177
  19.5 7.2 %collective-permute-start.8 = (bf16[32,4608]{1,0:T(8,128)(2,1)S(1)}, bf16[32,4608]{1,0:T(8,128)(2,1)S(1)}, u32[]{:S(2)}, u32[]{:S(2)}) collective-permute-start(bf16[32,4608]{1,0:T(8,128)(2,1)S(1)} %pad_maximum_fusion), channel_id=1, source_target_pairs={{0,16},{16,0},{1,17},{17,1},{2,18},{18,2},{3,19},{19,3},{4,20},{20... | collective-permute-start | bytes 884744 | tf_op jit(solution)/shard_map/ppermute | solution.py:180
  21.2 13.4 %collective-permute-start.12 = (bf16[96,4608]{1,0:T(8,128)(2,1)S(1)}, bf16[96,4608]{1,0:T(8,128)(2,1)S(1)}, u32[]{:S(2)}, u32[]{:S(2)}) collective-permute-start(bf16[96,4608]{1,0:T(8,128)(2,1)S(1)} %constant_dynamic-update-slice_fusion.refs_2_), channel_id=1, source_target_pairs={{0,1},{1,0},{2,3},{3,2},{4,5},{5,4},{6,7},{7,6},{8,9},{9,8},{10,11... | collective-permute-start | bytes 2654216 | tf_op jit(solution)/shard_map/ppermute | solution.py:177
  21.3 3.1 %copy-start = (bf16[128,28672]{1,0:T(8,128)(2,1)S(1)}, bf16[128,28672]{1,0:T(8,128)(2,1)}, u32[]{:S(2)}) copy-start(bf16[128,28672]{1,0:T(8,128)(2,1)} %in_ref.7) | copy-start | bytes 22020100
  24.3 0.7 %copy-start.3 = (s32[64]{0:T(128)S(1)}, s32[64]{0:T(128)}, u32[]{:S(2)}) copy-start(s32[64]{0:T(128)} %lengths_hbm) | copy-start | bytes 772
  25.0 9.7 %slice-start = ((s8[7340032]{0:T(1024)(128)(4,1)}), s8[4194304]{0:T(1024)(128)(4,1)S(1)}, s32[]{:S(2)}) async-start(s8[7340032]{0:T(1024)(128)(4,1)} %bitcast), calls=%async_computation | async-start | bytes 8388608
  25.7 9.0 %copy-start.2 = (bf16[32,4608]{1,0:T(8,128)(2,1)S(1)}, bf16[32,4608]{1,0:T(8,128)(2,1)}, u32[]{:S(2)}) copy-start(bf16[32,4608]{1,0:T(8,128)(2,1)} %get-tuple-element.28.refs_0_) | copy-start | bytes 884740
  26.7 5.6 %collective-permute-start.9 = (bf16[16,4608]{1,0:T(8,128)(2,1)S(1)}, bf16[16,4608]{1,0:T(8,128)(2,1)S(1)}, u32[]{:S(2)}, u32[]{:S(2)}) collective-permute-start(bf16[16,4608]{1,0:T(8,128)(2,1)S(1)} %collective-permute-done.2), channel_id=1, source_target_pairs={{0,2},{1,3},{2,0},{3,1},{4,6},{5,7},{6,4},{7,5},{8,10},{9,11},{10,... | collective-permute-start | bytes 442376 | tf_op jit(solution)/shard_map/ppermute | solution.py:177
  28.5 6.2 %slice-start.1 = ((s8[7340032]{0:T(1024)(128)(4,1)}), s8[3145728]{0:T(1024)(128)(4,1)S(1)}, s32[]{:S(2)}) async-start(s8[7340032]{0:T(1024)(128)(4,1)} %bitcast), calls=%async_computation.1 | async-start | bytes 6291456
  32.4 2.3 %collective-permute-start.13 = (bf16[80,4608]{1,0:T(8,128)(2,1)S(1)}, bf16[80,4608]{1,0:T(8,128)(2,1)S(1)}, u32[]{:S(2)}, u32[]{:S(2)}) collective-permute-start(bf16[80,4608]{1,0:T(8,128)(2,1)S(1)} %constant_dynamic-update-slice_fusion.5.refs_4_), channel_id=1, source_target_pairs={{0,1},{1,0},{2,3},{3,2},{4,5},{5,4},{6,7},{7,6},{8,9},{9,8},{10,11... | collective-permute-start | bytes 2211848 | tf_op jit(solution)/shard_map/ppermute | solution.py:177
  32.5 12.6 %collective-permute-start.10 = (bf16[32,4608]{1,0:T(8,128)(2,1)S(1)}, bf16[32,4608]{1,0:T(8,128)(2,1)S(1)}, u32[]{:S(2)}, u32[]{:S(2)}) collective-permute-start(bf16[32,4608]{1,0:T(8,128)(2,1)S(1)} %pad_maximum_fusion.1), channel_id=1, source_target_pairs={{0,16},{16,0},{1,17},{17,1},{2,18},{18,2},{3,19},{19,3},{4,20},{20... | collective-permute-start | bytes 884744 | tf_op jit(solution)/shard_map/ppermute | solution.py:180
  33.6 11.6 %collective-permute-start.11 = (bf16[16,4608]{1,0:T(8,128)(2,1)S(1)}, bf16[16,4608]{1,0:T(8,128)(2,1)S(1)}, u32[]{:S(2)}, u32[]{:S(2)}) collective-permute-start(bf16[16,4608]{1,0:T(8,128)(2,1)S(1)} %collective-permute-done.9), channel_id=1, source_target_pairs={{0,16},{16,0},{1,17},{17,1},{2,18},{18,2},{3,19},{19,3},{4,20},{20... | collective-permute-start | bytes 442376 | tf_op jit(solution)/shard_map/ppermute | solution.py:180
  45.2 1.9 %collective-permute-start.14 = (bf16[48,4608]{1,0:T(8,128)(2,1)S(1)}, bf16[48,4608]{1,0:T(8,128)(2,1)S(1)}, u32[]{:S(2)}, u32[]{:S(2)}) collective-permute-start(bf16[48,4608]{1,0:T(8,128)(2,1)S(1)} %constant_dynamic-update-slice_fusion.9.refs_6_), channel_id=1, source_target_pairs={{0,1},{1,0},{2,3},{3,2},{4,5},{5,4},{6,7},{7,6},{8,9},{9,8},{10,11... | collective-permute-start | bytes 1327112 | tf_op jit(solution)/shard_map/ppermute | solution.py:177

commit v5 on v4

--- a/solution.py
+++ b/solution.py
@@ -29,20 +29,27 @@
     return lax.axis_index("seq") % chunks if paired else 0
 
 
-def pack_kernel(chunks, paired, u_hbm, v_hbm, both_ref, *refs):
-    *own_refs, u_ref, v_ref, sems = refs
-    copies = []
-    for i, (hbm, ref) in enumerate(((u_hbm, u_ref), (v_hbm, v_ref))):
-        wide = ref.shape[1] // chunks
-        for j in range(chunks):
-            cols = pl.ds(j * wide, wide)
-            copies.append(pltpu.make_async_copy(hbm.at[:, cols], ref.at[:, cols], sems.at[i, j]))
+def pack_kernel(chunks, paired, seq_dev, u_hbm, v_hbm, lengths_hbm, member_ref, both_ref, *refs):
+    *own_refs, u_ref, v_ref, lengths_ref, sems = refs
+    pairs = ((v_hbm, v_ref), (u_hbm, u_ref), (lengths_hbm, lengths_ref))
+    copies = [pltpu.make_async_copy(hbm, ref, sems.at[i]) for i, (hbm, ref) in enumerate(pairs)]
     for copy in copies:
         copy.start()
     for copy in copies:
         copy.wait()
+    seqs, tok_cap = member_ref.shape
+    which = lax.broadcasted_iota(jnp.int32, (seqs, tok_cap), 0)
+    position = lax.broadcasted_iota(jnp.int32, (seqs, tok_cap), 1)
+    member = jnp.zeros((seqs, tok_cap), jnp.float32)
+    low = 0
+    for k in range(seq_dev):
+        high = low + lengths_ref[lax.axis_index("seq") * seq_dev + k]
+        inside = (which == k) & (position >= low) & (position < high)
+        member = jnp.where(inside, 1.0, member)
+        low = high
+    member_ref[...] = member
     rank_rows = u_ref.shape[0]
-    member = lax.axis_index("seq") % chunks
+    turned = lax.axis_index("seq") % chunks
     wide_u, wide_v = u_ref.shape[1] // (2 * chunks), v_ref.shape[1] // (2 * chunks)
     for side in range(2):
         half = first_half(paired) ^ side
@@ -50,7 +57,7 @@
         for ref, wide in ((u_ref, wide_u), (v_ref, wide_v)):
             rows = []
             for g in range(chunks):
-                start = pl.multiple_of(((g ^ member) * 2 + half) * wide, 128)
+                start = pl.multiple_of(((g ^ turned) * 2 + half) * wide, 128)
                 rows.append(ref[:, pl.ds(start, wide)].astype(jnp.float32))
             piece = jnp.concatenate(rows, axis=0).astype(both_ref.dtype)
             both_ref[side * PACK : (side + 1) * PACK, place : place + wide] = piece
@@ -60,30 +67,17 @@
             place += wide
 
 
-def head_kernel(after_ref, in_ref, gram_ref):
+def head_kernel(member_ref, in_ref, gram_ref):
     head = in_ref[:, :HEAD]
     gram_ref[...] = inner_rows(head, head)
 
 
-def norm_kernel(seq_dev, lengths_hbm, head_ref, out_ref, in_ref, norm_ref, member_ref, lengths_ref, sem):
-    copy = pltpu.make_async_copy(lengths_hbm, lengths_ref, sem)
-    copy.start()
-    gram_out = inner_rows(out_ref[...], out_ref[...])
+def norm_kernel(member_ref, head_ref, out_ref, in_ref, norm_ref):
     tail = in_ref[:, HEAD:]
-    paired = gram_out * (head_ref[...] + inner_rows(tail, tail))
-    copy.wait()
-    seqs, tok_cap = member_ref.shape
-    which = lax.broadcasted_iota(jnp.int32, (seqs, tok_cap), 0)
-    position = lax.broadcasted_iota(jnp.int32, (seqs, tok_cap), 1)
-    block = lax.axis_index("seq")
-    member = jnp.zeros((seqs, tok_cap), jnp.float32)
-    low = 0
-    for k in range(seq_dev):
-        high = low + lengths_ref[block * seq_dev + k]
-        inside = (which == k) & (position >= low) & (position < high)
-        member = jnp.where(inside, 1.0, member)
-        low = high
-    member_ref[...] = member
+    paired = inner_rows(out_ref[...], out_ref[...]) * (head_ref[...] + inner_rows(tail, tail))
+    member = member_ref[...]
+    which = lax.broadcasted_iota(jnp.int32, member.shape, 0)
+    position = lax.broadcasted_iota(jnp.int32, member.shape, 1)
     sums = jnp.dot(
         member, paired, precision=lax.Precision.HIGHEST, preferred_element_type=jnp.float32
     )
@@ -172,7 +166,7 @@
         score_ref[q : q + 1, :] = row[:, : score_ref.shape[1]]
 
 
-def gather_blocks(both, own, devices, lengths, head_step, norm_step, partial_step):
+def gather_blocks(both, own, devices, member, head_step, norm_step, partial_step):
     def swap(value, mask):
         return lax.ppermute(value, "seq", [(i, i ^ mask) for i in range(devices)])
 
@@ -184,15 +178,15 @@
     z1, z2, y0, both_core = swap(own, 4), swap(own, 8), swap(both, 2), swap(both, 1)
     z1, both_core, own = gate(z1, both_core, own)
     x1, y1, z3 = across(z1), swap(z1, 2), swap(own, 12)
-    z2, x1, y1, y0, lengths = gate(z2, x1, y1, y0, lengths)
+    z2, x1, y1, y0, member = gate(z2, x1, y1, y0, member)
     x_near, y2 = across(stack(z2, y1)), swap(z2, 2)
-    head = head_step(lengths)
-    z3, y2, x_near, head, lengths = gate(z3, y2, x_near, head, lengths)
+    head = head_step(member)
+    z3, y2, head, member = gate(z3, y2, head, member)
     x_far, y3 = across(stack(z3, y2)), swap(z3, 2)
     early = stack(y0, z1, y1, z2, x1)
     early_core = swap(early, 1)
-    normed = norm_step(lengths, head)
-    y3, norms = gate(y3, normed[0])
+    norms = norm_step(member, head)
+    y3, norms = gate(y3, norms)
     x_last = across(y3)
     middle = stack(y2, z3, y3, x_near)
     middle_core = swap(middle, 1)
@@ -206,10 +200,10 @@
     place(early, early_core, ((mine, 2), (other, 2), (mine, 4), (mine, 6), (mine, 8), (other, 4)))
     place(middle, middle_core, ((mine, 10), (mine, 12), (mine, 14), (other, 8), (other, 6)))
     partial = partial_step([mine[b] for b in range(devices)])
-    x_far, x_last, partial = gate(x_far, x_last, partial)
+    x_last, partial = gate(x_last, partial)
     late = stack(x_far, x_last)
     place(late, swap(late, 1), ((other, 12), (other, 10), (other, 14)))
-    return [other[b] for b in range(devices)], (norms, normed[1]), partial
+    return [other[b] for b in range(devices)], norms, partial
 
 
 def refs_of(blocks):
@@ -237,53 +231,48 @@
 
     score_params = pltpu.CompilerParams(vmem_limit_bytes=SCORE_VMEM)
     half_width = width // (2 * chunks)
-    packed = pl.pallas_call(
-        functools.partial(pack_kernel, chunks, paired),
-        out_shape=[jax.ShapeDtypeStruct((2 * PACK, half_width), factor_u.dtype)]
+    seqs = -(-seq_dev // 8) * 8
+    member, *packed = pl.pallas_call(
+        functools.partial(pack_kernel, chunks, paired, seq_dev),
+        out_shape=[
+            jax.ShapeDtypeStruct((seqs, tok_cap), jnp.float32),
+            jax.ShapeDtypeStruct((2 * PACK, half_width), factor_u.dtype),
+        ]
         + [jax.ShapeDtypeStruct((PACK, half_width), factor_u.dtype)] * paired,
-        in_specs=[hbm, hbm],
-        out_specs=[vmem] * (1 + paired),
+        in_specs=[hbm] * 3,
+        out_specs=[vmem] * (2 + paired),
         scratch_shapes=[
             pltpu.VMEM(factor_u.shape, factor_u.dtype),
             pltpu.VMEM(factor_v.shape, factor_v.dtype),
-            pltpu.SemaphoreType.DMA((2, chunks)),
+            pltpu.SMEM(seq_lengths.shape, seq_lengths.dtype),
+            pltpu.SemaphoreType.DMA((3,)),
         ],
         compiler_params=pltpu.CompilerParams(vmem_limit_bytes=PACK_VMEM),
-    )(factor_u, factor_v)
-    def head_step(lengths):
+    )(factor_u, factor_v, seq_lengths)
+
+    tiny = pl.CostEstimate(flops=1, bytes_accessed=1, transcendentals=0)
+
+    def head_step(member):
         return pl.pallas_call(
             head_kernel,
             out_shape=jax.ShapeDtypeStruct((tok_cap, tok_cap), jnp.float32),
-            in_specs=[hbm, vmem],
+            in_specs=[vmem] * 2,
             out_specs=vmem,
             compiler_params=score_params,
-            cost_estimate=pl.CostEstimate(
-                flops=1, bytes_accessed=1, transcendentals=0
-            ),
-        )(lengths, layer_inputs)
-
-    def norm_step(lengths, head):
+            cost_estimate=tiny,
+        )(member, layer_inputs)
+
+    def norm_step(member, head):
         return pl.pallas_call(
-            functools.partial(norm_kernel, seq_dev),
-            out_shape=[
-                jax.ShapeDtypeStruct((1, tok_cap), jnp.float32),
-                jax.ShapeDtypeStruct((8, tok_cap), jnp.float32),
-            ],
-            in_specs=[hbm, vmem, vmem, vmem],
-            out_specs=[vmem, vmem],
-            scratch_shapes=[pltpu.SMEM(seq_lengths.shape, seq_lengths.dtype), pltpu.SemaphoreType.DMA],
+            norm_kernel,
+            out_shape=jax.ShapeDtypeStruct((1, tok_cap), jnp.float32),
+            in_specs=[vmem] * 4,
+            out_specs=vmem,
             compiler_params=score_params,
-            cost_estimate=pl.CostEstimate(
-                flops=1, bytes_accessed=1,
-                transcendentals=0,
-            ),
-        )(lengths, head, out_grads, layer_inputs)
+            cost_estimate=tiny,
+        )(member, head, out_grads, layer_inputs)
 
     frows = devices * rank_rows
-    cost = pl.CostEstimate(
-        flops=1, bytes_accessed=1, transcendentals=0
-    )
-
     def partial_step(blocks):
         arrays, places = refs_of(blocks)
         return pl.pallas_call(
@@ -292,15 +281,15 @@
             in_specs=[vmem] * (2 + len(arrays)),
             out_specs=vmem,
             compiler_params=score_params,
-            cost_estimate=cost,
+            cost_estimate=tiny,
         )(out_grads, layer_inputs, *arrays)
 
     if paired:
-        other, normed, partial = gather_blocks(
-            packed[0], packed[1], devices, seq_lengths, head_step, norm_step, partial_step
+        other, norms, partial = gather_blocks(
+            packed[0], packed[1], devices, member, head_step, norm_step, partial_step
         )
     else:
-        normed = norm_step(seq_lengths, head_step(seq_lengths))
+        norms = norm_step(member, head_step(member))
         gathered = lax.all_gather(packed[0], "seq", axis=0, tiled=True)
         partial = partial_step([(gathered, 2 * PACK * b) for b in range(devices)])
         other = [(gathered, 2 * PACK * b + PACK) for b in range(devices)]
@@ -311,8 +300,8 @@
         in_specs=[vmem] * (5 + len(arrays)),
         out_specs=vmem,
         compiler_params=score_params,
-        cost_estimate=cost,
-    )(*normed, partial, out_grads, layer_inputs, *arrays)
+        cost_estimate=tiny,
+    )(norms, member, partial, out_grads, layer_inputs, *arrays)
 
 
 def solution(mesh):

time: 50 us -> 45.1 us (0.902)
  waiting for transfers between devices: 14.5 us -> 10.1 us
  starting transfers between devices: 21.4 us -> 20.8 us
    ppermute x4, waiting for transfers between devices: 10.7 us -> 6.33 us  [across(): return lax.ppermute(value, 'grp', [(0, 1), (1, 0)])]
    ppermute x4, starting transfers between devices: 5.14 us -> 4.25 us  [across(): return lax.ppermute(value, 'grp', [(0, 1), (1, 0)])]
  transfers between devices with their start and end apart: 15 -> 15, of which waited for: 7 -> 6; matrix products, arithmetic and copies ran while one was open for 0% -> 0% of each run, Pallas kernels for 10% -> 11%
where the time goes in v5:
time: 45.1 us; the launch traced here: 45 us
  starting transfers between devices  20.8 us (46%)
  waiting for transfers between devices  10.1 us (22%)
  Pallas kernels  9.79 us (22%)
  local copies, waits for them, and re-layouts  3.93 us (9%)
    ppermute x11, starting transfers between devices, swap(): return lax.ppermute(value, 'seq', [(i, i ^ mask) for i in range(devices)])  16.6 us
    ppermute x4, waiting for transfers between devices, across(): return lax.ppermute(value, 'grp', [(0, 1), (1, 0)])  6.33 us
    ppermute x4, starting transfers between devices, across(): return lax.ppermute(value, 'grp', [(0, 1), (1, 0)])  4.25 us
    unnamed x20, local copies, waits for them, and re-layouts  3.88 us
    ppermute x11, waiting for transfers between devices, swap(): return lax.ppermute(value, 'seq', [(i, i ^ mask) for i in range(devices)])  3.81 us
    pallas_call x1, Pallas kernels, local(): pl.pallas_call(functools.partial(score_kernel, rank_rows, paired, places)...  2.83 us
    pallas_call x1, Pallas kernels, norm_step(): pl.pallas_call(norm_kernel, out_shape=jax.ShapeDtypeStruct((1, tok_cap),...  2.36 us
    pallas_call x1, Pallas kernels, local(): pl.pallas_call(functools.partial(pack_kernel, chunks, paired, seq_dev), o...  1.99 us
  transfers between devices with their start and end apart: 15, of which 6 were waited for; matrix products, arithmetic and copies ran while one was open for 0% of the time, Pallas kernels for 11%

profile of v5, /device:TPU:0, one launch (start us, length us, event | category | flops | bytes accessed | tf_op | source)
XLA Modules:
  0.0 45.0 jit_solution(9362876126692196505)
XLA Ops:
  0.0 2.0 %shard_map.55 = (f32[8,128]{1,0:T(8,128)}, bf16[32,4608]{1,0:T(8,128)(2,1)}, bf16[16,4608]{1,0:T(8,128)(2,1)}) custom-call(bf16[4,8192]{1,0:T(4,128)(2,1)} %u_hbm.1, bf16[4,28672]{1,0:T(4,128)(2,1)} %v_hbm.1, s32[64]{0:T(128)} %lengths_hbm.1), custom_call_target="tpu_custom_call" | custom-call | tf_op jit(solution)/shard_map/pallas_call | solution.py:235
  2.0 0.5 %collective-permute-start.1 = (bf16[32,4608]{1,0:T(8,128)(2,1)}, bf16[32,4608]{1,0:T(8,128)(2,1)S(1)}, u32[]{:S(2)}, u32[]{:S(2)}) collective-permute-start(bf16[32,4608]{1,0:T(8,128)(2,1)} %get-tuple-element.25.refs_0_), channel_id=1, source_target_pairs={{0,1},{1,0},{2,3},{3,2},{4,5},{5,4},{6,7},{7,6},{8,9},{9,8},{10,11... | collective-permute-start | bytes 884744 | tf_op jit(solution)/shard_map/ppermute | solution.py:171
  2.5 2.6 %collective-permute-start = (bf16[16,4608]{1,0:T(8,128)(2,1)}, bf16[16,4608]{1,0:T(8,128)(2,1)S(1)}, u32[]{:S(2)}, u32[]{:S(2)}) collective-permute-start(bf16[16,4608]{1,0:T(8,128)(2,1)} %get-tuple-element.26), channel_id=1, source_target_pairs={{0,4},{1,5},{2,6},{3,7},{4,0},{5,1},{6,2},{7,3},{8,12},{9,13},{10,... | collective-permute-start | bytes 442376 | tf_op jit(solution)/shard_map/ppermute | solution.py:171
  5.2 1.5 %collective-permute-start.6 = (bf16[32,4608]{1,0:T(8,128)(2,1)}, bf16[32,4608]{1,0:T(8,128)(2,1)S(1)}, u32[]{:S(2)}, u32[]{:S(2)}) collective-permute-start(bf16[32,4608]{1,0:T(8,128)(2,1)} %get-tuple-element.25.refs_0_), channel_id=1, source_target_pairs={{0,2},{1,3},{2,0},{3,1},{4,6},{5,7},{6,4},{7,5},{8,10},{9,11},{10,... | collective-permute-start | bytes 884744 | tf_op jit(solution)/shard_map/ppermute | solution.py:171
  6.7 2.6 %collective-permute-start.3 = (bf16[16,4608]{1,0:T(8,128)(2,1)}, bf16[16,4608]{1,0:T(8,128)(2,1)S(1)}, u32[]{:S(2)}, u32[]{:S(2)}) collective-permute-start(bf16[16,4608]{1,0:T(8,128)(2,1)} %get-tuple-element.26), channel_id=1, source_target_pairs={{0,8},{1,9},{2,10},{3,11},{4,12},{5,13},{6,14},{7,15},{8,0},{9,1},... | collective-permute-start | bytes 442376 | tf_op jit(solution)/shard_map/ppermute | solution.py:171
  9.3 0.5 %collective-permute-done = bf16[16,4608]{1,0:T(8,128)(2,1)S(1)} collective-permute-done((bf16[16,4608]{1,0:T(8,128)(2,1)}, bf16[16,4608]{1,0:T(8,128)(2,1)S(1)}, u32[]{:S(2)}, u32[]{:S(2)}) %collective-permute-start) | collective-permute-done | bytes 147488 | tf_op jit(solution)/shard_map/ppermute | solution.py:171
  9.8 4.5 %collective-permute-start.5 = (bf16[16,4608]{1,0:T(8,128)(2,1)S(1)}, bf16[16,4608]{1,0:T(8,128)(2,1)S(1)}, u32[]{:S(2)}, u32[]{:S(2)}) collective-permute-start(bf16[16,4608]{1,0:T(8,128)(2,1)S(1)} %collective-permute-done), channel_id=1, source_target_pairs={{0,2},{1,3},{2,0},{3,1},{4,6},{5,7},{6,4},{7,5},{8,10},{9,11},{10,... | collective-permute-start | bytes 442376 | tf_op jit(solution)/shard_map/ppermute | solution.py:171
  14.3 1.5 %collective-permute-start.4 = (bf16[16,4608]{1,0:T(8,128)(2,1)S(1)}, bf16[16,4608]{1,0:T(8,128)(2,1)S(1)}, u32[]{:S(2)}, u32[]{:S(2)}) collective-permute-start(bf16[16,4608]{1,0:T(8,128)(2,1)S(1)} %collective-permute-done), channel_id=1, source_target_pairs={{0,16},{16,0},{1,17},{17,1},{2,18},{18,2},{3,19},{19,3},{4,20},{20... | collective-permute-start | bytes 442376 | tf_op jit(solution)/shard_map/ppermute | solution.py:174
  15.8 2.5 %collective-permute-start.2 = (bf16[16,4608]{1,0:T(8,128)(2,1)}, bf16[16,4608]{1,0:T(8,128)(2,1)S(1)}, u32[]{:S(2)}, u32[]{:S(2)}) collective-permute-start(bf16[16,4608]{1,0:T(8,128)(2,1)} %get-tuple-element.26), channel_id=1, source_target_pairs={{0,12},{1,13},{2,14},{3,15},{4,8},{5,9},{6,10},{7,11},{8,4},{9,5},... | collective-permute-start | bytes 442376 | tf_op jit(solution)/shard_map/ppermute | solution.py:171
  18.3 1.2 %collective-permute-done.4 = bf16[16,4608]{1,0:T(8,128)(2,1)S(1)} collective-permute-done((bf16[16,4608]{1,0:T(8,128)(2,1)S(1)}, bf16[16,4608]{1,0:T(8,128)(2,1)S(1)}, u32[]{:S(2)}, u32[]{:S(2)}) %collective-permute-start.4) | collective-permute-done | bytes 147488 | tf_op jit(solution)/shard_map/ppermute | solution.py:174
  19.5 1.6 %collective-permute-start.11 = (bf16[32,4608]{1,0:T(8,128)(2,1)S(1)}, bf16[32,4608]{1,0:T(8,128)(2,1)S(1)}, u32[]{:S(2)}, u32[]{:S(2)}) collective-permute-start(bf16[32,4608]{1,0:T(8,128)(2,1)S(1)} %pad_maximum_fusion), channel_id=1, source_target_pairs={{0,16},{16,0},{1,17},{17,1},{2,18},{18,2},{3,19},{19,3},{4,20},{20... | collective-permute-start | bytes 884744 | tf_op jit(solution)/shard_map/ppermute | solution.py:174
  21.3 3.1 %copy-done = bf16[128,28672]{1,0:T(8,128)(2,1)S(1)} copy-done((bf16[128,28672]{1,0:T(8,128)(2,1)S(1)}, bf16[128,28672]{1,0:T(8,128)(2,1)}, u32[]{:S(2)}) %copy-start) | copy-done | bytes 7340056
  24.3 0.7 %copy-done.3 = f32[8,128]{1,0:T(8,128)S(1)} copy-done((f32[8,128]{1,0:T(8,128)S(1)}, f32[8,128]{1,0:T(8,128)}, u32[]{:S(2)}) %copy-start.3) | copy-done | bytes 4120
  25.0 0.7 %shard_map.56.head_ref = f32[128,128]{1,0:T(8,128)S(1)} custom-call(f32[8,128]{1,0:T(8,128)S(1)} %copy-done.3, bf16[128,28672]{1,0:T(8,128)(2,1)S(1)} %copy-done), custom_call_target="tpu_custom_call" | custom-call | flops 1 | bytes 1 | tf_op jit(solution)/shard_map/pallas_call | solution.py:256
  25.8 2.1 %collective-permute-start.8 = (bf16[16,4608]{1,0:T(8,128)(2,1)S(1)}, bf16[16,4608]{1,0:T(8,128)(2,1)S(1)}, u32[]{:S(2)}, u32[]{:S(2)}) collective-permute-start(bf16[16,4608]{1,0:T(8,128)(2,1)S(1)} %collective-permute-done.2), channel_id=1, source_target_pairs={{0,2},{1,3},{2,0},{3,1},{4,6},{5,7},{6,4},{7,5},{8,10},{9,11},{10,... | collective-permute-start | bytes 442376 | tf_op jit(solution)/shard_map/ppermute | solution.py:171
  27.9 0.6 %collective-permute-start.13 = (bf16[32,4608]{1,0:T(8,128)(2,1)S(1)}, bf16[32,4608]{1,0:T(8,128)(2,1)S(1)}, u32[]{:S(2)}, u32[]{:S(2)}) collective-permute-start(bf16[32,4608]{1,0:T(8,128)(2,1)S(1)} %pad_maximum_fusion.1), channel_id=1, source_target_pairs={{0,16},{16,0},{1,17},{17,1},{2,18},{18,2},{3,19},{19,3},{4,20},{20... | collective-permute-start | bytes 884744 | tf_op jit(solution)/shard_map/ppermute | solution.py:174
  28.5 2.4 %shard_map.57.norm_ref = f32[1,128]{1,0:T(1,128)S(1)} custom-call(f32[8,128]{1,0:T(8,128)S(1)} %copy-done.3, f32[128,128]{1,0:T(8,128)S(1)} %shard_map.56.head_ref, bf16[128,8192]{1,0:T(8,128)(2,1)S(1)} %copy-done.1, bf16[128,28672]{1,0:T(8,128)(2,1)S(1)} %copy-done), custom_call_target="tpu_custom_call" | custom-call | flops 1 | bytes 1 | tf_op jit(solution)/shard_map/pallas_call | solution.py:266
  30.9 1.5 %collective-permute-done.8 = bf16[16,4608]{1,0:T(8,128)(2,1)S(1)} collective-permute-done((bf16[16,4608]{1,0:T(8,128)(2,1)S(1)}, bf16[16,4608]{1,0:T(8,128)(2,1)S(1)}, u32[]{:S(2)}, u32[]{:S(2)}) %collective-permute-start.8) | collective-permute-done | bytes 147488 | tf_op jit(solution)/shard_map/ppermute | solution.py:171
  32.5 0.6 %collective-permute-start.9 = (bf16[16,4608]{1,0:T(8,128)(2,1)S(1)}, bf16[16,4608]{1,0:T(8,128)(2,1)S(1)}, u32[]{:S(2)}, u32[]{:S(2)}) collective-permute-start(bf16[16,4608]{1,0:T(8,128)(2,1)S(1)} %collective-permute-done.8), channel_id=1, source_target_pairs={{0,16},{16,0},{1,17},{17,1},{2,18},{18,2},{3,19},{19,3},{4,20},{20... | collective-permute-start | bytes 442376 | tf_op jit(solution)/shard_map/ppermute | solution.py:174
  33.1 4.7 %collective-permute-done.13 = bf16[32,4608]{1,0:T(8,128)(2,1)S(1)} collective-permute-done((bf16[32,4608]{1,0:T(8,128)(2,1)S(1)}, bf16[32,4608]{1,0:T(8,128)(2,1)S(1)}, u32[]{:S(2)}, u32[]{:S(2)}) %collective-permute-start.13) | collective-permute-done | bytes 294944 | tf_op jit(solution)/shard_map/ppermute | solution.py:174
  37.9 1.9 %shard_map.58.held_ref = f32[2,128,64]{2,1,0:T(8,128)S(1)} custom-call(bf16[128,8192]{1,0:T(8,128)(2,1)S(1)} %copy-done.1, bf16[128,28672]{1,0:T(8,128)(2,1)S(1)} %bitcast.1, bf16[32,4608]{1,0:T(8,128)(2,1)S(1)} %copy-done.2, bf16[32,4608]{1,0:T(8,128)(2,1)S(1)} %collective-permute-done.1.refs_1_, ...), custom_call_target="tpu_custom_call" | custom-call | flops 1 | bytes 1 | tf_op jit(solution)/shard_map/pallas_call | solution.py:278
  39.8 0.5 %collective-permute-done.9 = bf16[16,4608]{1,0:T(8,128)(2,1)S(1)} collective-permute-done((bf16[16,4608]{1,0:T(8,128)(2,1)S(1)}, bf16[16,4608]{1,0:T(8,128)(2,1)S(1)}, u32[]{:S(2)}, u32[]{:S(2)}) %collective-permute-start.9) | collective-permute-done | bytes 147488 | tf_op jit(solution)/shard_map/ppermute | solution.py:174
  40.3 1.8 %collective-permute-done.14.refs_7_ = bf16[48,4608]{1,0:T(8,128)(2,1)S(1)} collective-permute-done((bf16[48,4608]{1,0:T(8,128)(2,1)S(1)}, bf16[48,4608]{1,0:T(8,128)(2,1)S(1)}, u32[]{:S(2)}, u32[]{:S(2)}) %collective-permute-start.14) | collective-permute-done | bytes 442400 | tf_op jit(solution)/shard_map/ppermute | solution.py:171
  42.1 2.8 %shard_map.59 = f32[2,4]{1,0:T(2,128)} custom-call(f32[1,128]{1,0:T(1,128)S(1)} %shard_map.57.norm_ref, f32[8,128]{1,0:T(8,128)S(1)} %copy-done.3, f32[2,128,64]{2,1,0:T(8,128)S(1)} %shard_map.58.held_ref, bf16[128,8192]{1,0:T(8,128)(2,1)S(1)} %copy-done.1, bf16[128,28672]{1,0:T(8,128)(2,1)S(1)} %bitcast.1, bf16[32,4608]{1,0:T(8,128)(2,1)S(1)} %copy-done.2, ...), custom_call_target="tpu_custom_call" | custom-call | flops 1 | bytes 1 | tf_op jit(solution)/shard_map/pallas_call | solution.py:297
  (37 shorter events, 0.5 us)
Async XLA Ops:
  0.0 28.5 %copy-start.1 = (bf16[128,8192]{1,0:T(8,128)(2,1)S(1)}, bf16[128,8192]{1,0:T(8,128)(2,1)}, u32[]{:S(2)}) copy-start(bf16[128,8192]{1,0:T(8,128)(2,1)} %out_ref.5) | copy-start | bytes 6291460
  2.0 7.8 %collective-permute-start.1 = (bf16[32,4608]{1,0:T(8,128)(2,1)}, bf16[32,4608]{1,0:T(8,128)(2,1)S(1)}, u32[]{:S(2)}, u32[]{:S(2)}) collective-permute-start(bf16[32,4608]{1,0:T(8,128)(2,1)} %get-tuple-element.25.refs_0_), channel_id=1, source_target_pairs={{0,1},{1,0},{2,3},{3,2},{4,5},{5,4},{6,7},{7,6},{8,9},{9,8},{10,11... | collective-permute-start | bytes 884744 | tf_op jit(solution)/shard_map/ppermute | solution.py:171
  2.5 7.3 %collective-permute-start = (bf16[16,4608]{1,0:T(8,128)(2,1)}, bf16[16,4608]{1,0:T(8,128)(2,1)S(1)}, u32[]{:S(2)}, u32[]{:S(2)}) collective-permute-start(bf16[16,4608]{1,0:T(8,128)(2,1)} %get-tuple-element.26), channel_id=1, source_target_pairs={{0,4},{1,5},{2,6},{3,7},{4,0},{5,1},{6,2},{7,3},{8,12},{9,13},{10,... | collective-permute-start | bytes 442376 | tf_op jit(solution)/shard_map/ppermute | solution.py:171
  5.2 13.1 %collective-permute-start.6 = (bf16[32,4608]{1,0:T(8,128)(2,1)}, bf16[32,4608]{1,0:T(8,128)(2,1)S(1)}, u32[]{:S(2)}, u32[]{:S(2)}) collective-permute-start(bf16[32,4608]{1,0:T(8,128)(2,1)} %get-tuple-element.25.refs_0_), channel_id=1, source_target_pairs={{0,2},{1,3},{2,0},{3,1},{4,6},{5,7},{6,4},{7,5},{8,10},{9,11},{10,... | collective-permute-start | bytes 884744 | tf_op jit(solution)/shard_map/ppermute | solution.py:171
  6.7 11.6 %collective-permute-start.3 = (bf16[16,4608]{1,0:T(8,128)(2,1)}, bf16[16,4608]{1,0:T(8,128)(2,1)S(1)}, u32[]{:S(2)}, u32[]{:S(2)}) collective-permute-start(bf16[16,4608]{1,0:T(8,128)(2,1)} %get-tuple-element.26), channel_id=1, source_target_pairs={{0,8},{1,9},{2,10},{3,11},{4,12},{5,13},{6,14},{7,15},{8,0},{9,1},... | collective-permute-start | bytes 442376 | tf_op jit(solution)/shard_map/ppermute | solution.py:171
  9.8 8.5 %collective-permute-start.5 = (bf16[16,4608]{1,0:T(8,128)(2,1)S(1)}, bf16[16,4608]{1,0:T(8,128)(2,1)S(1)}, u32[]{:S(2)}, u32[]{:S(2)}) collective-permute-start(bf16[16,4608]{1,0:T(8,128)(2,1)S(1)} %collective-permute-done), channel_id=1, source_target_pairs={{0,2},{1,3},{2,0},{3,1},{4,6},{5,7},{6,4},{7,5},{8,10},{9,11},{10,... | collective-permute-start | bytes 442376 | tf_op jit(solution)/shard_map/ppermute | solution.py:171
  14.3 5.1 %collective-permute-start.4 = (bf16[16,4608]{1,0:T(8,128)(2,1)S(1)}, bf16[16,4608]{1,0:T(8,128)(2,1)S(1)}, u32[]{:S(2)}, u32[]{:S(2)}) collective-permute-start(bf16[16,4608]{1,0:T(8,128)(2,1)S(1)} %collective-permute-done), channel_id=1, source_target_pairs={{0,16},{16,0},{1,17},{17,1},{2,18},{18,2},{3,19},{19,3},{4,20},{20... | collective-permute-start | bytes 442376 | tf_op jit(solution)/shard_map/ppermute | solution.py:174
  15.8 9.9 %collective-permute-start.2 = (bf16[16,4608]{1,0:T(8,128)(2,1)}, bf16[16,4608]{1,0:T(8,128)(2,1)S(1)}, u32[]{:S(2)}, u32[]{:S(2)}) collective-permute-start(bf16[16,4608]{1,0:T(8,128)(2,1)} %get-tuple-element.26), channel_id=1, source_target_pairs={{0,12},{1,13},{2,14},{3,15},{4,8},{5,9},{6,10},{7,11},{8,4},{9,5},... | collective-permute-start | bytes 442376 | tf_op jit(solution)/shard_map/ppermute | solution.py:171
  19.5 6.3 %collective-permute-start.7 = (bf16[16,4608]{1,0:T(8,128)(2,1)S(1)}, bf16[16,4608]{1,0:T(8,128)(2,1)S(1)}, u32[]{:S(2)}, u32[]{:S(2)}) collective-permute-start(bf16[16,4608]{1,0:T(8,128)(2,1)S(1)} %collective-permute-done.3), channel_id=1, source_target_pairs={{0,2},{1,3},{2,0},{3,1},{4,6},{5,7},{6,4},{7,5},{8,10},{9,11},{10,... | collective-permute-start | bytes 442376 | tf_op jit(solution)/shard_map/ppermute | solution.py:171
  19.5 12.9 %collective-permute-start.11 = (bf16[32,4608]{1,0:T(8,128)(2,1)S(1)}, bf16[32,4608]{1,0:T(8,128)(2,1)S(1)}, u32[]{:S(2)}, u32[]{:S(2)}) collective-permute-start(bf16[32,4608]{1,0:T(8,128)(2,1)S(1)} %pad_maximum_fusion), channel_id=1, source_target_pairs={{0,16},{16,0},{1,17},{17,1},{2,18},{18,2},{3,19},{19,3},{4,20},{20... | collective-permute-start | bytes 884744 | tf_op jit(solution)/shard_map/ppermute | solution.py:174
  21.2 16.6 %collective-permute-start.10 = (bf16[96,4608]{1,0:T(8,128)(2,1)S(1)}, bf16[96,4608]{1,0:T(8,128)(2,1)S(1)}, u32[]{:S(2)}, u32[]{:S(2)}) collective-permute-start(bf16[96,4608]{1,0:T(8,128)(2,1)S(1)} %constant_dynamic-update-slice_fusion.refs_2_), channel_id=1, source_target_pairs={{0,1},{1,0},{2,3},{3,2},{4,5},{5,4},{6,7},{7,6},{8,9},{9,8},{10,11... | collective-permute-start | bytes 2654216 | tf_op jit(solution)/shard_map/ppermute | solution.py:171
  21.3 3.1 %copy-start = (bf16[128,28672]{1,0:T(8,128)(2,1)S(1)}, bf16[128,28672]{1,0:T(8,128)(2,1)}, u32[]{:S(2)}) copy-start(bf16[128,28672]{1,0:T(8,128)(2,1)} %in_ref.7) | copy-start | bytes 22020100
  24.3 0.7 %copy-start.3 = (f32[8,128]{1,0:T(8,128)S(1)}, f32[8,128]{1,0:T(8,128)}, u32[]{:S(2)}) copy-start(f32[8,128]{1,0:T(8,128)} %get-tuple-element.32.member_ref) | copy-start | bytes 12292
  25.0 12.8 %slice-start = ((s8[7340032]{0:T(1024)(128)(4,1)}), s8[4194304]{0:T(1024)(128)(4,1)S(1)}, s32[]{:S(2)}) async-start(s8[7340032]{0:T(1024)(128)(4,1)} %bitcast), calls=%async_computation | async-start | bytes 8388608
  25.7 12.1 %copy-start.2 = (bf16[32,4608]{1,0:T(8,128)(2,1)S(1)}, bf16[32,4608]{1,0:T(8,128)(2,1)}, u32[]{:S(2)}) copy-start(bf16[32,4608]{1,0:T(8,128)(2,1)} %get-tuple-element.25.refs_0_) | copy-start | bytes 884740
  25.8 6.6 %collective-permute-start.8 = (bf16[16,4608]{1,0:T(8,128)(2,1)S(1)}, bf16[16,4608]{1,0:T(8,128)(2,1)S(1)}, u32[]{:S(2)}, u32[]{:S(2)}) collective-permute-start(bf16[16,4608]{1,0:T(8,128)(2,1)S(1)} %collective-permute-done.2), channel_id=1, source_target_pairs={{0,2},{1,3},{2,0},{3,1},{4,6},{5,7},{6,4},{7,5},{8,10},{9,11},{10,... | collective-permute-start | bytes 442376 | tf_op jit(solution)/shard_map/ppermute | solution.py:171
  27.9 9.9 %collective-permute-start.13 = (bf16[32,4608]{1,0:T(8,128)(2,1)S(1)}, bf16[32,4608]{1,0:T(8,128)(2,1)S(1)}, u32[]{:S(2)}, u32[]{:S(2)}) collective-permute-start(bf16[32,4608]{1,0:T(8,128)(2,1)S(1)} %pad_maximum_fusion.1), channel_id=1, source_target_pairs={{0,16},{16,0},{1,17},{17,1},{2,18},{18,2},{3,19},{19,3},{4,20},{20... | collective-permute-start | bytes 884744 | tf_op jit(solution)/shard_map/ppermute | solution.py:174
  28.5 9.3 %slice-start.1 = ((s8[7340032]{0:T(1024)(128)(4,1)}), s8[3145728]{0:T(1024)(128)(4,1)S(1)}, s32[]{:S(2)}) async-start(s8[7340032]{0:T(1024)(128)(4,1)} %bitcast), calls=%async_computation.1 | async-start | bytes 6291456
  32.4 5.4 %collective-permute-start.12 = (bf16[80,4608]{1,0:T(8,128)(2,1)S(1)}, bf16[80,4608]{1,0:T(8,128)(2,1)S(1)}, u32[]{:S(2)}, u32[]{:S(2)}) collective-permute-start(bf16[80,4608]{1,0:T(8,128)(2,1)S(1)} %constant_dynamic-update-slice_fusion.5.refs_4_), channel_id=1, source_target_pairs={{0,1},{1,0},{2,3},{3,2},{4,5},{5,4},{6,7},{7,6},{8,9},{9,8},{10,11... | collective-permute-start | bytes 2211848 | tf_op jit(solution)/shard_map/ppermute | solution.py:171
  32.5 7.8 %collective-permute-start.9 = (bf16[16,4608]{1,0:T(8,128)(2,1)S(1)}, bf16[16,4608]{1,0:T(8,128)(2,1)S(1)}, u32[]{:S(2)}, u32[]{:S(2)}) collective-permute-start(bf16[16,4608]{1,0:T(8,128)(2,1)S(1)} %collective-permute-done.8), channel_id=1, source_target_pairs={{0,16},{16,0},{1,17},{17,1},{2,18},{18,2},{3,19},{19,3},{4,20},{20... | collective-permute-start | bytes 442376 | tf_op jit(solution)/shard_map/ppermute | solution.py:174
  40.3 1.9 %collective-permute-start.14 = (bf16[48,4608]{1,0:T(8,128)(2,1)S(1)}, bf16[48,4608]{1,0:T(8,128)(2,1)S(1)}, u32[]{:S(2)}, u32[]{:S(2)}) collective-permute-start(bf16[48,4608]{1,0:T(8,128)(2,1)S(1)} %constant_dynamic-update-slice_fusion.9.refs_6_), channel_id=1, source_target_pairs={{0,1},{1,0},{2,3},{3,2},{4,5},{5,4},{6,7},{7,6},{8,9},{9,8},{10,11... | collective-permute-start | bytes 1327112 | tf_op jit(solution)/shard_map/ppermute | solution.py:171

commit v6 on v5

--- a/solution.py
+++ b/solution.py
@@ -12,7 +12,6 @@
 PACK = 16
 HEAD = 8192
 SCORE_VMEM = 24 * 1024 * 1024
-PACK_VMEM = 58 * 1024 * 1024
 
 NT = (((1,), (1,)), ((), ()))
 
@@ -29,25 +28,7 @@
     return lax.axis_index("seq") % chunks if paired else 0
 
 
-def pack_kernel(chunks, paired, seq_dev, u_hbm, v_hbm, lengths_hbm, member_ref, both_ref, *refs):
-    *own_refs, u_ref, v_ref, lengths_ref, sems = refs
-    pairs = ((v_hbm, v_ref), (u_hbm, u_ref), (lengths_hbm, lengths_ref))
-    copies = [pltpu.make_async_copy(hbm, ref, sems.at[i]) for i, (hbm, ref) in enumerate(pairs)]
-    for copy in copies:
-        copy.start()
-    for copy in copies:
-        copy.wait()
-    seqs, tok_cap = member_ref.shape
-    which = lax.broadcasted_iota(jnp.int32, (seqs, tok_cap), 0)
-    position = lax.broadcasted_iota(jnp.int32, (seqs, tok_cap), 1)
-    member = jnp.zeros((seqs, tok_cap), jnp.float32)
-    low = 0
-    for k in range(seq_dev):
-        high = low + lengths_ref[lax.axis_index("seq") * seq_dev + k]
-        inside = (which == k) & (position >= low) & (position < high)
-        member = jnp.where(inside, 1.0, member)
-        low = high
-    member_ref[...] = member
+def pack_kernel(chunks, paired, u_ref, v_ref, both_ref, *own_refs):
     rank_rows = u_ref.shape[0]
     turned = lax.axis_index("seq") % chunks
     wide_u, wide_v = u_ref.shape[1] // (2 * chunks), v_ref.shape[1] // (2 * chunks)
@@ -67,9 +48,23 @@
             place += wide
 
 
-def head_kernel(member_ref, in_ref, gram_ref):
+def head_kernel(seq_dev, lengths_hbm, in_ref, gram_ref, member_ref, lengths_ref, sem):
+    copy = pltpu.make_async_copy(lengths_hbm, lengths_ref, sem)
+    copy.start()
     head = in_ref[:, :HEAD]
     gram_ref[...] = inner_rows(head, head)
+    copy.wait()
+    seqs, tok_cap = member_ref.shape
+    which = lax.broadcasted_iota(jnp.int32, (seqs, tok_cap), 0)
+    position = lax.broadcasted_iota(jnp.int32, (seqs, tok_cap), 1)
+    member = jnp.zeros((seqs, tok_cap), jnp.float32)
+    low = 0
+    for k in range(seq_dev):
+        high = low + lengths_ref[lax.axis_index("seq") * seq_dev + k]
+        inside = (which == k) & (position >= low) & (position < high)
+        member = jnp.where(inside, 1.0, member)
+        low = high
+    member_ref[...] = member
 
 
 def norm_kernel(member_ref, head_ref, out_ref, in_ref, norm_ref):
@@ -166,7 +161,7 @@
         score_ref[q : q + 1, :] = row[:, : score_ref.shape[1]]
 
 
-def gather_blocks(both, own, devices, member, head_step, norm_step, partial_step):
+def gather_blocks(both, own, devices, lengths, head_step, norm_step, partial_step):
     def swap(value, mask):
         return lax.ppermute(value, "seq", [(i, i ^ mask) for i in range(devices)])
 
@@ -178,9 +173,9 @@
     z1, z2, y0, both_core = swap(own, 4), swap(own, 8), swap(both, 2), swap(both, 1)
     z1, both_core, own = gate(z1, both_core, own)
     x1, y1, z3 = across(z1), swap(z1, 2), swap(own, 12)
-    z2, x1, y1, y0, member = gate(z2, x1, y1, y0, member)
+    z2, y1, y0, lengths = gate(z2, y1, y0, lengths)
     x_near, y2 = across(stack(z2, y1)), swap(z2, 2)
-    head = head_step(member)
+    head, member = head_step(lengths)
     z3, y2, head, member = gate(z3, y2, head, member)
     x_far, y3 = across(stack(z3, y2)), swap(z3, 2)
     early = stack(y0, z1, y1, z2, x1)
@@ -203,7 +198,7 @@
     x_last, partial = gate(x_last, partial)
     late = stack(x_far, x_last)
     place(late, swap(late, 1), ((other, 12), (other, 10), (other, 14)))
-    return [other[b] for b in range(devices)], norms, partial
+    return [other[b] for b in range(devices)], norms, member, partial
 
 
 def refs_of(blocks):
@@ -232,35 +227,30 @@
     score_params = pltpu.CompilerParams(vmem_limit_bytes=SCORE_VMEM)
     half_width = width // (2 * chunks)
     seqs = -(-seq_dev // 8) * 8
-    member, *packed = pl.pallas_call(
-        functools.partial(pack_kernel, chunks, paired, seq_dev),
-        out_shape=[
-            jax.ShapeDtypeStruct((seqs, tok_cap), jnp.float32),
-            jax.ShapeDtypeStruct((2 * PACK, half_width), factor_u.dtype),
-        ]
+    packed = pl.pallas_call(
+        functools.partial(pack_kernel, chunks, paired),
+        out_shape=[jax.ShapeDtypeStruct((2 * PACK, half_width), factor_u.dtype)]
         + [jax.ShapeDtypeStruct((PACK, half_width), factor_u.dtype)] * paired,
-        in_specs=[hbm] * 3,
-        out_specs=[vmem] * (2 + paired),
-        scratch_shapes=[
-            pltpu.VMEM(factor_u.shape, factor_u.dtype),
-            pltpu.VMEM(factor_v.shape, factor_v.dtype),
-            pltpu.SMEM(seq_lengths.shape, seq_lengths.dtype),
-            pltpu.SemaphoreType.DMA((3,)),
-        ],
-        compiler_params=pltpu.CompilerParams(vmem_limit_bytes=PACK_VMEM),
-    )(factor_u, factor_v, seq_lengths)
+        in_specs=[vmem] * 2,
+        out_specs=[vmem] * (1 + paired),
+        compiler_params=score_params,
+    )(factor_u, factor_v)
 
     tiny = pl.CostEstimate(flops=1, bytes_accessed=1, transcendentals=0)
 
-    def head_step(member):
+    def head_step(lengths):
         return pl.pallas_call(
-            head_kernel,
-            out_shape=jax.ShapeDtypeStruct((tok_cap, tok_cap), jnp.float32),
-            in_specs=[vmem] * 2,
-            out_specs=vmem,
+            functools.partial(head_kernel, seq_dev),
+            out_shape=[
+                jax.ShapeDtypeStruct((tok_cap, tok_cap), jnp.float32),
+                jax.ShapeDtypeStruct((seqs, tok_cap), jnp.float32),
+            ],
+            in_specs=[hbm, vmem],
+            out_specs=[vmem] * 2,
+            scratch_shapes=[pltpu.SMEM(lengths.shape, lengths.dtype), pltpu.SemaphoreType.DMA],
             compiler_params=score_params,
             cost_estimate=tiny,
-        )(member, layer_inputs)
+        )(lengths, layer_inputs)
 
     def norm_step(member, head):
         return pl.pallas_call(
@@ -285,11 +275,12 @@
         )(out_grads, layer_inputs, *arrays)
 
     if paired:
-        other, norms, partial = gather_blocks(
-            packed[0], packed[1], devices, member, head_step, norm_step, partial_step
+        other, norms, member, partial = gather_blocks(
+            packed[0], packed[1], devices, seq_lengths, head_step, norm_step, partial_step
         )
     else:
-        norms = norm_step(member, head_step(member))
+        head, member = head_step(seq_lengths)
+        norms = norm_step(member, head)
         gathered = lax.all_gather(packed[0], "seq", axis=0, tiled=True)
         partial = partial_step([(gathered, 2 * PACK * b) for b in range(devices)])
         other = [(gathered, 2 * PACK * b + PACK) for b in range(devices)]

time: 45.1 us -> 43.2 us (0.958)
  waiting for transfers between devices: 10.1 us -> 7.64 us
  local copies, waits for them, and re-layouts: 3.93 us -> 6.33 us
  Pallas kernels: 9.79 us -> 7.85 us
    unnamed x20, local copies, waits for them, and re-layouts: 3.88 us -> 6.28 us
    ppermute x4, waiting for transfers between devices: 6.33 us -> 4.19 us  [across(): return lax.ppermute(value, 'grp', [(0, 1), (1, 0)])]
    pallas_call x2, Pallas kernels: 2.69 us -> 0.81 us  [the longest x1 0.74 us: head_step(): pl.pallas_call(functools.partial(head_kernel, seq_dev), out_shape=[jax.Sh...]
    ppermute x4, starting transfers between devices: 4.25 us -> 4.94 us  [across(): return lax.ppermute(value, 'grp', [(0, 1), (1, 0)])]
    ppermute x11, starting transfers between devices: 16.6 us -> 15.9 us  [swap(): return lax.ppermute(value, 'seq', [(i, i ^ mask) for i in range(devices)])]
  transfers between devices with their start and end apart: 15 -> 15, of which waited for: 6 -> 5; matrix products, arithmetic and copies ran while one was open for 0% -> 0% of each run, Pallas kernels for 11% -> 12%
where the time goes in v6:
time: 43.2 us; the launch traced here: 42.9 us
  starting transfers between devices  20.9 us (48%)
  Pallas kernels  7.85 us (18%)
  waiting for transfers between devices  7.64 us (18%)
  local copies, waits for them, and re-layouts  6.33 us (15%)
    ppermute x11, starting transfers between devices, swap(): return lax.ppermute(value, 'seq', [(i, i ^ mask) for i in range(devices)])  15.9 us
    unnamed x20, local copies, waits for them, and re-layouts  6.28 us
    ppermute x4, starting transfers between devices, across(): return lax.ppermute(value, 'grp', [(0, 1), (1, 0)])  4.94 us
    ppermute x4, waiting for transfers between devices, across(): return lax.ppermute(value, 'grp', [(0, 1), (1, 0)])  4.19 us
    ppermute x11, waiting for transfers between devices, swap(): return lax.ppermute(value, 'seq', [(i, i ^ mask) for i in range(devices)])  3.45 us
    pallas_call x1, Pallas kernels, local(): pl.pallas_call(functools.partial(score_kernel, rank_rows, paired, places)...  2.8 us
    pallas_call x1, Pallas kernels, norm_step(): pl.pallas_call(norm_kernel, out_shape=jax.ShapeDtypeStruct((1, tok_cap),...  2.36 us
    pallas_call x1, Pallas kernels, partial_step(): pl.pallas_call(functools.partial(partial_kernel, rank_rows, paired, place...  1.88 us
  transfers between devices with their start and end apart: 15, of which 5 were waited for; matrix products, arithmetic and copies ran while one was open for 0% of the time, Pallas kernels for 12%

profile of v6, /device:TPU:0, one launch (start us, length us, event | category | flops | bytes accessed | tf_op | source)
XLA Modules:
  0.0 42.9 jit_solution(85628004127628501)
XLA Ops:
  0.0 0.9 %copy-done.3 = bf16[4,28672]{1,0:T(4,128)(2,1)S(1)} copy-done((bf16[4,28672]{1,0:T(4,128)(2,1)S(1)}, bf16[4,28672]{1,0:T(4,128)(2,1)}, u32[]{:S(2)}) %copy-start.3) | copy-done | bytes 229400
  0.9 0.8 %copy-done.4 = bf16[4,8192]{1,0:T(4,128)(2,1)S(1)} copy-done((bf16[4,8192]{1,0:T(4,128)(2,1)S(1)}, bf16[4,8192]{1,0:T(4,128)(2,1)}, u32[]{:S(2)}) %copy-start.4) | copy-done | bytes 65560
  1.9 0.5 %collective-permute-start.1 = (bf16[32,4608]{1,0:T(8,128)(2,1)S(1)}, bf16[32,4608]{1,0:T(8,128)(2,1)S(1)}, u32[]{:S(2)}, u32[]{:S(2)}) collective-permute-start(bf16[32,4608]{1,0:T(8,128)(2,1)S(1)} %get-tuple-element.25.refs_0_), channel_id=1, source_target_pairs={{0,1},{1,0},{2,3},{3,2},{4,5},{5,4},{6,7},{7,6},{8,9},{9,8},{10,11... | collective-permute-start | bytes 884744 | tf_op jit(solution)/shard_map/ppermute | solution.py:166
  2.4 2.6 %collective-permute-start = (bf16[16,4608]{1,0:T(8,128)(2,1)S(1)}, bf16[16,4608]{1,0:T(8,128)(2,1)S(1)}, u32[]{:S(2)}, u32[]{:S(2)}) collective-permute-start(bf16[16,4608]{1,0:T(8,128)(2,1)S(1)} %get-tuple-element.26), channel_id=1, source_target_pairs={{0,4},{1,5},{2,6},{3,7},{4,0},{5,1},{6,2},{7,3},{8,12},{9,13},{10,... | collective-permute-start | bytes 442376 | tf_op jit(solution)/shard_map/ppermute | solution.py:166
  5.0 1.5 %collective-permute-start.5 = (bf16[32,4608]{1,0:T(8,128)(2,1)S(1)}, bf16[32,4608]{1,0:T(8,128)(2,1)S(1)}, u32[]{:S(2)}, u32[]{:S(2)}) collective-permute-start(bf16[32,4608]{1,0:T(8,128)(2,1)S(1)} %get-tuple-element.25.refs_0_), channel_id=1, source_target_pairs={{0,2},{1,3},{2,0},{3,1},{4,6},{5,7},{6,4},{7,5},{8,10},{9,11},{10,... | collective-permute-start | bytes 884744 | tf_op jit(solution)/shard_map/ppermute | solution.py:166
  6.5 2.6 %collective-permute-start.3 = (bf16[16,4608]{1,0:T(8,128)(2,1)S(1)}, bf16[16,4608]{1,0:T(8,128)(2,1)S(1)}, u32[]{:S(2)}, u32[]{:S(2)}) collective-permute-start(bf16[16,4608]{1,0:T(8,128)(2,1)S(1)} %get-tuple-element.26), channel_id=1, source_target_pairs={{0,8},{1,9},{2,10},{3,11},{4,12},{5,13},{6,14},{7,15},{8,0},{9,1},... | collective-permute-start | bytes 442376 | tf_op jit(solution)/shard_map/ppermute | solution.py:166
  9.5 4.5 %collective-permute-start.4 = (bf16[16,4608]{1,0:T(8,128)(2,1)S(1)}, bf16[16,4608]{1,0:T(8,128)(2,1)S(1)}, u32[]{:S(2)}, u32[]{:S(2)}) collective-permute-start(bf16[16,4608]{1,0:T(8,128)(2,1)S(1)} %collective-permute-done), channel_id=1, source_target_pairs={{0,2},{1,3},{2,0},{3,1},{4,6},{5,7},{6,4},{7,5},{8,10},{9,11},{10,... | collective-permute-start | bytes 442376 | tf_op jit(solution)/shard_map/ppermute | solution.py:166
  14.0 1.5 %collective-permute-start.9 = (bf16[16,4608]{1,0:T(8,128)(2,1)S(1)}, bf16[16,4608]{1,0:T(8,128)(2,1)S(1)}, u32[]{:S(2)}, u32[]{:S(2)}) collective-permute-start(bf16[16,4608]{1,0:T(8,128)(2,1)S(1)} %collective-permute-done), channel_id=1, source_target_pairs={{0,16},{16,0},{1,17},{17,1},{2,18},{18,2},{3,19},{19,3},{4,20},{20... | collective-permute-start | bytes 442376 | tf_op jit(solution)/shard_map/ppermute | solution.py:169
  15.5 2.5 %collective-permute-start.2 = (bf16[16,4608]{1,0:T(8,128)(2,1)S(1)}, bf16[16,4608]{1,0:T(8,128)(2,1)S(1)}, u32[]{:S(2)}, u32[]{:S(2)}) collective-permute-start(bf16[16,4608]{1,0:T(8,128)(2,1)S(1)} %get-tuple-element.26), channel_id=1, source_target_pairs={{0,12},{1,13},{2,14},{3,15},{4,8},{5,9},{6,10},{7,11},{8,4},{9,5},... | collective-permute-start | bytes 442376 | tf_op jit(solution)/shard_map/ppermute | solution.py:166
  18.0 1.2 %collective-permute-start.6 = (bf16[16,4608]{1,0:T(8,128)(2,1)S(1)}, bf16[16,4608]{1,0:T(8,128)(2,1)S(1)}, u32[]{:S(2)}, u32[]{:S(2)}) collective-permute-start(bf16[16,4608]{1,0:T(8,128)(2,1)S(1)} %collective-permute-done.3), channel_id=1, source_target_pairs={{0,2},{1,3},{2,0},{3,1},{4,6},{5,7},{6,4},{7,5},{8,10},{9,11},{10,... | collective-permute-start | bytes 442376 | tf_op jit(solution)/shard_map/ppermute | solution.py:166
  19.4 1.6 %collective-permute-start.11 = (bf16[32,4608]{1,0:T(8,128)(2,1)S(1)}, bf16[32,4608]{1,0:T(8,128)(2,1)S(1)}, u32[]{:S(2)}, u32[]{:S(2)}) collective-permute-start(bf16[32,4608]{1,0:T(8,128)(2,1)S(1)} %pad_maximum_fusion), channel_id=1, source_target_pairs={{0,16},{16,0},{1,17},{17,1},{2,18},{18,2},{3,19},{19,3},{4,20},{20... | collective-permute-start | bytes 884744 | tf_op jit(solution)/shard_map/ppermute | solution.py:169
  20.9 3.1 %copy-done = bf16[128,28672]{1,0:T(8,128)(2,1)S(1)} copy-done((bf16[128,28672]{1,0:T(8,128)(2,1)S(1)}, bf16[128,28672]{1,0:T(8,128)(2,1)}, u32[]{:S(2)}) %copy-start) | copy-done | bytes 7340056
  24.0 0.7 %copy-done.5 = s32[64]{0:T(128)S(1)} copy-done((s32[64]{0:T(128)S(1)}, s32[64]{0:T(128)}, u32[]{:S(2)}) %copy-start.5) | copy-done | bytes 280
  24.7 0.7 %shard_map.56 = (f32[128,128]{1,0:T(8,128)S(1)}, f32[8,128]{1,0:T(8,128)S(1)}) custom-call(s32[64]{0:T(128)S(1)} %copy-done.5, bf16[128,28672]{1,0:T(8,128)(2,1)S(1)} %copy-done), custom_call_target="tpu_custom_call" | custom-call | flops 1 | bytes 1 | tf_op jit(solution)/shard_map/pallas_call | solution.py:242
  25.8 1.3 %collective-permute-start.13 = (bf16[32,4608]{1,0:T(8,128)(2,1)S(1)}, bf16[32,4608]{1,0:T(8,128)(2,1)S(1)}, u32[]{:S(2)}, u32[]{:S(2)}) collective-permute-start(bf16[32,4608]{1,0:T(8,128)(2,1)S(1)} %pad_maximum_fusion.1), channel_id=1, source_target_pairs={{0,16},{16,0},{1,17},{17,1},{2,18},{18,2},{3,19},{19,3},{4,20},{20... | collective-permute-start | bytes 884744 | tf_op jit(solution)/shard_map/ppermute | solution.py:169
  27.1 0.7 %copy-done.1 = bf16[128,28672]{1,0:T(8,128)(2,1)S(1)} copy-done((bf16[128,28672]{1,0:T(8,128)(2,1)S(1)}, bf16[128,28672]{1,0:T(8,128)(2,1)}, u32[]{:S(2)}) %copy-start.1) | copy-done | bytes 7340056
  27.7 2.4 %shard_map.57.norm_ref = f32[1,128]{1,0:T(1,128)S(1)} custom-call(f32[8,128]{1,0:T(8,128)S(1)} %get-tuple-element.33.member_ref, f32[128,128]{1,0:T(8,128)S(1)} %get-tuple-element.34.head_ref, bf16[128,8192]{1,0:T(8,128)(2,1)S(1)} %copy-done.2, bf16[128,28672]{1,0:T(8,128)(2,1)S(1)} %copy-done.1), custom_call_target="tpu_custom_call" | custom-call | flops 1 | bytes 1 | tf_op jit(solution)/shard_map/pallas_call | solution.py:256
  30.1 1.3 %collective-permute-done.7 = bf16[16,4608]{1,0:T(8,128)(2,1)S(1)} collective-permute-done((bf16[16,4608]{1,0:T(8,128)(2,1)S(1)}, bf16[16,4608]{1,0:T(8,128)(2,1)S(1)}, u32[]{:S(2)}, u32[]{:S(2)}) %collective-permute-start.7) | collective-permute-done | bytes 147488 | tf_op jit(solution)/shard_map/ppermute | solution.py:166
  31.5 0.6 %collective-permute-start.8 = (bf16[16,4608]{1,0:T(8,128)(2,1)S(1)}, bf16[16,4608]{1,0:T(8,128)(2,1)S(1)}, u32[]{:S(2)}, u32[]{:S(2)}) collective-permute-start(bf16[16,4608]{1,0:T(8,128)(2,1)S(1)} %collective-permute-done.7), channel_id=1, source_target_pairs={{0,16},{16,0},{1,17},{17,1},{2,18},{18,2},{3,19},{19,3},{4,20},{20... | collective-permute-start | bytes 442376 | tf_op jit(solution)/shard_map/ppermute | solution.py:169
  32.1 3.3 %collective-permute-done.13 = bf16[32,4608]{1,0:T(8,128)(2,1)S(1)} collective-permute-done((bf16[32,4608]{1,0:T(8,128)(2,1)S(1)}, bf16[32,4608]{1,0:T(8,128)(2,1)S(1)}, u32[]{:S(2)}, u32[]{:S(2)}) %collective-permute-start.13) | collective-permute-done | bytes 294944 | tf_op jit(solution)/shard_map/ppermute | solution.py:169
  35.5 1.9 %shard_map.58.held_ref = f32[2,128,64]{2,1,0:T(8,128)S(1)} custom-call(bf16[128,8192]{1,0:T(8,128)(2,1)S(1)} %copy-done.2, bf16[128,28672]{1,0:T(8,128)(2,1)S(1)} %copy-done.1, bf16[32,4608]{1,0:T(8,128)(2,1)S(1)} %get-tuple-element.25.refs_0_, bf16[32,4608]{1,0:T(8,128)(2,1)S(1)} %collective-permute-done.1.refs_1_, ...), custom_call_target="tpu_custom_call" | custom-call | flops 1 | bytes 1 | tf_op jit(solution)/shard_map/pallas_call | solution.py:268
  37.4 0.8 %collective-permute-done.8 = bf16[16,4608]{1,0:T(8,128)(2,1)S(1)} collective-permute-done((bf16[16,4608]{1,0:T(8,128)(2,1)S(1)}, bf16[16,4608]{1,0:T(8,128)(2,1)S(1)}, u32[]{:S(2)}, u32[]{:S(2)}) %collective-permute-start.8) | collective-permute-done | bytes 147488 | tf_op jit(solution)/shard_map/ppermute | solution.py:169
  38.4 1.8 %collective-permute-done.14.refs_7_ = bf16[48,4608]{1,0:T(8,128)(2,1)S(1)} collective-permute-done((bf16[48,4608]{1,0:T(8,128)(2,1)S(1)}, bf16[48,4608]{1,0:T(8,128)(2,1)S(1)}, u32[]{:S(2)}, u32[]{:S(2)}) %collective-permute-start.14) | collective-permute-done | bytes 442400 | tf_op jit(solution)/shard_map/ppermute | solution.py:166
  40.1 2.8 %shard_map.59 = f32[2,4]{1,0:T(2,128)} custom-call(f32[1,128]{1,0:T(1,128)S(1)} %shard_map.57.norm_ref, f32[8,128]{1,0:T(8,128)S(1)} %get-tuple-element.33.member_ref, f32[2,128,64]{2,1,0:T(8,128)S(1)} %shard_map.58.held_ref, bf16[128,8192]{1,0:T(8,128)(2,1)S(1)} %copy-done.2, bf16[128,28672]{1,0:T(8,128)(2,1)S(1)} %copy-done.1, ...), custom_call_target="tpu_custom_call" | custom-call | flops 1 | bytes 1 | tf_op jit(solution)/shard_map/pallas_call | solution.py:288
  (36 shorter events, 1.1 us)
Async XLA Ops:
  0.0 0.9 %copy-start.3 = (bf16[4,28672]{1,0:T(4,128)(2,1)S(1)}, bf16[4,28672]{1,0:T(4,128)(2,1)}, u32[]{:S(2)}) copy-start(bf16[4,28672]{1,0:T(4,128)(2,1)} %v_ref.1) | copy-start | bytes 688132
  0.9 0.8 %copy-start.4 = (bf16[4,8192]{1,0:T(4,128)(2,1)S(1)}, bf16[4,8192]{1,0:T(4,128)(2,1)}, u32[]{:S(2)}) copy-start(bf16[4,8192]{1,0:T(4,128)(2,1)} %u_ref.1) | copy-start | bytes 196612
  1.8 25.3 %copy-start.2 = (bf16[128,8192]{1,0:T(8,128)(2,1)S(1)}, bf16[128,8192]{1,0:T(8,128)(2,1)}, u32[]{:S(2)}) copy-start(bf16[128,8192]{1,0:T(8,128)(2,1)} %out_ref.5) | copy-start | bytes 6291460
  1.9 7.6 %collective-permute-start.1 = (bf16[32,4608]{1,0:T(8,128)(2,1)S(1)}, bf16[32,4608]{1,0:T(8,128)(2,1)S(1)}, u32[]{:S(2)}, u32[]{:S(2)}) collective-permute-start(bf16[32,4608]{1,0:T(8,128)(2,1)S(1)} %get-tuple-element.25.refs_0_), channel_id=1, source_target_pairs={{0,1},{1,0},{2,3},{3,2},{4,5},{5,4},{6,7},{7,6},{8,9},{9,8},{10,11... | collective-permute-start | bytes 884744 | tf_op jit(solution)/shard_map/ppermute | solution.py:166
  2.4 7.1 %collective-permute-start = (bf16[16,4608]{1,0:T(8,128)(2,1)S(1)}, bf16[16,4608]{1,0:T(8,128)(2,1)S(1)}, u32[]{:S(2)}, u32[]{:S(2)}) collective-permute-start(bf16[16,4608]{1,0:T(8,128)(2,1)S(1)} %get-tuple-element.26), channel_id=1, source_target_pairs={{0,4},{1,5},{2,6},{3,7},{4,0},{5,1},{6,2},{7,3},{8,12},{9,13},{10,... | collective-permute-start | bytes 442376 | tf_op jit(solution)/shard_map/ppermute | solution.py:166
  5.0 12.9 %collective-permute-start.5 = (bf16[32,4608]{1,0:T(8,128)(2,1)S(1)}, bf16[32,4608]{1,0:T(8,128)(2,1)S(1)}, u32[]{:S(2)}, u32[]{:S(2)}) collective-permute-start(bf16[32,4608]{1,0:T(8,128)(2,1)S(1)} %get-tuple-element.25.refs_0_), channel_id=1, source_target_pairs={{0,2},{1,3},{2,0},{3,1},{4,6},{5,7},{6,4},{7,5},{8,10},{9,11},{10,... | collective-permute-start | bytes 884744 | tf_op jit(solution)/shard_map/ppermute | solution.py:166
  6.5 11.4 %collective-permute-start.3 = (bf16[16,4608]{1,0:T(8,128)(2,1)S(1)}, bf16[16,4608]{1,0:T(8,128)(2,1)S(1)}, u32[]{:S(2)}, u32[]{:S(2)}) collective-permute-start(bf16[16,4608]{1,0:T(8,128)(2,1)S(1)} %get-tuple-element.26), channel_id=1, source_target_pairs={{0,8},{1,9},{2,10},{3,11},{4,12},{5,13},{6,14},{7,15},{8,0},{9,1},... | collective-permute-start | bytes 442376 | tf_op jit(solution)/shard_map/ppermute | solution.py:166
  9.5 8.5 %collective-permute-start.4 = (bf16[16,4608]{1,0:T(8,128)(2,1)S(1)}, bf16[16,4608]{1,0:T(8,128)(2,1)S(1)}, u32[]{:S(2)}, u32[]{:S(2)}) collective-permute-start(bf16[16,4608]{1,0:T(8,128)(2,1)S(1)} %collective-permute-done), channel_id=1, source_target_pairs={{0,2},{1,3},{2,0},{3,1},{4,6},{5,7},{6,4},{7,5},{8,10},{9,11},{10,... | collective-permute-start | bytes 442376 | tf_op jit(solution)/shard_map/ppermute | solution.py:166
  14.0 5.3 %collective-permute-start.9 = (bf16[16,4608]{1,0:T(8,128)(2,1)S(1)}, bf16[16,4608]{1,0:T(8,128)(2,1)S(1)}, u32[]{:S(2)}, u32[]{:S(2)}) collective-permute-start(bf16[16,4608]{1,0:T(8,128)(2,1)S(1)} %collective-permute-done), channel_id=1, source_target_pairs={{0,16},{16,0},{1,17},{17,1},{2,18},{18,2},{3,19},{19,3},{4,20},{20... | collective-permute-start | bytes 442376 | tf_op jit(solution)/shard_map/ppermute | solution.py:169
  15.5 9.9 %collective-permute-start.2 = (bf16[16,4608]{1,0:T(8,128)(2,1)S(1)}, bf16[16,4608]{1,0:T(8,128)(2,1)S(1)}, u32[]{:S(2)}, u32[]{:S(2)}) collective-permute-start(bf16[16,4608]{1,0:T(8,128)(2,1)S(1)} %get-tuple-element.26), channel_id=1, source_target_pairs={{0,12},{1,13},{2,14},{3,15},{4,8},{5,9},{6,10},{7,11},{8,4},{9,5},... | collective-permute-start | bytes 442376 | tf_op jit(solution)/shard_map/ppermute | solution.py:166
  18.0 7.5 %collective-permute-start.6 = (bf16[16,4608]{1,0:T(8,128)(2,1)S(1)}, bf16[16,4608]{1,0:T(8,128)(2,1)S(1)}, u32[]{:S(2)}, u32[]{:S(2)}) collective-permute-start(bf16[16,4608]{1,0:T(8,128)(2,1)S(1)} %collective-permute-done.3), channel_id=1, source_target_pairs={{0,2},{1,3},{2,0},{3,1},{4,6},{5,7},{6,4},{7,5},{8,10},{9,11},{10,... | collective-permute-start | bytes 442376 | tf_op jit(solution)/shard_map/ppermute | solution.py:166
  19.3 16.2 %collective-permute-start.10 = (bf16[96,4608]{1,0:T(8,128)(2,1)S(1)}, bf16[96,4608]{1,0:T(8,128)(2,1)S(1)}, u32[]{:S(2)}, u32[]{:S(2)}) collective-permute-start(bf16[96,4608]{1,0:T(8,128)(2,1)S(1)} %constant_dynamic-update-slice_fusion.refs_2_), channel_id=1, source_target_pairs={{0,1},{1,0},{2,3},{3,2},{4,5},{5,4},{6,7},{7,6},{8,9},{9,8},{10,11... | collective-permute-start | bytes 2654216 | tf_op jit(solution)/shard_map/ppermute | solution.py:166
  19.4 12.1 %collective-permute-start.11 = (bf16[32,4608]{1,0:T(8,128)(2,1)S(1)}, bf16[32,4608]{1,0:T(8,128)(2,1)S(1)}, u32[]{:S(2)}, u32[]{:S(2)}) collective-permute-start(bf16[32,4608]{1,0:T(8,128)(2,1)S(1)} %pad_maximum_fusion), channel_id=1, source_target_pairs={{0,16},{16,0},{1,17},{17,1},{2,18},{18,2},{3,19},{19,3},{4,20},{20... | collective-permute-start | bytes 884744 | tf_op jit(solution)/shard_map/ppermute | solution.py:169
  20.9 3.1 %copy-start = (bf16[128,28672]{1,0:T(8,128)(2,1)S(1)}, bf16[128,28672]{1,0:T(8,128)(2,1)}, u32[]{:S(2)}) copy-start(bf16[128,28672]{1,0:T(8,128)(2,1)} %in_ref.7) | copy-start | bytes 22020100
  24.0 0.7 %copy-start.5 = (s32[64]{0:T(128)S(1)}, s32[64]{0:T(128)}, u32[]{:S(2)}) copy-start(s32[64]{0:T(128)} %lengths_hbm) | copy-start | bytes 772
  24.7 3.1 %copy-start.1 = (bf16[128,28672]{1,0:T(8,128)(2,1)S(1)}, bf16[128,28672]{1,0:T(8,128)(2,1)}, u32[]{:S(2)}) copy-start(bf16[128,28672]{1,0:T(8,128)(2,1)} %in_ref.7) | copy-start | bytes 22020100
  25.4 6.0 %collective-permute-start.7 = (bf16[16,4608]{1,0:T(8,128)(2,1)S(1)}, bf16[16,4608]{1,0:T(8,128)(2,1)S(1)}, u32[]{:S(2)}, u32[]{:S(2)}) collective-permute-start(bf16[16,4608]{1,0:T(8,128)(2,1)S(1)} %collective-permute-done.2), channel_id=1, source_target_pairs={{0,2},{1,3},{2,0},{3,1},{4,6},{5,7},{6,4},{7,5},{8,10},{9,11},{10,... | collective-permute-start | bytes 442376 | tf_op jit(solution)/shard_map/ppermute | solution.py:166
  25.8 9.7 %collective-permute-start.13 = (bf16[32,4608]{1,0:T(8,128)(2,1)S(1)}, bf16[32,4608]{1,0:T(8,128)(2,1)S(1)}, u32[]{:S(2)}, u32[]{:S(2)}) collective-permute-start(bf16[32,4608]{1,0:T(8,128)(2,1)S(1)} %pad_maximum_fusion.1), channel_id=1, source_target_pairs={{0,16},{16,0},{1,17},{17,1},{2,18},{18,2},{3,19},{19,3},{4,20},{20... | collective-permute-start | bytes 884744 | tf_op jit(solution)/shard_map/ppermute | solution.py:169
  31.5 4.1 %collective-permute-start.12 = (bf16[80,4608]{1,0:T(8,128)(2,1)S(1)}, bf16[80,4608]{1,0:T(8,128)(2,1)S(1)}, u32[]{:S(2)}, u32[]{:S(2)}) collective-permute-start(bf16[80,4608]{1,0:T(8,128)(2,1)S(1)} %constant_dynamic-update-slice_fusion.5.refs_4_), channel_id=1, source_target_pairs={{0,1},{1,0},{2,3},{3,2},{4,5},{5,4},{6,7},{7,6},{8,9},{9,8},{10,11... | collective-permute-start | bytes 2211848 | tf_op jit(solution)/shard_map/ppermute | solution.py:166
  31.5 6.7 %collective-permute-start.8 = (bf16[16,4608]{1,0:T(8,128)(2,1)S(1)}, bf16[16,4608]{1,0:T(8,128)(2,1)S(1)}, u32[]{:S(2)}, u32[]{:S(2)}) collective-permute-start(bf16[16,4608]{1,0:T(8,128)(2,1)S(1)} %collective-permute-done.7), channel_id=1, source_target_pairs={{0,16},{16,0},{1,17},{17,1},{2,18},{18,2},{3,19},{19,3},{4,20},{20... | collective-permute-start | bytes 442376 | tf_op jit(solution)/shard_map/ppermute | solution.py:169
  38.3 1.9 %collective-permute-start.14 = (bf16[48,4608]{1,0:T(8,128)(2,1)S(1)}, bf16[48,4608]{1,0:T(8,128)(2,1)S(1)}, u32[]{:S(2)}, u32[]{:S(2)}) collective-permute-start(bf16[48,4608]{1,0:T(8,128)(2,1)S(1)} %constant_dynamic-update-slice_fusion.9.refs_6_), channel_id=1, source_target_pairs={{0,1},{1,0},{2,3},{3,2},{4,5},{5,4},{6,7},{7,6},{8,9},{9,8},{10,11... | collective-permute-start | bytes 1327112 | tf_op jit(solution)/shard_map/ppermute | solution.py:166

commit v7 on v6

--- a/solution.py
+++ b/solution.py
@@ -48,7 +48,7 @@
             place += wide
 
 
-def head_kernel(seq_dev, lengths_hbm, in_ref, gram_ref, member_ref, lengths_ref, sem):
+def head_kernel(seq_dev, lengths_hbm, in_ref, gram_ref, member_ref, spread_ref, lengths_ref, sem):
     copy = pltpu.make_async_copy(lengths_hbm, lengths_ref, sem)
     copy.start()
     head = in_ref[:, :HEAD]
@@ -58,11 +58,13 @@
     which = lax.broadcasted_iota(jnp.int32, (seqs, tok_cap), 0)
     position = lax.broadcasted_iota(jnp.int32, (seqs, tok_cap), 1)
     member = jnp.zeros((seqs, tok_cap), jnp.float32)
+    rows = lax.broadcasted_iota(jnp.int32, spread_ref.shape[1:], 0)
     low = 0
     for k in range(seq_dev):
         high = low + lengths_ref[lax.axis_index("seq") * seq_dev + k]
         inside = (which == k) & (position >= low) & (position < high)
         member = jnp.where(inside, 1.0, member)
+        spread_ref[k] = ((rows >= low) & (rows < high)).astype(jnp.float32)
         low = high
     member_ref[...] = member
 
@@ -107,7 +109,7 @@
     for ref in (out_ref, in_ref):
         wide = ref.shape[1] // (2 * chunks)
         result = None
-        for j in range(chunks):
+        for j in reversed(range(chunks)):
             rows = merged_rows(blocks, offset, wide, j, chunks, rank_rows)
             start = pl.multiple_of(((j ^ turn(paired, chunks)) * 2 + half) * wide, 128)
             part = inner_rows(ref[:, pl.ds(start, wide)], rows)
@@ -133,7 +135,7 @@
     held_ref[1] = held_in
 
 
-def score_kernel(rank_rows, paired, places, norm_ref, member_ref, held_ref, out_ref, in_ref, *refs):
+def score_kernel(rank_rows, paired, places, norm_ref, spread_ref, held_ref, out_ref, in_ref, *refs):
     *array_refs, score_ref = refs
     blocks = [(array_refs[i], row) for i, row in places]
     half = 1 - first_half(paired)
@@ -147,10 +149,11 @@
     if paired:
         source = source ^ me
     query = (source * rank_rows) // RANK
-    sums = jnp.dot(
-        member_ref[...], product, precision=lax.Precision.HIGHEST, preferred_element_type=jnp.float32
-    )
-    seqs, tok_cap = member_ref.shape
+    seqs, tok_cap = -(-spread_ref.shape[0] // 8) * 8, spread_ref.shape[1]
+    which = lax.broadcasted_iota(jnp.int32, (seqs, product.shape[1]), 0)
+    sums = jnp.zeros(which.shape, jnp.float32)
+    for k in range(spread_ref.shape[0]):
+        sums = jnp.where(which == k, jnp.sum(product * spread_ref[k], axis=0, keepdims=True), sums)
     diagonal = lax.broadcasted_iota(jnp.int32, (seqs, tok_cap), 0) == lax.broadcasted_iota(
         jnp.int32, (seqs, tok_cap), 1
     )
@@ -175,14 +178,14 @@
     x1, y1, z3 = across(z1), swap(z1, 2), swap(own, 12)
     z2, y1, y0, lengths = gate(z2, y1, y0, lengths)
     x_near, y2 = across(stack(z2, y1)), swap(z2, 2)
-    head, member = head_step(lengths)
+    head, member, spread = head_step(lengths)
     z3, y2, head, member = gate(z3, y2, head, member)
     x_far, y3 = across(stack(z3, y2)), swap(z3, 2)
     early = stack(y0, z1, y1, z2, x1)
     early_core = swap(early, 1)
+    y3, member = gate(y3, member)
+    x_last = across(y3)
     norms = norm_step(member, head)
-    y3, norms = gate(y3, norms)
-    x_last = across(y3)
     middle = stack(y2, z3, y3, x_near)
     middle_core = swap(middle, 1)
     mine, other = {}, {}
@@ -195,10 +198,10 @@
     place(early, early_core, ((mine, 2), (other, 2), (mine, 4), (mine, 6), (mine, 8), (other, 4)))
     place(middle, middle_core, ((mine, 10), (mine, 12), (mine, 14), (other, 8), (other, 6)))
     partial = partial_step([mine[b] for b in range(devices)])
-    x_last, partial = gate(x_last, partial)
+    x_last, partial, norms = gate(x_last, partial, norms)
     late = stack(x_far, x_last)
     place(late, swap(late, 1), ((other, 12), (other, 10), (other, 14)))
-    return [other[b] for b in range(devices)], norms, member, partial
+    return [other[b] for b in range(devices)], norms, spread, partial
 
 
 def refs_of(blocks):
@@ -236,6 +239,7 @@
         compiler_params=score_params,
     )(factor_u, factor_v)
 
+    frows = devices * rank_rows
     tiny = pl.CostEstimate(flops=1, bytes_accessed=1, transcendentals=0)
 
     def head_step(lengths):
@@ -244,9 +248,10 @@
             out_shape=[
                 jax.ShapeDtypeStruct((tok_cap, tok_cap), jnp.float32),
                 jax.ShapeDtypeStruct((seqs, tok_cap), jnp.float32),
+                jax.ShapeDtypeStruct((seq_dev, tok_cap, frows), jnp.float32),
             ],
             in_specs=[hbm, vmem],
-            out_specs=[vmem] * 2,
+            out_specs=[vmem] * 3,
             scratch_shapes=[pltpu.SMEM(lengths.shape, lengths.dtype), pltpu.SemaphoreType.DMA],
             compiler_params=score_params,
             cost_estimate=tiny,
@@ -262,7 +267,6 @@
             cost_estimate=tiny,
         )(member, head, out_grads, layer_inputs)
 
-    frows = devices * rank_rows
     def partial_step(blocks):
         arrays, places = refs_of(blocks)
         return pl.pallas_call(
@@ -275,11 +279,11 @@
         )(out_grads, layer_inputs, *arrays)
 
     if paired:
-        other, norms, member, partial = gather_blocks(
+        other, norms, spread, partial = gather_blocks(
             packed[0], packed[1], devices, seq_lengths, head_step, norm_step, partial_step
         )
     else:
-        head, member = head_step(seq_lengths)
+        head, member, spread = head_step(seq_lengths)
         norms = norm_step(member, head)
         gathered = lax.all_gather(packed[0], "seq", axis=0, tiled=True)
         partial = partial_step([(gathered, 2 * PACK * b) for b in range(devices)])
@@ -292,7 +296,7 @@
         out_specs=vmem,
         compiler_params=score_params,
         cost_estimate=tiny,
-    )(norms, member, partial, out_grads, layer_inputs, *arrays)
+    )(norms, spread, partial, out_grads, layer_inputs, *arrays)
 
 
 def solution(mesh):

time: 43.2 us -> 42.7 us (0.988)
  waiting for transfers between devices: 7.64 us -> 8.51 us
  Pallas kernels: 7.85 us -> 7.14 us
  local copies, waits for them, and re-layouts: 6.33 us -> 5.68 us
    ppermute x11, waiting for transfers between devices: 3.45 us -> 6.46 us  [swap(): return lax.ppermute(value, 'seq', [(i, i ^ mask) for i in range(devices)])]
    ppermute x4, waiting for transfers between devices: 4.19 us -> 2.05 us  [across(): return lax.ppermute(value, 'grp', [(0, 1), (1, 0)])]
    unnamed x20, local copies, waits for them, and re-layouts: 6.28 us -> 5.63 us
    pallas_call x1, Pallas kernels: 2.8 us -> 2.31 us  [local(): pl.pallas_call(functools.partial(score_kernel, rank_rows, paired, places)...]
  transfers between devices with their start and end apart: 15 -> 15, of which waited for: 5 -> 5; matrix products, arithmetic and copies ran while one was open for 0% -> 0% of each run, Pallas kernels for 12% -> 11%
where the time goes in v7:
time: 42.7 us; the launch traced here: 42.4 us
  starting transfers between devices  20.9 us (49%)
  waiting for transfers between devices  8.51 us (20%)
  Pallas kernels  7.14 us (17%)
  local copies, waits for them, and re-layouts  5.68 us (13%)
    ppermute x11, starting transfers between devices, swap(): return lax.ppermute(value, 'seq', [(i, i ^ mask) for i in range(devices)])  15.9 us
    ppermute x11, waiting for transfers between devices, swap(): return lax.ppermute(value, 'seq', [(i, i ^ mask) for i in range(devices)])  6.46 us
    unnamed x20, local copies, waits for them, and re-layouts  5.63 us
    ppermute x4, starting transfers between devices, across(): return lax.ppermute(value, 'grp', [(0, 1), (1, 0)])  4.94 us
    pallas_call x1, Pallas kernels, norm_step(): pl.pallas_call(norm_kernel, out_shape=jax.ShapeDtypeStruct((1, tok_cap),...  2.36 us
    pallas_call x1, Pallas kernels, local(): pl.pallas_call(functools.partial(score_kernel, rank_rows, paired, places)...  2.31 us
    ppermute x4, waiting for transfers between devices, across(): return lax.ppermute(value, 'grp', [(0, 1), (1, 0)])  2.05 us
    pallas_call x1, Pallas kernels, partial_step(): pl.pallas_call(functools.partial(partial_kernel, rank_rows, paired, place...  1.63 us
  transfers between devices with their start and end apart: 15, of which 5 were waited for; matrix products, arithmetic and copies ran while one was open for 0% of the time, Pallas kernels for 11%

profile of v7, /device:TPU:0, one launch (start us, length us, event | category | flops | bytes accessed | tf_op | source)
XLA Modules:
  0.0 42.4 jit_solution(9746500689857575419)
XLA Ops:
  0.0 0.9 %copy-done.3 = bf16[4,28672]{1,0:T(4,128)(2,1)S(1)} copy-done((bf16[4,28672]{1,0:T(4,128)(2,1)S(1)}, bf16[4,28672]{1,0:T(4,128)(2,1)}, u32[]{:S(2)}) %copy-start.3) | copy-done | bytes 229400
  0.9 0.8 %copy-done.4 = bf16[4,8192]{1,0:T(4,128)(2,1)S(1)} copy-done((bf16[4,8192]{1,0:T(4,128)(2,1)S(1)}, bf16[4,8192]{1,0:T(4,128)(2,1)}, u32[]{:S(2)}) %copy-start.4) | copy-done | bytes 65560
  1.9 0.5 %collective-permute-start.1 = (bf16[32,4608]{1,0:T(8,128)(2,1)S(1)}, bf16[32,4608]{1,0:T(8,128)(2,1)S(1)}, u32[]{:S(2)}, u32[]{:S(2)}) collective-permute-start(bf16[32,4608]{1,0:T(8,128)(2,1)S(1)} %get-tuple-element.27.refs_0_), channel_id=1, source_target_pairs={{0,1},{1,0},{2,3},{3,2},{4,5},{5,4},{6,7},{7,6},{8,9},{9,8},{10,11... | collective-permute-start | bytes 884744 | tf_op jit(solution)/shard_map/ppermute | solution.py:169
  2.4 2.6 %collective-permute-start = (bf16[16,4608]{1,0:T(8,128)(2,1)S(1)}, bf16[16,4608]{1,0:T(8,128)(2,1)S(1)}, u32[]{:S(2)}, u32[]{:S(2)}) collective-permute-start(bf16[16,4608]{1,0:T(8,128)(2,1)S(1)} %get-tuple-element.28), channel_id=1, source_target_pairs={{0,4},{1,5},{2,6},{3,7},{4,0},{5,1},{6,2},{7,3},{8,12},{9,13},{10,... | collective-permute-start | bytes 442376 | tf_op jit(solution)/shard_map/ppermute | solution.py:169
  5.0 1.5 %collective-permute-start.5 = (bf16[32,4608]{1,0:T(8,128)(2,1)S(1)}, bf16[32,4608]{1,0:T(8,128)(2,1)S(1)}, u32[]{:S(2)}, u32[]{:S(2)}) collective-permute-start(bf16[32,4608]{1,0:T(8,128)(2,1)S(1)} %get-tuple-element.27.refs_0_), channel_id=1, source_target_pairs={{0,2},{1,3},{2,0},{3,1},{4,6},{5,7},{6,4},{7,5},{8,10},{9,11},{10,... | collective-permute-start | bytes 884744 | tf_op jit(solution)/shard_map/ppermute | solution.py:169
  6.5 2.6 %collective-permute-start.3 = (bf16[16,4608]{1,0:T(8,128)(2,1)S(1)}, bf16[16,4608]{1,0:T(8,128)(2,1)S(1)}, u32[]{:S(2)}, u32[]{:S(2)}) collective-permute-start(bf16[16,4608]{1,0:T(8,128)(2,1)S(1)} %get-tuple-element.28), channel_id=1, source_target_pairs={{0,8},{1,9},{2,10},{3,11},{4,12},{5,13},{6,14},{7,15},{8,0},{9,1},... | collective-permute-start | bytes 442376 | tf_op jit(solution)/shard_map/ppermute | solution.py:169
  9.1 0.3 collective-permute-done
  9.5 4.5 %collective-permute-start.4 = (bf16[16,4608]{1,0:T(8,128)(2,1)S(1)}, bf16[16,4608]{1,0:T(8,128)(2,1)S(1)}, u32[]{:S(2)}, u32[]{:S(2)}) collective-permute-start(bf16[16,4608]{1,0:T(8,128)(2,1)S(1)} %collective-permute-done), channel_id=1, source_target_pairs={{0,2},{1,3},{2,0},{3,1},{4,6},{5,7},{6,4},{7,5},{8,10},{9,11},{10,... | collective-permute-start | bytes 442376 | tf_op jit(solution)/shard_map/ppermute | solution.py:169
  14.0 1.5 %collective-permute-start.9 = (bf16[16,4608]{1,0:T(8,128)(2,1)S(1)}, bf16[16,4608]{1,0:T(8,128)(2,1)S(1)}, u32[]{:S(2)}, u32[]{:S(2)}) collective-permute-start(bf16[16,4608]{1,0:T(8,128)(2,1)S(1)} %collective-permute-done), channel_id=1, source_target_pairs={{0,16},{16,0},{1,17},{17,1},{2,18},{18,2},{3,19},{19,3},{4,20},{20... | collective-permute-start | bytes 442376 | tf_op jit(solution)/shard_map/ppermute | solution.py:172
  15.5 2.5 %collective-permute-start.2 = (bf16[16,4608]{1,0:T(8,128)(2,1)S(1)}, bf16[16,4608]{1,0:T(8,128)(2,1)S(1)}, u32[]{:S(2)}, u32[]{:S(2)}) collective-permute-start(bf16[16,4608]{1,0:T(8,128)(2,1)S(1)} %get-tuple-element.28), channel_id=1, source_target_pairs={{0,12},{1,13},{2,14},{3,15},{4,8},{5,9},{6,10},{7,11},{8,4},{9,5},... | collective-permute-start | bytes 442376 | tf_op jit(solution)/shard_map/ppermute | solution.py:169
  18.0 1.2 %collective-permute-start.6 = (bf16[16,4608]{1,0:T(8,128)(2,1)S(1)}, bf16[16,4608]{1,0:T(8,128)(2,1)S(1)}, u32[]{:S(2)}, u32[]{:S(2)}) collective-permute-start(bf16[16,4608]{1,0:T(8,128)(2,1)S(1)} %collective-permute-done.3), channel_id=1, source_target_pairs={{0,2},{1,3},{2,0},{3,1},{4,6},{5,7},{6,4},{7,5},{8,10},{9,11},{10,... | collective-permute-start | bytes 442376 | tf_op jit(solution)/shard_map/ppermute | solution.py:169
  19.4 1.6 %collective-permute-start.11 = (bf16[32,4608]{1,0:T(8,128)(2,1)S(1)}, bf16[32,4608]{1,0:T(8,128)(2,1)S(1)}, u32[]{:S(2)}, u32[]{:S(2)}) collective-permute-start(bf16[32,4608]{1,0:T(8,128)(2,1)S(1)} %pad_maximum_fusion), channel_id=1, source_target_pairs={{0,16},{16,0},{1,17},{17,1},{2,18},{18,2},{3,19},{19,3},{4,20},{20... | collective-permute-start | bytes 884744 | tf_op jit(solution)/shard_map/ppermute | solution.py:172
  20.9 3.1 %copy-done = bf16[128,28672]{1,0:T(8,128)(2,1)S(1)} copy-done((bf16[128,28672]{1,0:T(8,128)(2,1)S(1)}, bf16[128,28672]{1,0:T(8,128)(2,1)}, u32[]{:S(2)}) %copy-start) | copy-done | bytes 7340056
  24.0 0.7 %copy-done.5 = s32[64]{0:T(128)S(1)} copy-done((s32[64]{0:T(128)S(1)}, s32[64]{0:T(128)}, u32[]{:S(2)}) %copy-start.5) | copy-done | bytes 280
  24.7 0.8 %shard_map.56 = (f32[128,128]{1,0:T(8,128)S(1)}, f32[8,128]{1,0:T(8,128)S(1)}, f32[4,128,64]{2,1,0:T(8,128)S(1)}) custom-call(s32[64]{0:T(128)S(1)} %copy-done.5, bf16[128,28672]{1,0:T(8,128)(2,1)S(1)} %copy-done), custom_call_target="tpu_custom_call" | custom-call | flops 1 | bytes 1 | tf_op jit(solution)/shard_map/pallas_call | solution.py:246
  25.8 1.3 %collective-permute-start.13 = (bf16[32,4608]{1,0:T(8,128)(2,1)S(1)}, bf16[32,4608]{1,0:T(8,128)(2,1)S(1)}, u32[]{:S(2)}, u32[]{:S(2)}) collective-permute-start(bf16[32,4608]{1,0:T(8,128)(2,1)S(1)} %pad_maximum_fusion.1), channel_id=1, source_target_pairs={{0,16},{16,0},{1,17},{17,1},{2,18},{18,2},{3,19},{19,3},{4,20},{20... | collective-permute-start | bytes 884744 | tf_op jit(solution)/shard_map/ppermute | solution.py:172
  27.1 4.3 %collective-permute-done.7 = bf16[16,4608]{1,0:T(8,128)(2,1)S(1)} collective-permute-done((bf16[16,4608]{1,0:T(8,128)(2,1)S(1)}, bf16[16,4608]{1,0:T(8,128)(2,1)S(1)}, u32[]{:S(2)}, u32[]{:S(2)}) %collective-permute-start.7) | collective-permute-done | bytes 147488 | tf_op jit(solution)/shard_map/ppermute | solution.py:169
  31.6 0.6 %collective-permute-start.8 = (bf16[16,4608]{1,0:T(8,128)(2,1)S(1)}, bf16[16,4608]{1,0:T(8,128)(2,1)S(1)}, u32[]{:S(2)}, u32[]{:S(2)}) collective-permute-start(bf16[16,4608]{1,0:T(8,128)(2,1)S(1)} %collective-permute-done.7), channel_id=1, source_target_pairs={{0,16},{16,0},{1,17},{17,1},{2,18},{18,2},{3,19},{19,3},{4,20},{20... | collective-permute-start | bytes 442376 | tf_op jit(solution)/shard_map/ppermute | solution.py:172
  32.2 2.4 %shard_map.58.norm_ref = f32[1,128]{1,0:T(1,128)S(1)} custom-call(f32[8,128]{1,0:T(8,128)S(1)} %get-tuple-element.41.member_ref, f32[128,128]{1,0:T(8,128)S(1)} %get-tuple-element.42.head_ref, bf16[128,8192]{1,0:T(8,128)(2,1)S(1)} %copy-done.2, bf16[128,28672]{1,0:T(8,128)(2,1)S(1)} %copy-done.1), custom_call_target="tpu_custom_call" | custom-call | flops 1 | bytes 1 | tf_op jit(solution)/shard_map/pallas_call | solution.py:261
  34.5 0.9 %collective-permute-done.13 = bf16[32,4608]{1,0:T(8,128)(2,1)S(1)} collective-permute-done((bf16[32,4608]{1,0:T(8,128)(2,1)S(1)}, bf16[32,4608]{1,0:T(8,128)(2,1)S(1)}, u32[]{:S(2)}, u32[]{:S(2)}) %collective-permute-start.13) | collective-permute-done | bytes 294944 | tf_op jit(solution)/shard_map/ppermute | solution.py:172
  35.5 1.6 %shard_map.57.held_ref = f32[2,128,64]{2,1,0:T(8,128)S(1)} custom-call(bf16[128,8192]{1,0:T(8,128)(2,1)S(1)} %copy-done.2, bf16[128,28672]{1,0:T(8,128)(2,1)S(1)} %copy-done.1, bf16[32,4608]{1,0:T(8,128)(2,1)S(1)} %get-tuple-element.27.refs_0_, bf16[32,4608]{1,0:T(8,128)(2,1)S(1)} %collective-permute-done.1.refs_1_, ...), custom_call_target="tpu_custom_call" | custom-call | flops 1 | bytes 1 | tf_op jit(solution)/shard_map/pallas_call | solution.py:272
  37.1 1.1 %collective-permute-done.8 = bf16[16,4608]{1,0:T(8,128)(2,1)S(1)} collective-permute-done((bf16[16,4608]{1,0:T(8,128)(2,1)S(1)}, bf16[16,4608]{1,0:T(8,128)(2,1)S(1)}, u32[]{:S(2)}, u32[]{:S(2)}) %collective-permute-start.8) | collective-permute-done | bytes 147488 | tf_op jit(solution)/shard_map/ppermute | solution.py:172
  38.4 1.8 %collective-permute-done.14.refs_7_ = bf16[48,4608]{1,0:T(8,128)(2,1)S(1)} collective-permute-done((bf16[48,4608]{1,0:T(8,128)(2,1)S(1)}, bf16[48,4608]{1,0:T(8,128)(2,1)S(1)}, u32[]{:S(2)}, u32[]{:S(2)}) %collective-permute-start.14) | collective-permute-done | bytes 442400 | tf_op jit(solution)/shard_map/ppermute | solution.py:169
  40.1 2.3 %shard_map.59 = f32[2,4]{1,0:T(2,128)} custom-call(f32[1,128]{1,0:T(1,128)S(1)} %shard_map.58.norm_ref, f32[4,128,64]{2,1,0:T(8,128)S(1)} %get-tuple-element.44.spread_ref, f32[2,128,64]{2,1,0:T(8,128)S(1)} %shard_map.57.held_ref, bf16[128,8192]{1,0:T(8,128)(2,1)S(1)} %copy-done.2, bf16[128,28672]{1,0:T(8,128)(2,1)S(1)} %copy-done.1, ...), custom_call_target="tpu_custom_call" | custom-call | flops 1 | bytes 1 | tf_op jit(solution)/shard_map/pallas_call | solution.py:292
  (36 shorter events, 0.8 us)
Async XLA Ops:
  0.0 0.9 %copy-start.3 = (bf16[4,28672]{1,0:T(4,128)(2,1)S(1)}, bf16[4,28672]{1,0:T(4,128)(2,1)}, u32[]{:S(2)}) copy-start(bf16[4,28672]{1,0:T(4,128)(2,1)} %v_ref.1) | copy-start | bytes 688132
  0.9 0.8 %copy-start.4 = (bf16[4,8192]{1,0:T(4,128)(2,1)S(1)}, bf16[4,8192]{1,0:T(4,128)(2,1)}, u32[]{:S(2)}) copy-start(bf16[4,8192]{1,0:T(4,128)(2,1)} %u_ref.1) | copy-start | bytes 196612
  1.8 30.4 %copy-start.2 = (bf16[128,8192]{1,0:T(8,128)(2,1)S(1)}, bf16[128,8192]{1,0:T(8,128)(2,1)}, u32[]{:S(2)}) copy-start(bf16[128,8192]{1,0:T(8,128)(2,1)} %out_ref.5) | copy-start | bytes 6291460
  1.9 7.6 %collective-permute-start.1 = (bf16[32,4608]{1,0:T(8,128)(2,1)S(1)}, bf16[32,4608]{1,0:T(8,128)(2,1)S(1)}, u32[]{:S(2)}, u32[]{:S(2)}) collective-permute-start(bf16[32,4608]{1,0:T(8,128)(2,1)S(1)} %get-tuple-element.27.refs_0_), channel_id=1, source_target_pairs={{0,1},{1,0},{2,3},{3,2},{4,5},{5,4},{6,7},{7,6},{8,9},{9,8},{10,11... | collective-permute-start | bytes 884744 | tf_op jit(solution)/shard_map/ppermute | solution.py:169
  2.4 7.1 %collective-permute-start = (bf16[16,4608]{1,0:T(8,128)(2,1)S(1)}, bf16[16,4608]{1,0:T(8,128)(2,1)S(1)}, u32[]{:S(2)}, u32[]{:S(2)}) collective-permute-start(bf16[16,4608]{1,0:T(8,128)(2,1)S(1)} %get-tuple-element.28), channel_id=1, source_target_pairs={{0,4},{1,5},{2,6},{3,7},{4,0},{5,1},{6,2},{7,3},{8,12},{9,13},{10,... | collective-permute-start | bytes 442376 | tf_op jit(solution)/shard_map/ppermute | solution.py:169
  5.0 12.9 %collective-permute-start.5 = (bf16[32,4608]{1,0:T(8,128)(2,1)S(1)}, bf16[32,4608]{1,0:T(8,128)(2,1)S(1)}, u32[]{:S(2)}, u32[]{:S(2)}) collective-permute-start(bf16[32,4608]{1,0:T(8,128)(2,1)S(1)} %get-tuple-element.27.refs_0_), channel_id=1, source_target_pairs={{0,2},{1,3},{2,0},{3,1},{4,6},{5,7},{6,4},{7,5},{8,10},{9,11},{10,... | collective-permute-start | bytes 884744 | tf_op jit(solution)/shard_map/ppermute | solution.py:169
  6.5 11.4 %collective-permute-start.3 = (bf16[16,4608]{1,0:T(8,128)(2,1)S(1)}, bf16[16,4608]{1,0:T(8,128)(2,1)S(1)}, u32[]{:S(2)}, u32[]{:S(2)}) collective-permute-start(bf16[16,4608]{1,0:T(8,128)(2,1)S(1)} %get-tuple-element.28), channel_id=1, source_target_pairs={{0,8},{1,9},{2,10},{3,11},{4,12},{5,13},{6,14},{7,15},{8,0},{9,1},... | collective-permute-start | bytes 442376 | tf_op jit(solution)/shard_map/ppermute | solution.py:169
  9.5 8.5 %collective-permute-start.4 = (bf16[16,4608]{1,0:T(8,128)(2,1)S(1)}, bf16[16,4608]{1,0:T(8,128)(2,1)S(1)}, u32[]{:S(2)}, u32[]{:S(2)}) collective-permute-start(bf16[16,4608]{1,0:T(8,128)(2,1)S(1)} %collective-permute-done), channel_id=1, source_target_pairs={{0,2},{1,3},{2,0},{3,1},{4,6},{5,7},{6,4},{7,5},{8,10},{9,11},{10,... | collective-permute-start | bytes 442376 | tf_op jit(solution)/shard_map/ppermute | solution.py:169
  14.0 5.3 %collective-permute-start.9 = (bf16[16,4608]{1,0:T(8,128)(2,1)S(1)}, bf16[16,4608]{1,0:T(8,128)(2,1)S(1)}, u32[]{:S(2)}, u32[]{:S(2)}) collective-permute-start(bf16[16,4608]{1,0:T(8,128)(2,1)S(1)} %collective-permute-done), channel_id=1, source_target_pairs={{0,16},{16,0},{1,17},{17,1},{2,18},{18,2},{3,19},{19,3},{4,20},{20... | collective-permute-start | bytes 442376 | tf_op jit(solution)/shard_map/ppermute | solution.py:172
  15.5 10.0 %collective-permute-start.2 = (bf16[16,4608]{1,0:T(8,128)(2,1)S(1)}, bf16[16,4608]{1,0:T(8,128)(2,1)S(1)}, u32[]{:S(2)}, u32[]{:S(2)}) collective-permute-start(bf16[16,4608]{1,0:T(8,128)(2,1)S(1)} %get-tuple-element.28), channel_id=1, source_target_pairs={{0,12},{1,13},{2,14},{3,15},{4,8},{5,9},{6,10},{7,11},{8,4},{9,5},... | collective-permute-start | bytes 442376 | tf_op jit(solution)/shard_map/ppermute | solution.py:169
  18.0 7.5 %collective-permute-start.6 = (bf16[16,4608]{1,0:T(8,128)(2,1)S(1)}, bf16[16,4608]{1,0:T(8,128)(2,1)S(1)}, u32[]{:S(2)}, u32[]{:S(2)}) collective-permute-start(bf16[16,4608]{1,0:T(8,128)(2,1)S(1)} %collective-permute-done.3), channel_id=1, source_target_pairs={{0,2},{1,3},{2,0},{3,1},{4,6},{5,7},{6,4},{7,5},{8,10},{9,11},{10,... | collective-permute-start | bytes 442376 | tf_op jit(solution)/shard_map/ppermute | solution.py:169
  19.3 16.2 %collective-permute-start.10 = (bf16[96,4608]{1,0:T(8,128)(2,1)S(1)}, bf16[96,4608]{1,0:T(8,128)(2,1)S(1)}, u32[]{:S(2)}, u32[]{:S(2)}) collective-permute-start(bf16[96,4608]{1,0:T(8,128)(2,1)S(1)} %constant_dynamic-update-slice_fusion.refs_2_), channel_id=1, source_target_pairs={{0,1},{1,0},{2,3},{3,2},{4,5},{5,4},{6,7},{7,6},{8,9},{9,8},{10,11... | collective-permute-start | bytes 2654216 | tf_op jit(solution)/shard_map/ppermute | solution.py:169
  19.4 12.1 %collective-permute-start.11 = (bf16[32,4608]{1,0:T(8,128)(2,1)S(1)}, bf16[32,4608]{1,0:T(8,128)(2,1)S(1)}, u32[]{:S(2)}, u32[]{:S(2)}) collective-permute-start(bf16[32,4608]{1,0:T(8,128)(2,1)S(1)} %pad_maximum_fusion), channel_id=1, source_target_pairs={{0,16},{16,0},{1,17},{17,1},{2,18},{18,2},{3,19},{19,3},{4,20},{20... | collective-permute-start | bytes 884744 | tf_op jit(solution)/shard_map/ppermute | solution.py:172
  20.9 3.1 %copy-start = (bf16[128,28672]{1,0:T(8,128)(2,1)S(1)}, bf16[128,28672]{1,0:T(8,128)(2,1)}, u32[]{:S(2)}) copy-start(bf16[128,28672]{1,0:T(8,128)(2,1)} %in_ref.7) | copy-start | bytes 22020100
  24.0 0.7 %copy-start.5 = (s32[64]{0:T(128)S(1)}, s32[64]{0:T(128)}, u32[]{:S(2)}) copy-start(s32[64]{0:T(128)} %lengths_hbm) | copy-start | bytes 772
  24.7 7.5 %copy-start.1 = (bf16[128,28672]{1,0:T(8,128)(2,1)S(1)}, bf16[128,28672]{1,0:T(8,128)(2,1)}, u32[]{:S(2)}) copy-start(bf16[128,28672]{1,0:T(8,128)(2,1)} %in_ref.7) | copy-start | bytes 22020100
  25.5 6.0 %collective-permute-start.7 = (bf16[16,4608]{1,0:T(8,128)(2,1)S(1)}, bf16[16,4608]{1,0:T(8,128)(2,1)S(1)}, u32[]{:S(2)}, u32[]{:S(2)}) collective-permute-start(bf16[16,4608]{1,0:T(8,128)(2,1)S(1)} %collective-permute-done.2), channel_id=1, source_target_pairs={{0,2},{1,3},{2,0},{3,1},{4,6},{5,7},{6,4},{7,5},{8,10},{9,11},{10,... | collective-permute-start | bytes 442376 | tf_op jit(solution)/shard_map/ppermute | solution.py:169
  25.8 9.6 %collective-permute-start.13 = (bf16[32,4608]{1,0:T(8,128)(2,1)S(1)}, bf16[32,4608]{1,0:T(8,128)(2,1)S(1)}, u32[]{:S(2)}, u32[]{:S(2)}) collective-permute-start(bf16[32,4608]{1,0:T(8,128)(2,1)S(1)} %pad_maximum_fusion.1), channel_id=1, source_target_pairs={{0,16},{16,0},{1,17},{17,1},{2,18},{18,2},{3,19},{19,3},{4,20},{20... | collective-permute-start | bytes 884744 | tf_op jit(solution)/shard_map/ppermute | solution.py:172
  31.5 4.0 %collective-permute-start.12 = (bf16[80,4608]{1,0:T(8,128)(2,1)S(1)}, bf16[80,4608]{1,0:T(8,128)(2,1)S(1)}, u32[]{:S(2)}, u32[]{:S(2)}) collective-permute-start(bf16[80,4608]{1,0:T(8,128)(2,1)S(1)} %constant_dynamic-update-slice_fusion.5.refs_4_), channel_id=1, source_target_pairs={{0,1},{1,0},{2,3},{3,2},{4,5},{5,4},{6,7},{7,6},{8,9},{9,8},{10,11... | collective-permute-start | bytes 2211848 | tf_op jit(solution)/shard_map/ppermute | solution.py:169
  31.6 6.7 %collective-permute-start.8 = (bf16[16,4608]{1,0:T(8,128)(2,1)S(1)}, bf16[16,4608]{1,0:T(8,128)(2,1)S(1)}, u32[]{:S(2)}, u32[]{:S(2)}) collective-permute-start(bf16[16,4608]{1,0:T(8,128)(2,1)S(1)} %collective-permute-done.7), channel_id=1, source_target_pairs={{0,16},{16,0},{1,17},{17,1},{2,18},{18,2},{3,19},{19,3},{4,20},{20... | collective-permute-start | bytes 442376 | tf_op jit(solution)/shard_map/ppermute | solution.py:172
  38.3 1.9 %collective-permute-start.14 = (bf16[48,4608]{1,0:T(8,128)(2,1)S(1)}, bf16[48,4608]{1,0:T(8,128)(2,1)S(1)}, u32[]{:S(2)}, u32[]{:S(2)}) collective-permute-start(bf16[48,4608]{1,0:T(8,128)(2,1)S(1)} %constant_dynamic-update-slice_fusion.9.refs_6_), channel_id=1, source_target_pairs={{0,1},{1,0},{2,3},{3,2},{4,5},{5,4},{6,7},{7,6},{8,9},{9,8},{10,11... | collective-permute-start | bytes 1327112 | tf_op jit(solution)/shard_map/ppermute | solution.py:169

commit v8 on v7

--- a/solution.py
+++ b/solution.py
@@ -178,12 +178,14 @@
     x1, y1, z3 = across(z1), swap(z1, 2), swap(own, 12)
     z2, y1, y0, lengths = gate(z2, y1, y0, lengths)
     x_near, y2 = across(stack(z2, y1)), swap(z2, 2)
+    z3, y2, lengths = gate(z3, y2, lengths)
     head, member, spread = head_step(lengths)
-    z3, y2, head, member = gate(z3, y2, head, member)
-    x_far, y3 = across(stack(z3, y2)), swap(z3, 2)
+    x3, y3 = across(z3), swap(z3, 2)
     early = stack(y0, z1, y1, z2, x1)
     early_core = swap(early, 1)
-    y3, member = gate(y3, member)
+    x_near, head = gate(x_near, head)
+    yx2 = swap(x_near[:PACK], 2)
+    y3, member, head = gate(y3, member, head)
     x_last = across(y3)
     norms = norm_step(member, head)
     middle = stack(y2, z3, y3, x_near)
@@ -199,7 +201,7 @@
     place(middle, middle_core, ((mine, 10), (mine, 12), (mine, 14), (other, 8), (other, 6)))
     partial = partial_step([mine[b] for b in range(devices)])
     x_last, partial, norms = gate(x_last, partial, norms)
-    late = stack(x_far, x_last)
+    late = stack(x3, yx2, x_last)
     place(late, swap(late, 1), ((other, 12), (other, 10), (other, 14)))
     return [other[b] for b in range(devices)], norms, spread, partial
 

time: 42.7 us -> 41.7 us (0.977)
  waiting for transfers between devices: 8.51 us -> 5 us
  starting transfers between devices: 20.9 us -> 22.8 us
  local copies, waits for them, and re-layouts: 5.68 us -> 6.26 us
    ppermute x11 -> x12, starting transfers between devices: 15.9 us -> 18.3 us  [swap(): return lax.ppermute(value, 'seq', [(i, i ^ mask) for i in range(devices)])]
    ppermute x4, waiting for transfers between devices: 2.05 us -> 0.01 us  [across(): return lax.ppermute(value, 'grp', [(0, 1), (1, 0)])]
    ppermute x11 -> x12, waiting for transfers between devices: 6.46 us -> 4.99 us  [swap(): return lax.ppermute(value, 'seq', [(i, i ^ mask) for i in range(devices)])]
    unnamed x20 -> x21, local copies, waits for them, and re-layouts: 5.63 us -> 6.2 us
  transfers between devices with their start and end apart: 15 -> 16, of which waited for: 5 -> 5; matrix products, arithmetic and copies ran while one was open for 0% -> 0% of each run, Pallas kernels for 11% -> 11%
where the time goes in v8:
time: 41.7 us; the launch traced here: 41.4 us
  starting transfers between devices  22.8 us (55%)
  Pallas kernels  7.14 us (17%)
  local copies, waits for them, and re-layouts  6.26 us (15%)
  waiting for transfers between devices  5 us (12%)
    ppermute x12, starting transfers between devices, swap(): return lax.ppermute(value, 'seq', [(i, i ^ mask) for i in range(devices)])  18.3 us
    unnamed x21, local copies, waits for them, and re-layouts  6.2 us
    ppermute x12, waiting for transfers between devices, swap(): return lax.ppermute(value, 'seq', [(i, i ^ mask) for i in range(devices)])  4.99 us
    ppermute x4, starting transfers between devices, across(): return lax.ppermute(value, 'grp', [(0, 1), (1, 0)])  4.55 us
    pallas_call x1, Pallas kernels, norm_step(): pl.pallas_call(norm_kernel, out_shape=jax.ShapeDtypeStruct((1, tok_cap),...  2.36 us
    pallas_call x1, Pallas kernels, local(): pl.pallas_call(functools.partial(score_kernel, rank_rows, paired, places)...  2.31 us
    pallas_call x1, Pallas kernels, partial_step(): pl.pallas_call(functools.partial(partial_kernel, rank_rows, paired, place...  1.63 us
  transfers between devices with their start and end apart: 16, of which 5 were waited for; matrix products, arithmetic and copies ran while one was open for 0% of the time, Pallas kernels for 11%

profile of v8, /device:TPU:0, one launch (start us, length us, event | category | flops | bytes accessed | tf_op | source)
XLA Modules:
  0.0 41.4 jit_solution(15899796918858881567)
XLA Ops:
  0.0 0.9 %copy-done.3 = bf16[4,28672]{1,0:T(4,128)(2,1)S(1)} copy-done((bf16[4,28672]{1,0:T(4,128)(2,1)S(1)}, bf16[4,28672]{1,0:T(4,128)(2,1)}, u32[]{:S(2)}) %copy-start.3) | copy-done | bytes 229400
  0.9 0.8 %copy-done.4 = bf16[4,8192]{1,0:T(4,128)(2,1)S(1)} copy-done((bf16[4,8192]{1,0:T(4,128)(2,1)S(1)}, bf16[4,8192]{1,0:T(4,128)(2,1)}, u32[]{:S(2)}) %copy-start.4) | copy-done | bytes 65560
  2.4 2.6 %collective-permute-start = (bf16[16,4608]{1,0:T(8,128)(2,1)S(1)}, bf16[16,4608]{1,0:T(8,128)(2,1)S(1)}, u32[]{:S(2)}, u32[]{:S(2)}) collective-permute-start(bf16[16,4608]{1,0:T(8,128)(2,1)S(1)} %get-tuple-element.30), channel_id=1, source_target_pairs={{0,4},{1,5},{2,6},{3,7},{4,0},{5,1},{6,2},{7,3},{8,12},{9,13},{10,... | collective-permute-start | bytes 442376 | tf_op jit(solution)/shard_map/ppermute | solution.py:169
  5.0 1.5 %collective-permute-start.5 = (bf16[32,4608]{1,0:T(8,128)(2,1)S(1)}, bf16[32,4608]{1,0:T(8,128)(2,1)S(1)}, u32[]{:S(2)}, u32[]{:S(2)}) collective-permute-start(bf16[32,4608]{1,0:T(8,128)(2,1)S(1)} %get-tuple-element.29.refs_0_), channel_id=1, source_target_pairs={{0,2},{1,3},{2,0},{3,1},{4,6},{5,7},{6,4},{7,5},{8,10},{9,11},{10,... | collective-permute-start | bytes 884744 | tf_op jit(solution)/shard_map/ppermute | solution.py:169
  6.5 2.6 %collective-permute-start.3 = (bf16[16,4608]{1,0:T(8,128)(2,1)S(1)}, bf16[16,4608]{1,0:T(8,128)(2,1)S(1)}, u32[]{:S(2)}, u32[]{:S(2)}) collective-permute-start(bf16[16,4608]{1,0:T(8,128)(2,1)S(1)} %get-tuple-element.30), channel_id=1, source_target_pairs={{0,8},{1,9},{2,10},{3,11},{4,12},{5,13},{6,14},{7,15},{8,0},{9,1},... | collective-permute-start | bytes 442376 | tf_op jit(solution)/shard_map/ppermute | solution.py:169
  9.5 4.5 %collective-permute-start.4 = (bf16[16,4608]{1,0:T(8,128)(2,1)S(1)}, bf16[16,4608]{1,0:T(8,128)(2,1)S(1)}, u32[]{:S(2)}, u32[]{:S(2)}) collective-permute-start(bf16[16,4608]{1,0:T(8,128)(2,1)S(1)} %collective-permute-done), channel_id=1, source_target_pairs={{0,2},{1,3},{2,0},{3,1},{4,6},{5,7},{6,4},{7,5},{8,10},{9,11},{10,... | collective-permute-start | bytes 442376 | tf_op jit(solution)/shard_map/ppermute | solution.py:169
  14.0 1.5 %collective-permute-start.10 = (bf16[16,4608]{1,0:T(8,128)(2,1)S(1)}, bf16[16,4608]{1,0:T(8,128)(2,1)S(1)}, u32[]{:S(2)}, u32[]{:S(2)}) collective-permute-start(bf16[16,4608]{1,0:T(8,128)(2,1)S(1)} %collective-permute-done), channel_id=1, source_target_pairs={{0,16},{16,0},{1,17},{17,1},{2,18},{18,2},{3,19},{19,3},{4,20},{20... | collective-permute-start | bytes 442376 | tf_op jit(solution)/shard_map/ppermute | solution.py:172
  15.5 2.5 %collective-permute-start.2 = (bf16[16,4608]{1,0:T(8,128)(2,1)S(1)}, bf16[16,4608]{1,0:T(8,128)(2,1)S(1)}, u32[]{:S(2)}, u32[]{:S(2)}) collective-permute-start(bf16[16,4608]{1,0:T(8,128)(2,1)S(1)} %get-tuple-element.30), channel_id=1, source_target_pairs={{0,12},{1,13},{2,14},{3,15},{4,8},{5,9},{6,10},{7,11},{8,4},{9,5},... | collective-permute-start | bytes 442376 | tf_op jit(solution)/shard_map/ppermute | solution.py:169
  18.0 1.2 %collective-permute-start.6 = (bf16[16,4608]{1,0:T(8,128)(2,1)S(1)}, bf16[16,4608]{1,0:T(8,128)(2,1)S(1)}, u32[]{:S(2)}, u32[]{:S(2)}) collective-permute-start(bf16[16,4608]{1,0:T(8,128)(2,1)S(1)} %collective-permute-done.3), channel_id=1, source_target_pairs={{0,2},{1,3},{2,0},{3,1},{4,6},{5,7},{6,4},{7,5},{8,10},{9,11},{10,... | collective-permute-start | bytes 442376 | tf_op jit(solution)/shard_map/ppermute | solution.py:169
  19.2 1.6 %collective-permute-start.8 = (bf16[32,4608]{1,0:T(8,128)(2,1)S(1)}, bf16[32,4608]{1,0:T(8,128)(2,1)S(1)}, u32[]{:S(2)}, u32[]{:S(2)}) collective-permute-start(bf16[32,4608]{1,0:T(8,128)(2,1)S(1)} %pad_maximum_fusion), channel_id=1, source_target_pairs={{0,16},{16,0},{1,17},{17,1},{2,18},{18,2},{3,19},{19,3},{4,20},{20... | collective-permute-start | bytes 884744 | tf_op jit(solution)/shard_map/ppermute | solution.py:172
  20.9 1.6 %collective-permute-done.2 = bf16[16,4608]{1,0:T(8,128)(2,1)S(1)} collective-permute-done((bf16[16,4608]{1,0:T(8,128)(2,1)S(1)}, bf16[16,4608]{1,0:T(8,128)(2,1)S(1)}, u32[]{:S(2)}, u32[]{:S(2)}) %collective-permute-start.2) | collective-permute-done | bytes 147488 | tf_op jit(solution)/shard_map/ppermute | solution.py:169
  22.5 0.6 %collective-permute-done.6 = bf16[16,4608]{1,0:T(8,128)(2,1)S(1)} collective-permute-done((bf16[16,4608]{1,0:T(8,128)(2,1)S(1)}, bf16[16,4608]{1,0:T(8,128)(2,1)S(1)}, u32[]{:S(2)}, u32[]{:S(2)}) %collective-permute-start.6) | collective-permute-done | bytes 147488 | tf_op jit(solution)/shard_map/ppermute | solution.py:169
  23.2 0.8 %collective-permute-start.13 = (bf16[16,4608]{1,0:T(8,128)(2,1)S(1)}, bf16[16,4608]{1,0:T(8,128)(2,1)S(1)}, u32[]{:S(2)}, u32[]{:S(2)}) collective-permute-start(bf16[16,4608]{1,0:T(8,128)(2,1)S(1)} %collective-permute-done.2), channel_id=1, source_target_pairs={{0,16},{16,0},{1,17},{17,1},{2,18},{18,2},{3,19},{19,3},{4,20},{20... | collective-permute-start | bytes 442376 | tf_op jit(solution)/shard_map/ppermute | solution.py:172
  24.0 1.8 %collective-permute-start.7 = (bf16[16,4608]{1,0:T(8,128)(2,1)S(1)}, bf16[16,4608]{1,0:T(8,128)(2,1)S(1)}, u32[]{:S(2)}, u32[]{:S(2)}) collective-permute-start(bf16[16,4608]{1,0:T(8,128)(2,1)S(1)} %collective-permute-done.2), channel_id=1, source_target_pairs={{0,2},{1,3},{2,0},{3,1},{4,6},{5,7},{6,4},{7,5},{8,10},{9,11},{10,... | collective-permute-start | bytes 442376 | tf_op jit(solution)/shard_map/ppermute | solution.py:169
  25.8 3.1 %copy-done = bf16[128,28672]{1,0:T(8,128)(2,1)S(1)} copy-done((bf16[128,28672]{1,0:T(8,128)(2,1)S(1)}, bf16[128,28672]{1,0:T(8,128)(2,1)}, u32[]{:S(2)}) %copy-start) | copy-done | bytes 7340056
  28.9 0.7 %copy-done.5 = s32[64]{0:T(128)S(1)} copy-done((s32[64]{0:T(128)S(1)}, s32[64]{0:T(128)}, u32[]{:S(2)}) %copy-start.5) | copy-done | bytes 280
  29.5 0.8 %shard_map.56 = (f32[128,128]{1,0:T(8,128)S(1)}, f32[8,128]{1,0:T(8,128)S(1)}, f32[4,128,64]{2,1,0:T(8,128)S(1)}) custom-call(s32[64]{0:T(128)S(1)} %copy-done.5, bf16[128,28672]{1,0:T(8,128)(2,1)S(1)} %copy-done), custom_call_target="tpu_custom_call" | custom-call | flops 1 | bytes 1 | tf_op jit(solution)/shard_map/pallas_call | solution.py:248
  30.4 0.8 %collective-permute-start.14 = (bf16[16,4608]{1,0:T(8,128)(2,1)S(1)}, bf16[16,4608]{1,0:T(8,128)(2,1)S(1)}, u32[]{:S(2)}, u32[]{:S(2)}) collective-permute-start(bf16[16,4608]{1,0:T(8,128)(2,1)S(1)} %slice.3), channel_id=1, source_target_pairs={{0,2},{1,3},{2,0},{3,1},{4,6},{5,7},{6,4},{7,5},{8,10},{9,11},{10,... | collective-permute-start | bytes 442376 | tf_op jit(solution)/shard_map/ppermute | solution.py:169
  31.2 0.7 %collective-permute-start.9 = (bf16[16,4608]{1,0:T(8,128)(2,1)S(1)}, bf16[16,4608]{1,0:T(8,128)(2,1)S(1)}, u32[]{:S(2)}, u32[]{:S(2)}) collective-permute-start(bf16[16,4608]{1,0:T(8,128)(2,1)S(1)} %collective-permute-done.7), channel_id=1, source_target_pairs={{0,16},{16,0},{1,17},{17,1},{2,18},{18,2},{3,19},{19,3},{4,20},{20... | collective-permute-start | bytes 442376 | tf_op jit(solution)/shard_map/ppermute | solution.py:172
  32.6 2.4 %shard_map.58.norm_ref = f32[1,128]{1,0:T(1,128)S(1)} custom-call(f32[8,128]{1,0:T(8,128)S(1)} %get-tuple-element.45.member_ref, f32[128,128]{1,0:T(8,128)S(1)} %get-tuple-element.46.head_ref, bf16[128,8192]{1,0:T(8,128)(2,1)S(1)} %copy-done.2, bf16[128,28672]{1,0:T(8,128)(2,1)S(1)} %copy-done.1), custom_call_target="tpu_custom_call" | custom-call | flops 1 | bytes 1 | tf_op jit(solution)/shard_map/pallas_call | solution.py:263
  35.0 0.6 %collective-permute-done.14 = bf16[16,4608]{1,0:T(8,128)(2,1)S(1)} collective-permute-done((bf16[16,4608]{1,0:T(8,128)(2,1)S(1)}, bf16[16,4608]{1,0:T(8,128)(2,1)S(1)}, u32[]{:S(2)}, u32[]{:S(2)}) %collective-permute-start.14) | collective-permute-done | bytes 147488 | tf_op jit(solution)/shard_map/ppermute | solution.py:169
  35.6 1.6 %shard_map.57.held_ref = f32[2,128,64]{2,1,0:T(8,128)S(1)} custom-call(bf16[128,8192]{1,0:T(8,128)(2,1)S(1)} %copy-done.2, bf16[128,28672]{1,0:T(8,128)(2,1)S(1)} %copy-done.1, bf16[32,4608]{1,0:T(8,128)(2,1)S(1)} %get-tuple-element.29.refs_0_, bf16[32,4608]{1,0:T(8,128)(2,1)S(1)} %collective-permute-done.1.refs_1_, ...), custom_call_target="tpu_custom_call" | custom-call | flops 1 | bytes 1 | tf_op jit(solution)/shard_map/pallas_call | solution.py:274
  37.4 1.8 %collective-permute-done.15.refs_7_ = bf16[48,4608]{1,0:T(8,128)(2,1)S(1)} collective-permute-done((bf16[48,4608]{1,0:T(8,128)(2,1)S(1)}, bf16[48,4608]{1,0:T(8,128)(2,1)S(1)}, u32[]{:S(2)}, u32[]{:S(2)}) %collective-permute-start.15) | collective-permute-done | bytes 442400 | tf_op jit(solution)/shard_map/ppermute | solution.py:169
  39.1 2.3 %shard_map.59 = f32[2,4]{1,0:T(2,128)} custom-call(f32[1,128]{1,0:T(1,128)S(1)} %shard_map.58.norm_ref, f32[4,128,64]{2,1,0:T(8,128)S(1)} %get-tuple-element.48.spread_ref, f32[2,128,64]{2,1,0:T(8,128)S(1)} %shard_map.57.held_ref, bf16[128,8192]{1,0:T(8,128)(2,1)S(1)} %copy-done.2, bf16[128,28672]{1,0:T(8,128)(2,1)S(1)} %copy-done.1, ...), custom_call_target="tpu_custom_call" | custom-call | flops 1 | bytes 1 | tf_op jit(solution)/shard_map/pallas_call | solution.py:294
  (39 shorter events, 1.9 us)
Async XLA Ops:
  0.0 0.9 %copy-start.3 = (bf16[4,28672]{1,0:T(4,128)(2,1)S(1)}, bf16[4,28672]{1,0:T(4,128)(2,1)}, u32[]{:S(2)}) copy-start(bf16[4,28672]{1,0:T(4,128)(2,1)} %v_ref.1) | copy-start | bytes 688132
  0.9 0.8 %copy-start.4 = (bf16[4,8192]{1,0:T(4,128)(2,1)S(1)}, bf16[4,8192]{1,0:T(4,128)(2,1)}, u32[]{:S(2)}) copy-start(bf16[4,8192]{1,0:T(4,128)(2,1)} %u_ref.1) | copy-start | bytes 196612
  1.8 30.3 %copy-start.2 = (bf16[128,8192]{1,0:T(8,128)(2,1)S(1)}, bf16[128,8192]{1,0:T(8,128)(2,1)}, u32[]{:S(2)}) copy-start(bf16[128,8192]{1,0:T(8,128)(2,1)} %out_ref.5) | copy-start | bytes 6291460
  1.9 7.6 %collective-permute-start.1 = (bf16[32,4608]{1,0:T(8,128)(2,1)S(1)}, bf16[32,4608]{1,0:T(8,128)(2,1)S(1)}, u32[]{:S(2)}, u32[]{:S(2)}) collective-permute-start(bf16[32,4608]{1,0:T(8,128)(2,1)S(1)} %get-tuple-element.29.refs_0_), channel_id=1, source_target_pairs={{0,1},{1,0},{2,3},{3,2},{4,5},{5,4},{6,7},{7,6},{8,9},{9,8},{10,11... | collective-permute-start | bytes 884744 | tf_op jit(solution)/shard_map/ppermute | solution.py:169
  2.4 7.1 %collective-permute-start = (bf16[16,4608]{1,0:T(8,128)(2,1)S(1)}, bf16[16,4608]{1,0:T(8,128)(2,1)S(1)}, u32[]{:S(2)}, u32[]{:S(2)}) collective-permute-start(bf16[16,4608]{1,0:T(8,128)(2,1)S(1)} %get-tuple-element.30), channel_id=1, source_target_pairs={{0,4},{1,5},{2,6},{3,7},{4,0},{5,1},{6,2},{7,3},{8,12},{9,13},{10,... | collective-permute-start | bytes 442376 | tf_op jit(solution)/shard_map/ppermute | solution.py:169
  5.0 12.9 %collective-permute-start.5 = (bf16[32,4608]{1,0:T(8,128)(2,1)S(1)}, bf16[32,4608]{1,0:T(8,128)(2,1)S(1)}, u32[]{:S(2)}, u32[]{:S(2)}) collective-permute-start(bf16[32,4608]{1,0:T(8,128)(2,1)S(1)} %get-tuple-element.29.refs_0_), channel_id=1, source_target_pairs={{0,2},{1,3},{2,0},{3,1},{4,6},{5,7},{6,4},{7,5},{8,10},{9,11},{10,... | collective-permute-start | bytes 884744 | tf_op jit(solution)/shard_map/ppermute | solution.py:169
  6.5 11.4 %collective-permute-start.3 = (bf16[16,4608]{1,0:T(8,128)(2,1)S(1)}, bf16[16,4608]{1,0:T(8,128)(2,1)S(1)}, u32[]{:S(2)}, u32[]{:S(2)}) collective-permute-start(bf16[16,4608]{1,0:T(8,128)(2,1)S(1)} %get-tuple-element.30), channel_id=1, source_target_pairs={{0,8},{1,9},{2,10},{3,11},{4,12},{5,13},{6,14},{7,15},{8,0},{9,1},... | collective-permute-start | bytes 442376 | tf_op jit(solution)/shard_map/ppermute | solution.py:169
  9.5 8.5 %collective-permute-start.4 = (bf16[16,4608]{1,0:T(8,128)(2,1)S(1)}, bf16[16,4608]{1,0:T(8,128)(2,1)S(1)}, u32[]{:S(2)}, u32[]{:S(2)}) collective-permute-start(bf16[16,4608]{1,0:T(8,128)(2,1)S(1)} %collective-permute-done), channel_id=1, source_target_pairs={{0,2},{1,3},{2,0},{3,1},{4,6},{5,7},{6,4},{7,5},{8,10},{9,11},{10,... | collective-permute-start | bytes 442376 | tf_op jit(solution)/shard_map/ppermute | solution.py:169
  14.0 6.8 %collective-permute-start.10 = (bf16[16,4608]{1,0:T(8,128)(2,1)S(1)}, bf16[16,4608]{1,0:T(8,128)(2,1)S(1)}, u32[]{:S(2)}, u32[]{:S(2)}) collective-permute-start(bf16[16,4608]{1,0:T(8,128)(2,1)S(1)} %collective-permute-done), channel_id=1, source_target_pairs={{0,16},{16,0},{1,17},{17,1},{2,18},{18,2},{3,19},{19,3},{4,20},{20... | collective-permute-start | bytes 442376 | tf_op jit(solution)/shard_map/ppermute | solution.py:172
  15.5 7.0 %collective-permute-start.2 = (bf16[16,4608]{1,0:T(8,128)(2,1)S(1)}, bf16[16,4608]{1,0:T(8,128)(2,1)S(1)}, u32[]{:S(2)}, u32[]{:S(2)}) collective-permute-start(bf16[16,4608]{1,0:T(8,128)(2,1)S(1)} %get-tuple-element.30), channel_id=1, source_target_pairs={{0,12},{1,13},{2,14},{3,15},{4,8},{5,9},{6,10},{7,11},{8,4},{9,5},... | collective-permute-start | bytes 442376 | tf_op jit(solution)/shard_map/ppermute | solution.py:169
  18.0 5.2 %collective-permute-start.6 = (bf16[16,4608]{1,0:T(8,128)(2,1)S(1)}, bf16[16,4608]{1,0:T(8,128)(2,1)S(1)}, u32[]{:S(2)}, u32[]{:S(2)}) collective-permute-start(bf16[16,4608]{1,0:T(8,128)(2,1)S(1)} %collective-permute-done.3), channel_id=1, source_target_pairs={{0,2},{1,3},{2,0},{3,1},{4,6},{5,7},{6,4},{7,5},{8,10},{9,11},{10,... | collective-permute-start | bytes 442376 | tf_op jit(solution)/shard_map/ppermute | solution.py:169
  19.2 11.2 %collective-permute-start.8 = (bf16[32,4608]{1,0:T(8,128)(2,1)S(1)}, bf16[32,4608]{1,0:T(8,128)(2,1)S(1)}, u32[]{:S(2)}, u32[]{:S(2)}) collective-permute-start(bf16[32,4608]{1,0:T(8,128)(2,1)S(1)} %pad_maximum_fusion), channel_id=1, source_target_pairs={{0,16},{16,0},{1,17},{17,1},{2,18},{18,2},{3,19},{19,3},{4,20},{20... | collective-permute-start | bytes 884744 | tf_op jit(solution)/shard_map/ppermute | solution.py:172
  20.8 14.8 %collective-permute-start.11 = (bf16[96,4608]{1,0:T(8,128)(2,1)S(1)}, bf16[96,4608]{1,0:T(8,128)(2,1)S(1)}, u32[]{:S(2)}, u32[]{:S(2)}) collective-permute-start(bf16[96,4608]{1,0:T(8,128)(2,1)S(1)} %constant_dynamic-update-slice_fusion.refs_2_), channel_id=1, source_target_pairs={{0,1},{1,0},{2,3},{3,2},{4,5},{5,4},{6,7},{7,6},{8,9},{9,8},{10,11... | collective-permute-start | bytes 2654216 | tf_op jit(solution)/shard_map/ppermute | solution.py:169
  23.2 8.8 %collective-permute-start.13 = (bf16[16,4608]{1,0:T(8,128)(2,1)S(1)}, bf16[16,4608]{1,0:T(8,128)(2,1)S(1)}, u32[]{:S(2)}, u32[]{:S(2)}) collective-permute-start(bf16[16,4608]{1,0:T(8,128)(2,1)S(1)} %collective-permute-done.2), channel_id=1, source_target_pairs={{0,16},{16,0},{1,17},{17,1},{2,18},{18,2},{3,19},{19,3},{4,20},{20... | collective-permute-start | bytes 442376 | tf_op jit(solution)/shard_map/ppermute | solution.py:172
  24.0 6.4 %collective-permute-start.7 = (bf16[16,4608]{1,0:T(8,128)(2,1)S(1)}, bf16[16,4608]{1,0:T(8,128)(2,1)S(1)}, u32[]{:S(2)}, u32[]{:S(2)}) collective-permute-start(bf16[16,4608]{1,0:T(8,128)(2,1)S(1)} %collective-permute-done.2), channel_id=1, source_target_pairs={{0,2},{1,3},{2,0},{3,1},{4,6},{5,7},{6,4},{7,5},{8,10},{9,11},{10,... | collective-permute-start | bytes 442376 | tf_op jit(solution)/shard_map/ppermute | solution.py:169
  25.8 3.1 %copy-start = (bf16[128,28672]{1,0:T(8,128)(2,1)S(1)}, bf16[128,28672]{1,0:T(8,128)(2,1)}, u32[]{:S(2)}) copy-start(bf16[128,28672]{1,0:T(8,128)(2,1)} %in_ref.7) | copy-start | bytes 22020100
  28.9 0.7 %copy-start.5 = (s32[64]{0:T(128)S(1)}, s32[64]{0:T(128)}, u32[]{:S(2)}) copy-start(s32[64]{0:T(128)} %lengths_hbm) | copy-start | bytes 772
  29.5 3.1 %copy-start.1 = (bf16[128,28672]{1,0:T(8,128)(2,1)S(1)}, bf16[128,28672]{1,0:T(8,128)(2,1)}, u32[]{:S(2)}) copy-start(bf16[128,28672]{1,0:T(8,128)(2,1)} %in_ref.7) | copy-start | bytes 22020100
  30.4 5.2 %collective-permute-start.14 = (bf16[16,4608]{1,0:T(8,128)(2,1)S(1)}, bf16[16,4608]{1,0:T(8,128)(2,1)S(1)}, u32[]{:S(2)}, u32[]{:S(2)}) collective-permute-start(bf16[16,4608]{1,0:T(8,128)(2,1)S(1)} %slice.3), channel_id=1, source_target_pairs={{0,2},{1,3},{2,0},{3,1},{4,6},{5,7},{6,4},{7,5},{8,10},{9,11},{10,... | collective-permute-start | bytes 442376 | tf_op jit(solution)/shard_map/ppermute | solution.py:169
  31.2 6.1 %collective-permute-start.9 = (bf16[16,4608]{1,0:T(8,128)(2,1)S(1)}, bf16[16,4608]{1,0:T(8,128)(2,1)S(1)}, u32[]{:S(2)}, u32[]{:S(2)}) collective-permute-start(bf16[16,4608]{1,0:T(8,128)(2,1)S(1)} %collective-permute-done.7), channel_id=1, source_target_pairs={{0,16},{16,0},{1,17},{17,1},{2,18},{18,2},{3,19},{19,3},{4,20},{20... | collective-permute-start | bytes 442376 | tf_op jit(solution)/shard_map/ppermute | solution.py:172
  31.9 3.7 %collective-permute-start.12 = (bf16[80,4608]{1,0:T(8,128)(2,1)S(1)}, bf16[80,4608]{1,0:T(8,128)(2,1)S(1)}, u32[]{:S(2)}, u32[]{:S(2)}) collective-permute-start(bf16[80,4608]{1,0:T(8,128)(2,1)S(1)} %constant_dynamic-update-slice_fusion.5.refs_4_), channel_id=1, source_target_pairs={{0,1},{1,0},{2,3},{3,2},{4,5},{5,4},{6,7},{7,6},{8,9},{9,8},{10,11... | collective-permute-start | bytes 2211848 | tf_op jit(solution)/shard_map/ppermute | solution.py:169
  37.3 1.9 %collective-permute-start.15 = (bf16[48,4608]{1,0:T(8,128)(2,1)S(1)}, bf16[48,4608]{1,0:T(8,128)(2,1)S(1)}, u32[]{:S(2)}, u32[]{:S(2)}) collective-permute-start(bf16[48,4608]{1,0:T(8,128)(2,1)S(1)} %constant_dynamic-update-slice_fusion.9.refs_6_), channel_id=1, source_target_pairs={{0,1},{1,0},{2,3},{3,2},{4,5},{5,4},{6,7},{7,6},{8,9},{9,8},{10,11... | collective-permute-start | bytes 1327112 | tf_op jit(solution)/shard_map/ppermute | solution.py:169

commit v9 on v8

--- a/solution.py
+++ b/solution.py
@@ -48,11 +48,9 @@
             place += wide
 
 
-def head_kernel(seq_dev, lengths_hbm, in_ref, gram_ref, member_ref, spread_ref, lengths_ref, sem):
+def member_kernel(seq_dev, lengths_hbm, after_ref, member_ref, spread_ref, lengths_ref, sem):
     copy = pltpu.make_async_copy(lengths_hbm, lengths_ref, sem)
     copy.start()
-    head = in_ref[:, :HEAD]
-    gram_ref[...] = inner_rows(head, head)
     copy.wait()
     seqs, tok_cap = member_ref.shape
     which = lax.broadcasted_iota(jnp.int32, (seqs, tok_cap), 0)
@@ -67,6 +65,11 @@
         spread_ref[k] = ((rows >= low) & (rows < high)).astype(jnp.float32)
         low = high
     member_ref[...] = member
+
+
+def head_kernel(member_ref, in_ref, gram_ref):
+    head = in_ref[:, :HEAD]
+    gram_ref[...] = inner_rows(head, head)
 
 
 def norm_kernel(member_ref, head_ref, out_ref, in_ref, norm_ref):
@@ -164,7 +167,7 @@
         score_ref[q : q + 1, :] = row[:, : score_ref.shape[1]]
 
 
-def gather_blocks(both, own, devices, lengths, head_step, norm_step, partial_step):
+def gather_blocks(both, own, devices, lengths, member_step, head_step, norm_step, partial_step):
     def swap(value, mask):
         return lax.ppermute(value, "seq", [(i, i ^ mask) for i in range(devices)])
 
@@ -178,15 +181,14 @@
     x1, y1, z3 = across(z1), swap(z1, 2), swap(own, 12)
     z2, y1, y0, lengths = gate(z2, y1, y0, lengths)
     x_near, y2 = across(stack(z2, y1)), swap(z2, 2)
-    z3, y2, lengths = gate(z3, y2, lengths)
-    head, member, spread = head_step(lengths)
+    member, spread = member_step(lengths, x1)
+    z3, y2, member = gate(z3, y2, member)
+    head = head_step(member)
     x3, y3 = across(z3), swap(z3, 2)
     early = stack(y0, z1, y1, z2, x1)
     early_core = swap(early, 1)
-    x_near, head = gate(x_near, head)
-    yx2 = swap(x_near[:PACK], 2)
-    y3, member, head = gate(y3, member, head)
-    x_last = across(y3)
+    y3, x_near, head, member = gate(y3, x_near, head, member)
+    x_last, yx2 = across(y3), swap(x_near[:PACK], 2)
     norms = norm_step(member, head)
     middle = stack(y2, z3, y3, x_near)
     middle_core = swap(middle, 1)
@@ -244,22 +246,31 @@
     frows = devices * rank_rows
     tiny = pl.CostEstimate(flops=1, bytes_accessed=1, transcendentals=0)
 
-    def head_step(lengths):
+    def member_step(lengths, earlier):
         return pl.pallas_call(
-            functools.partial(head_kernel, seq_dev),
+            functools.partial(member_kernel, seq_dev),
             out_shape=[
-                jax.ShapeDtypeStruct((tok_cap, tok_cap), jnp.float32),
                 jax.ShapeDtypeStruct((seqs, tok_cap), jnp.float32),
                 jax.ShapeDtypeStruct((seq_dev, tok_cap, frows), jnp.float32),
             ],
-            in_specs=[hbm, vmem],
-            out_specs=[vmem] * 3,
+            in_specs=[hbm] + [vmem] * 1,
+            out_specs=[vmem] * 2,
             scratch_shapes=[pltpu.SMEM(lengths.shape, lengths.dtype), pltpu.SemaphoreType.DMA],
             compiler_params=score_params,
             cost_estimate=tiny,
-        )(lengths, layer_inputs)
-
-    def norm_step(member, head):
+        )(lengths, earlier)
+
+    def head_step(member):
+        return pl.pallas_call(
+            head_kernel,
+            out_shape=jax.ShapeDtypeStruct((tok_cap, tok_cap), jnp.float32),
+            in_specs=[vmem] * 2,
+            out_specs=vmem,
+            compiler_params=score_params,
+            cost_estimate=tiny,
+        )(member, layer_inputs)
+
+    def norm_step(*known):
         return pl.pallas_call(
             norm_kernel,
             out_shape=jax.ShapeDtypeStruct((1, tok_cap), jnp.float32),
@@ -267,7 +278,7 @@
             out_specs=vmem,
             compiler_params=score_params,
             cost_estimate=tiny,
-        )(member, head, out_grads, layer_inputs)
+        )(*known, out_grads, layer_inputs)
 
     def partial_step(blocks):
         arrays, places = refs_of(blocks)
@@ -282,11 +293,11 @@
 
     if paired:
         other, norms, spread, partial = gather_blocks(
-            packed[0], packed[1], devices, seq_lengths, head_step, norm_step, partial_step
+            packed[0], packed[1], devices, seq_lengths, member_step, head_step, norm_step, partial_step
         )
     else:
-        head, member, spread = head_step(seq_lengths)
-        norms = norm_step(member, head)
+        member, spread = member_step(seq_lengths, packed[0])
+        norms = norm_step(member, head_step(member))
         gathered = lax.all_gather(packed[0], "seq", axis=0, tiled=True)
         partial = partial_step([(gathered, 2 * PACK * b) for b in range(devices)])
         other = [(gathered, 2 * PACK * b + PACK) for b in range(devices)]

time: 41.7 us -> 41 us (0.983)
  waiting for transfers between devices: 5 us -> 3.93 us
  local copies, waits for them, and re-layouts: 6.26 us -> 5.69 us
  Pallas kernels: 7.14 us -> 7.65 us
    ppermute x12, waiting for transfers between devices: 4.99 us -> 3.92 us  [swap(): return lax.ppermute(value, 'seq', [(i, i ^ mask) for i in range(devices)])]
    unnamed x21 -> x23, local copies, waits for them, and re-layouts: 6.2 us -> 5.63 us
    ppermute x12, starting transfers between devices: 18.3 us -> 18.8 us  [swap(): return lax.ppermute(value, 'seq', [(i, i ^ mask) for i in range(devices)])]
    pallas_call x1 -> x2, Pallas kernels: 0.77 us -> 1.3 us  [the longest x1 0.7 us: head_step(): pl.pallas_call(head_kernel, out_shape=jax.ShapeDtypeStruct((tok_cap, tok_...]
  transfers between devices with their start and end apart: 16 -> 16, of which waited for: 5 -> 5; matrix products, arithmetic and copies ran while one was open for 0% -> 0% of each run, Pallas kernels for 11% -> 13%
where the time goes in v9:
time: 41 us; the launch traced here: 40.7 us
  starting transfers between devices  23.2 us (57%)
  Pallas kernels  7.65 us (19%)
  local copies, waits for them, and re-layouts  5.69 us (14%)
  waiting for transfers between devices  3.93 us (10%)
    ppermute x12, starting transfers between devices, swap(): return lax.ppermute(value, 'seq', [(i, i ^ mask) for i in range(devices)])  18.8 us
    unnamed x23, local copies, waits for them, and re-layouts  5.63 us
    ppermute x4, starting transfers between devices, across(): return lax.ppermute(value, 'grp', [(0, 1), (1, 0)])  4.38 us
    ppermute x12, waiting for transfers between devices, swap(): return lax.ppermute(value, 'seq', [(i, i ^ mask) for i in range(devices)])  3.92 us
    pallas_call x1, Pallas kernels, norm_step(): pl.pallas_call(norm_kernel, out_shape=jax.ShapeDtypeStruct((1, tok_cap),...  2.36 us
    pallas_call x1, Pallas kernels, local(): pl.pallas_call(functools.partial(score_kernel, rank_rows, paired, places)...  2.32 us
    pallas_call x1, Pallas kernels, partial_step(): pl.pallas_call(functools.partial(partial_kernel, rank_rows, paired, place...  1.61 us
  transfers between devices with their start and end apart: 16, of which 5 were waited for; matrix products, arithmetic and copies ran while one was open for 0% of the time, Pallas kernels for 13%

profile of v9, /device:TPU:0, one launch (start us, length us, event | category | flops | bytes accessed | tf_op | source)
XLA Modules:
  0.0 40.7 jit_solution(13881473562790784505)
XLA Ops:
  0.0 0.9 %copy-done.2 = bf16[4,28672]{1,0:T(4,128)(2,1)S(1)} copy-done((bf16[4,28672]{1,0:T(4,128)(2,1)S(1)}, bf16[4,28672]{1,0:T(4,128)(2,1)}, u32[]{:S(2)}) %copy-start.2) | copy-done | bytes 229400
  0.9 0.8 %copy-done.3 = bf16[4,8192]{1,0:T(4,128)(2,1)S(1)} copy-done((bf16[4,8192]{1,0:T(4,128)(2,1)S(1)}, bf16[4,8192]{1,0:T(4,128)(2,1)}, u32[]{:S(2)}) %copy-start.3) | copy-done | bytes 65560
  2.4 2.6 %collective-permute-start = (bf16[16,4608]{1,0:T(8,128)(2,1)S(1)}, bf16[16,4608]{1,0:T(8,128)(2,1)S(1)}, u32[]{:S(2)}, u32[]{:S(2)}) collective-permute-start(bf16[16,4608]{1,0:T(8,128)(2,1)S(1)} %get-tuple-element.28), channel_id=1, source_target_pairs={{0,4},{1,5},{2,6},{3,7},{4,0},{5,1},{6,2},{7,3},{8,12},{9,13},{10,... | collective-permute-start | bytes 442376 | tf_op jit(solution)/shard_map/ppermute | solution.py:172
  5.0 1.5 %collective-permute-start.5 = (bf16[32,4608]{1,0:T(8,128)(2,1)S(1)}, bf16[32,4608]{1,0:T(8,128)(2,1)S(1)}, u32[]{:S(2)}, u32[]{:S(2)}) collective-permute-start(bf16[32,4608]{1,0:T(8,128)(2,1)S(1)} %get-tuple-element.27.refs_0_), channel_id=1, source_target_pairs={{0,2},{1,3},{2,0},{3,1},{4,6},{5,7},{6,4},{7,5},{8,10},{9,11},{10,... | collective-permute-start | bytes 884744 | tf_op jit(solution)/shard_map/ppermute | solution.py:172
  6.5 2.6 %collective-permute-start.3 = (bf16[16,4608]{1,0:T(8,128)(2,1)S(1)}, bf16[16,4608]{1,0:T(8,128)(2,1)S(1)}, u32[]{:S(2)}, u32[]{:S(2)}) collective-permute-start(bf16[16,4608]{1,0:T(8,128)(2,1)S(1)} %get-tuple-element.28), channel_id=1, source_target_pairs={{0,8},{1,9},{2,10},{3,11},{4,12},{5,13},{6,14},{7,15},{8,0},{9,1},... | collective-permute-start | bytes 442376 | tf_op jit(solution)/shard_map/ppermute | solution.py:172
  9.5 4.5 %collective-permute-start.4 = (bf16[16,4608]{1,0:T(8,128)(2,1)S(1)}, bf16[16,4608]{1,0:T(8,128)(2,1)S(1)}, u32[]{:S(2)}, u32[]{:S(2)}) collective-permute-start(bf16[16,4608]{1,0:T(8,128)(2,1)S(1)} %collective-permute-done), channel_id=1, source_target_pairs={{0,2},{1,3},{2,0},{3,1},{4,6},{5,7},{6,4},{7,5},{8,10},{9,11},{10,... | collective-permute-start | bytes 442376 | tf_op jit(solution)/shard_map/ppermute | solution.py:172
  14.0 1.5 %collective-permute-start.7 = (bf16[16,4608]{1,0:T(8,128)(2,1)S(1)}, bf16[16,4608]{1,0:T(8,128)(2,1)S(1)}, u32[]{:S(2)}, u32[]{:S(2)}) collective-permute-start(bf16[16,4608]{1,0:T(8,128)(2,1)S(1)} %collective-permute-done), channel_id=1, source_target_pairs={{0,16},{16,0},{1,17},{17,1},{2,18},{18,2},{3,19},{19,3},{4,20},{20... | collective-permute-start | bytes 442376 | tf_op jit(solution)/shard_map/ppermute | solution.py:175
  15.5 2.5 %collective-permute-start.2 = (bf16[16,4608]{1,0:T(8,128)(2,1)S(1)}, bf16[16,4608]{1,0:T(8,128)(2,1)S(1)}, u32[]{:S(2)}, u32[]{:S(2)}) collective-permute-start(bf16[16,4608]{1,0:T(8,128)(2,1)S(1)} %get-tuple-element.28), channel_id=1, source_target_pairs={{0,12},{1,13},{2,14},{3,15},{4,8},{5,9},{6,10},{7,11},{8,4},{9,5},... | collective-permute-start | bytes 442376 | tf_op jit(solution)/shard_map/ppermute | solution.py:172
  18.0 1.2 %collective-permute-start.6 = (bf16[16,4608]{1,0:T(8,128)(2,1)S(1)}, bf16[16,4608]{1,0:T(8,128)(2,1)S(1)}, u32[]{:S(2)}, u32[]{:S(2)}) collective-permute-start(bf16[16,4608]{1,0:T(8,128)(2,1)S(1)} %collective-permute-done.3), channel_id=1, source_target_pairs={{0,2},{1,3},{2,0},{3,1},{4,6},{5,7},{6,4},{7,5},{8,10},{9,11},{10,... | collective-permute-start | bytes 442376 | tf_op jit(solution)/shard_map/ppermute | solution.py:172
  19.2 1.6 %collective-permute-start.9 = (bf16[32,4608]{1,0:T(8,128)(2,1)S(1)}, bf16[32,4608]{1,0:T(8,128)(2,1)S(1)}, u32[]{:S(2)}, u32[]{:S(2)}) collective-permute-start(bf16[32,4608]{1,0:T(8,128)(2,1)S(1)} %pad_maximum_fusion), channel_id=1, source_target_pairs={{0,16},{16,0},{1,17},{17,1},{2,18},{18,2},{3,19},{19,3},{4,20},{20... | collective-permute-start | bytes 884744 | tf_op jit(solution)/shard_map/ppermute | solution.py:175
  20.9 0.6 %copy-done.4 = s32[64]{0:T(128)S(1)} copy-done((s32[64]{0:T(128)S(1)}, s32[64]{0:T(128)}, u32[]{:S(2)}) %copy-start.4) | copy-done | bytes 280
  21.6 0.6 %shard_map.56 = (f32[8,128]{1,0:T(8,128)S(1)}, f32[4,128,64]{2,1,0:T(8,128)S(1)}) custom-call(s32[64]{0:T(128)S(1)} %copy-done.4, bf16[16,4608]{1,0:T(8,128)(2,1)S(1)} %collective-permute-done.7.after_ref), custom_call_target="tpu_custom_call" | custom-call | flops 1 | bytes 1 | tf_op jit(solution)/shard_map/pallas_call | solution.py:250
  22.5 0.6 %collective-permute-done.6 = bf16[16,4608]{1,0:T(8,128)(2,1)S(1)} collective-permute-done((bf16[16,4608]{1,0:T(8,128)(2,1)S(1)}, bf16[16,4608]{1,0:T(8,128)(2,1)S(1)}, u32[]{:S(2)}, u32[]{:S(2)}) %collective-permute-start.6) | collective-permute-done | bytes 147488 | tf_op jit(solution)/shard_map/ppermute | solution.py:172
  23.2 0.8 %collective-permute-start.13 = (bf16[16,4608]{1,0:T(8,128)(2,1)S(1)}, bf16[16,4608]{1,0:T(8,128)(2,1)S(1)}, u32[]{:S(2)}, u32[]{:S(2)}) collective-permute-start(bf16[16,4608]{1,0:T(8,128)(2,1)S(1)} %collective-permute-done.2), channel_id=1, source_target_pairs={{0,16},{16,0},{1,17},{17,1},{2,18},{18,2},{3,19},{19,3},{4,20},{20... | collective-permute-start | bytes 442376 | tf_op jit(solution)/shard_map/ppermute | solution.py:175
  24.0 1.8 %collective-permute-start.8 = (bf16[16,4608]{1,0:T(8,128)(2,1)S(1)}, bf16[16,4608]{1,0:T(8,128)(2,1)S(1)}, u32[]{:S(2)}, u32[]{:S(2)}) collective-permute-start(bf16[16,4608]{1,0:T(8,128)(2,1)S(1)} %collective-permute-done.2), channel_id=1, source_target_pairs={{0,2},{1,3},{2,0},{3,1},{4,6},{5,7},{6,4},{7,5},{8,10},{9,11},{10,... | collective-permute-start | bytes 442376 | tf_op jit(solution)/shard_map/ppermute | solution.py:172
  25.8 3.1 %copy-done = bf16[128,28672]{1,0:T(8,128)(2,1)S(1)} copy-done((bf16[128,28672]{1,0:T(8,128)(2,1)S(1)}, bf16[128,28672]{1,0:T(8,128)(2,1)}, u32[]{:S(2)}) %copy-start) | copy-done | bytes 7340056
  28.9 0.7 %shard_map.57.head_ref = f32[128,128]{1,0:T(8,128)S(1)} custom-call(f32[8,128]{1,0:T(8,128)S(1)} %get-tuple-element.41.member_ref, bf16[128,28672]{1,0:T(8,128)(2,1)S(1)} %copy-done), custom_call_target="tpu_custom_call" | custom-call | flops 1 | bytes 1 | tf_op jit(solution)/shard_map/pallas_call | solution.py:264
  29.6 1.4 %collective-permute-start.14 = (bf16[16,4608]{1,0:T(8,128)(2,1)S(1)}, bf16[16,4608]{1,0:T(8,128)(2,1)S(1)}, u32[]{:S(2)}, u32[]{:S(2)}) collective-permute-start(bf16[16,4608]{1,0:T(8,128)(2,1)S(1)} %slice.3), channel_id=1, source_target_pairs={{0,2},{1,3},{2,0},{3,1},{4,6},{5,7},{6,4},{7,5},{8,10},{9,11},{10,... | collective-permute-start | bytes 442376 | tf_op jit(solution)/shard_map/ppermute | solution.py:172
  31.0 0.5 %collective-permute-start.10 = (bf16[16,4608]{1,0:T(8,128)(2,1)S(1)}, bf16[16,4608]{1,0:T(8,128)(2,1)S(1)}, u32[]{:S(2)}, u32[]{:S(2)}) collective-permute-start(bf16[16,4608]{1,0:T(8,128)(2,1)S(1)} %collective-permute-done.8), channel_id=1, source_target_pairs={{0,16},{16,0},{1,17},{17,1},{2,18},{18,2},{3,19},{19,3},{4,20},{20... | collective-permute-start | bytes 442376 | tf_op jit(solution)/shard_map/ppermute | solution.py:175
  31.7 2.4 %shard_map.59.norm_ref = f32[1,128]{1,0:T(1,128)S(1)} custom-call(f32[8,128]{1,0:T(8,128)S(1)} %get-tuple-element.41.member_ref, f32[128,128]{1,0:T(8,128)S(1)} %shard_map.57.head_ref, bf16[128,8192]{1,0:T(8,128)(2,1)S(1)} %copy-done.1, bf16[128,28672]{1,0:T(8,128)(2,1)S(1)} %copy-done), custom_call_target="tpu_custom_call" | custom-call | flops 1 | bytes 1 | tf_op jit(solution)/shard_map/pallas_call | solution.py:274
  34.1 0.8 %collective-permute-done.14 = bf16[16,4608]{1,0:T(8,128)(2,1)S(1)} collective-permute-done((bf16[16,4608]{1,0:T(8,128)(2,1)S(1)}, bf16[16,4608]{1,0:T(8,128)(2,1)S(1)}, u32[]{:S(2)}, u32[]{:S(2)}) %collective-permute-start.14) | collective-permute-done | bytes 147488 | tf_op jit(solution)/shard_map/ppermute | solution.py:172
  34.9 1.6 %shard_map.58.held_ref = f32[2,128,64]{2,1,0:T(8,128)S(1)} custom-call(bf16[128,8192]{1,0:T(8,128)(2,1)S(1)} %copy-done.1, bf16[128,28672]{1,0:T(8,128)(2,1)S(1)} %bitcast.1, bf16[32,4608]{1,0:T(8,128)(2,1)S(1)} %get-tuple-element.27.refs_0_, bf16[32,4608]{1,0:T(8,128)(2,1)S(1)} %collective-permute-done.1.refs_1_, ...), custom_call_target="tpu_custom_call" | custom-call | flops 1 | bytes 1 | tf_op jit(solution)/shard_map/pallas_call | solution.py:285
  36.6 1.8 %collective-permute-done.15.refs_7_ = bf16[48,4608]{1,0:T(8,128)(2,1)S(1)} collective-permute-done((bf16[48,4608]{1,0:T(8,128)(2,1)S(1)}, bf16[48,4608]{1,0:T(8,128)(2,1)S(1)}, u32[]{:S(2)}, u32[]{:S(2)}) %collective-permute-start.15) | collective-permute-done | bytes 442400 | tf_op jit(solution)/shard_map/ppermute | solution.py:172
  38.4 2.3 %shard_map.60 = f32[2,4]{1,0:T(2,128)} custom-call(f32[1,128]{1,0:T(1,128)S(1)} %shard_map.59.norm_ref, f32[4,128,64]{2,1,0:T(8,128)S(1)} %get-tuple-element.44.spread_ref, f32[2,128,64]{2,1,0:T(8,128)S(1)} %shard_map.58.held_ref, bf16[128,8192]{1,0:T(8,128)(2,1)S(1)} %copy-done.1, bf16[128,28672]{1,0:T(8,128)(2,1)S(1)} %bitcast.1, ...), custom_call_target="tpu_custom_call" | custom-call | flops 1 | bytes 1 | tf_op jit(solution)/shard_map/pallas_call | solution.py:305
  (43 shorter events, 1.7 us)
Async XLA Ops:
  0.0 0.9 %copy-start.2 = (bf16[4,28672]{1,0:T(4,128)(2,1)S(1)}, bf16[4,28672]{1,0:T(4,128)(2,1)}, u32[]{:S(2)}) copy-start(bf16[4,28672]{1,0:T(4,128)(2,1)} %v_ref.1) | copy-start | bytes 688132
  0.9 0.8 %copy-start.3 = (bf16[4,8192]{1,0:T(4,128)(2,1)S(1)}, bf16[4,8192]{1,0:T(4,128)(2,1)}, u32[]{:S(2)}) copy-start(bf16[4,8192]{1,0:T(4,128)(2,1)} %u_ref.1) | copy-start | bytes 196612
  1.8 29.9 %copy-start.1 = (bf16[128,8192]{1,0:T(8,128)(2,1)S(1)}, bf16[128,8192]{1,0:T(8,128)(2,1)}, u32[]{:S(2)}) copy-start(bf16[128,8192]{1,0:T(8,128)(2,1)} %out_ref.5) | copy-start | bytes 6291460
  1.9 7.6 %collective-permute-start.1 = (bf16[32,4608]{1,0:T(8,128)(2,1)S(1)}, bf16[32,4608]{1,0:T(8,128)(2,1)S(1)}, u32[]{:S(2)}, u32[]{:S(2)}) collective-permute-start(bf16[32,4608]{1,0:T(8,128)(2,1)S(1)} %get-tuple-element.27.refs_0_), channel_id=1, source_target_pairs={{0,1},{1,0},{2,3},{3,2},{4,5},{5,4},{6,7},{7,6},{8,9},{9,8},{10,11... | collective-permute-start | bytes 884744 | tf_op jit(solution)/shard_map/ppermute | solution.py:172
  2.4 7.1 %collective-permute-start = (bf16[16,4608]{1,0:T(8,128)(2,1)S(1)}, bf16[16,4608]{1,0:T(8,128)(2,1)S(1)}, u32[]{:S(2)}, u32[]{:S(2)}) collective-permute-start(bf16[16,4608]{1,0:T(8,128)(2,1)S(1)} %get-tuple-element.28), channel_id=1, source_target_pairs={{0,4},{1,5},{2,6},{3,7},{4,0},{5,1},{6,2},{7,3},{8,12},{9,13},{10,... | collective-permute-start | bytes 442376 | tf_op jit(solution)/shard_map/ppermute | solution.py:172
  5.0 12.9 %collective-permute-start.5 = (bf16[32,4608]{1,0:T(8,128)(2,1)S(1)}, bf16[32,4608]{1,0:T(8,128)(2,1)S(1)}, u32[]{:S(2)}, u32[]{:S(2)}) collective-permute-start(bf16[32,4608]{1,0:T(8,128)(2,1)S(1)} %get-tuple-element.27.refs_0_), channel_id=1, source_target_pairs={{0,2},{1,3},{2,0},{3,1},{4,6},{5,7},{6,4},{7,5},{8,10},{9,11},{10,... | collective-permute-start | bytes 884744 | tf_op jit(solution)/shard_map/ppermute | solution.py:172
  6.5 11.4 %collective-permute-start.3 = (bf16[16,4608]{1,0:T(8,128)(2,1)S(1)}, bf16[16,4608]{1,0:T(8,128)(2,1)S(1)}, u32[]{:S(2)}, u32[]{:S(2)}) collective-permute-start(bf16[16,4608]{1,0:T(8,128)(2,1)S(1)} %get-tuple-element.28), channel_id=1, source_target_pairs={{0,8},{1,9},{2,10},{3,11},{4,12},{5,13},{6,14},{7,15},{8,0},{9,1},... | collective-permute-start | bytes 442376 | tf_op jit(solution)/shard_map/ppermute | solution.py:172
  9.5 8.5 %collective-permute-start.4 = (bf16[16,4608]{1,0:T(8,128)(2,1)S(1)}, bf16[16,4608]{1,0:T(8,128)(2,1)S(1)}, u32[]{:S(2)}, u32[]{:S(2)}) collective-permute-start(bf16[16,4608]{1,0:T(8,128)(2,1)S(1)} %collective-permute-done), channel_id=1, source_target_pairs={{0,2},{1,3},{2,0},{3,1},{4,6},{5,7},{6,4},{7,5},{8,10},{9,11},{10,... | collective-permute-start | bytes 442376 | tf_op jit(solution)/shard_map/ppermute | solution.py:172
  14.0 6.8 %collective-permute-start.7 = (bf16[16,4608]{1,0:T(8,128)(2,1)S(1)}, bf16[16,4608]{1,0:T(8,128)(2,1)S(1)}, u32[]{:S(2)}, u32[]{:S(2)}) collective-permute-start(bf16[16,4608]{1,0:T(8,128)(2,1)S(1)} %collective-permute-done), channel_id=1, source_target_pairs={{0,16},{16,0},{1,17},{17,1},{2,18},{18,2},{3,19},{19,3},{4,20},{20... | collective-permute-start | bytes 442376 | tf_op jit(solution)/shard_map/ppermute | solution.py:175
  15.5 7.0 %collective-permute-start.2 = (bf16[16,4608]{1,0:T(8,128)(2,1)S(1)}, bf16[16,4608]{1,0:T(8,128)(2,1)S(1)}, u32[]{:S(2)}, u32[]{:S(2)}) collective-permute-start(bf16[16,4608]{1,0:T(8,128)(2,1)S(1)} %get-tuple-element.28), channel_id=1, source_target_pairs={{0,12},{1,13},{2,14},{3,15},{4,8},{5,9},{6,10},{7,11},{8,4},{9,5},... | collective-permute-start | bytes 442376 | tf_op jit(solution)/shard_map/ppermute | solution.py:172
  18.0 5.2 %collective-permute-start.6 = (bf16[16,4608]{1,0:T(8,128)(2,1)S(1)}, bf16[16,4608]{1,0:T(8,128)(2,1)S(1)}, u32[]{:S(2)}, u32[]{:S(2)}) collective-permute-start(bf16[16,4608]{1,0:T(8,128)(2,1)S(1)} %collective-permute-done.3), channel_id=1, source_target_pairs={{0,2},{1,3},{2,0},{3,1},{4,6},{5,7},{6,4},{7,5},{8,10},{9,11},{10,... | collective-permute-start | bytes 442376 | tf_op jit(solution)/shard_map/ppermute | solution.py:172
  19.2 10.5 %collective-permute-start.9 = (bf16[32,4608]{1,0:T(8,128)(2,1)S(1)}, bf16[32,4608]{1,0:T(8,128)(2,1)S(1)}, u32[]{:S(2)}, u32[]{:S(2)}) collective-permute-start(bf16[32,4608]{1,0:T(8,128)(2,1)S(1)} %pad_maximum_fusion), channel_id=1, source_target_pairs={{0,16},{16,0},{1,17},{17,1},{2,18},{18,2},{3,19},{19,3},{4,20},{20... | collective-permute-start | bytes 884744 | tf_op jit(solution)/shard_map/ppermute | solution.py:175
  20.8 14.0 %collective-permute-start.11 = (bf16[96,4608]{1,0:T(8,128)(2,1)S(1)}, bf16[96,4608]{1,0:T(8,128)(2,1)S(1)}, u32[]{:S(2)}, u32[]{:S(2)}) collective-permute-start(bf16[96,4608]{1,0:T(8,128)(2,1)S(1)} %constant_dynamic-update-slice_fusion.refs_2_), channel_id=1, source_target_pairs={{0,1},{1,0},{2,3},{3,2},{4,5},{5,4},{6,7},{7,6},{8,9},{9,8},{10,11... | collective-permute-start | bytes 2654216 | tf_op jit(solution)/shard_map/ppermute | solution.py:172
  20.9 0.7 %copy-start.4 = (s32[64]{0:T(128)S(1)}, s32[64]{0:T(128)}, u32[]{:S(2)}) copy-start(s32[64]{0:T(128)} %lengths_hbm) | copy-start | bytes 772
  23.2 8.5 %collective-permute-start.13 = (bf16[16,4608]{1,0:T(8,128)(2,1)S(1)}, bf16[16,4608]{1,0:T(8,128)(2,1)S(1)}, u32[]{:S(2)}, u32[]{:S(2)}) collective-permute-start(bf16[16,4608]{1,0:T(8,128)(2,1)S(1)} %collective-permute-done.2), channel_id=1, source_target_pairs={{0,16},{16,0},{1,17},{17,1},{2,18},{18,2},{3,19},{19,3},{4,20},{20... | collective-permute-start | bytes 442376 | tf_op jit(solution)/shard_map/ppermute | solution.py:175
  24.0 5.6 %collective-permute-start.8 = (bf16[16,4608]{1,0:T(8,128)(2,1)S(1)}, bf16[16,4608]{1,0:T(8,128)(2,1)S(1)}, u32[]{:S(2)}, u32[]{:S(2)}) collective-permute-start(bf16[16,4608]{1,0:T(8,128)(2,1)S(1)} %collective-permute-done.2), channel_id=1, source_target_pairs={{0,2},{1,3},{2,0},{3,1},{4,6},{5,7},{6,4},{7,5},{8,10},{9,11},{10,... | collective-permute-start | bytes 442376 | tf_op jit(solution)/shard_map/ppermute | solution.py:172
  25.8 3.1 %copy-start = (bf16[128,28672]{1,0:T(8,128)(2,1)S(1)}, bf16[128,28672]{1,0:T(8,128)(2,1)}, u32[]{:S(2)}) copy-start(bf16[128,28672]{1,0:T(8,128)(2,1)} %in_ref.7) | copy-start | bytes 22020100
  28.9 6.0 %slice-start = ((s8[7340032]{0:T(1024)(128)(4,1)}), s8[4194304]{0:T(1024)(128)(4,1)S(1)}, s32[]{:S(2)}) async-start(s8[7340032]{0:T(1024)(128)(4,1)} %bitcast), calls=%async_computation | async-start | bytes 8388608
  29.6 5.2 %collective-permute-start.14 = (bf16[16,4608]{1,0:T(8,128)(2,1)S(1)}, bf16[16,4608]{1,0:T(8,128)(2,1)S(1)}, u32[]{:S(2)}, u32[]{:S(2)}) collective-permute-start(bf16[16,4608]{1,0:T(8,128)(2,1)S(1)} %slice.3), channel_id=1, source_target_pairs={{0,2},{1,3},{2,0},{3,1},{4,6},{5,7},{6,4},{7,5},{8,10},{9,11},{10,... | collective-permute-start | bytes 442376 | tf_op jit(solution)/shard_map/ppermute | solution.py:172
  31.0 5.5 %collective-permute-start.10 = (bf16[16,4608]{1,0:T(8,128)(2,1)S(1)}, bf16[16,4608]{1,0:T(8,128)(2,1)S(1)}, u32[]{:S(2)}, u32[]{:S(2)}) collective-permute-start(bf16[16,4608]{1,0:T(8,128)(2,1)S(1)} %collective-permute-done.8), channel_id=1, source_target_pairs={{0,16},{16,0},{1,17},{17,1},{2,18},{18,2},{3,19},{19,3},{4,20},{20... | collective-permute-start | bytes 442376 | tf_op jit(solution)/shard_map/ppermute | solution.py:175
  31.6 3.3 %collective-permute-start.12 = (bf16[80,4608]{1,0:T(8,128)(2,1)S(1)}, bf16[80,4608]{1,0:T(8,128)(2,1)S(1)}, u32[]{:S(2)}, u32[]{:S(2)}) collective-permute-start(bf16[80,4608]{1,0:T(8,128)(2,1)S(1)} %constant_dynamic-update-slice_fusion.5.refs_4_), channel_id=1, source_target_pairs={{0,1},{1,0},{2,3},{3,2},{4,5},{5,4},{6,7},{7,6},{8,9},{9,8},{10,11... | collective-permute-start | bytes 2211848 | tf_op jit(solution)/shard_map/ppermute | solution.py:172
  31.7 3.2 %slice-start.1 = ((s8[7340032]{0:T(1024)(128)(4,1)}), s8[3145728]{0:T(1024)(128)(4,1)S(1)}, s32[]{:S(2)}) async-start(s8[7340032]{0:T(1024)(128)(4,1)} %bitcast), calls=%async_computation.1 | async-start | bytes 6291456
  36.6 1.9 %collective-permute-start.15 = (bf16[48,4608]{1,0:T(8,128)(2,1)S(1)}, bf16[48,4608]{1,0:T(8,128)(2,1)S(1)}, u32[]{:S(2)}, u32[]{:S(2)}) collective-permute-start(bf16[48,4608]{1,0:T(8,128)(2,1)S(1)} %constant_dynamic-update-slice_fusion.9.refs_6_), channel_id=1, source_target_pairs={{0,1},{1,0},{2,3},{3,2},{4,5},{5,4},{6,7},{7,6},{8,9},{9,8},{10,11... | collective-permute-start | bytes 1327112 | tf_op jit(solution)/shard_map/ppermute | solution.py:172

commit v10 on v9

--- a/solution.py
+++ b/solution.py
@@ -10,7 +10,7 @@
 RANK = 32
 EPSILON = 1e-06
 PACK = 16
-HEAD = 8192
+HEAD = 2048
 SCORE_VMEM = 24 * 1024 * 1024
 
 NT = (((1,), (1,)), ((), ()))

time: 41 us -> 40.8 us (level)
  waiting for transfers between devices: 3.93 us -> 2.79 us
  starting transfers between devices: 23.2 us -> 24.1 us
    ppermute x12, waiting for transfers between devices: 3.92 us -> 2.78 us  [swap(): return lax.ppermute(value, 'seq', [(i, i ^ mask) for i in range(devices)])]
    ppermute x12, starting transfers between devices: 18.8 us -> 19.7 us  [swap(): return lax.ppermute(value, 'seq', [(i, i ^ mask) for i in range(devices)])]
    pallas_call x1, Pallas kernels: 2.36 us -> 2.79 us  [norm_step(): pl.pallas_call(norm_kernel, out_shape=jax.ShapeDtypeStruct((1, tok_cap),...]
  transfers between devices with their start and end apart: 16 -> 16, of which waited for: 5 -> 4; matrix products, arithmetic and copies ran while one was open for 0% -> 1% of each run, Pallas kernels for 13% -> 13%
where the time goes in v10:
time: 40.8 us; the launch traced here: 40.5 us
  starting transfers between devices  24.1 us (59%)
  Pallas kernels  7.67 us (19%)
  local copies, waits for them, and re-layouts  5.74 us (14%)
  waiting for transfers between devices  2.79 us (7%)
    ppermute x12, starting transfers between devices, swap(): return lax.ppermute(value, 'seq', [(i, i ^ mask) for i in range(devices)])  19.7 us
    unnamed x23, local copies, waits for them, and re-layouts  5.68 us
    ppermute x4, starting transfers between devices, across(): return lax.ppermute(value, 'grp', [(0, 1), (1, 0)])  4.38 us
    pallas_call x1, Pallas kernels, norm_step(): pl.pallas_call(norm_kernel, out_shape=jax.ShapeDtypeStruct((1, tok_cap),...  2.79 us
    ppermute x12, waiting for transfers between devices, swap(): return lax.ppermute(value, 'seq', [(i, i ^ mask) for i in range(devices)])  2.78 us
    pallas_call x1, Pallas kernels, local(): pl.pallas_call(functools.partial(score_kernel, rank_rows, paired, places)...  2.32 us
    pallas_call x1, Pallas kernels, partial_step(): pl.pallas_call(functools.partial(partial_kernel, rank_rows, paired, place...  1.61 us
  transfers between devices with their start and end apart: 16, of which 4 were waited for; matrix products, arithmetic and copies ran while one was open for 1% of the time, Pallas kernels for 13%

profile of v10, /device:TPU:0, one launch (start us, length us, event | category | flops | bytes accessed | tf_op | source)
XLA Modules:
  0.0 40.5 jit_solution(16286262221546524291)
XLA Ops:
  0.0 0.9 %copy-done.2 = bf16[4,28672]{1,0:T(4,128)(2,1)S(1)} copy-done((bf16[4,28672]{1,0:T(4,128)(2,1)S(1)}, bf16[4,28672]{1,0:T(4,128)(2,1)}, u32[]{:S(2)}) %copy-start.2) | copy-done | bytes 229400
  0.9 0.8 %copy-done.3 = bf16[4,8192]{1,0:T(4,128)(2,1)S(1)} copy-done((bf16[4,8192]{1,0:T(4,128)(2,1)S(1)}, bf16[4,8192]{1,0:T(4,128)(2,1)}, u32[]{:S(2)}) %copy-start.3) | copy-done | bytes 65560
  1.9 0.5 %collective-permute-start.1 = (bf16[32,4608]{1,0:T(8,128)(2,1)S(1)}, bf16[32,4608]{1,0:T(8,128)(2,1)S(1)}, u32[]{:S(2)}, u32[]{:S(2)}) collective-permute-start(bf16[32,4608]{1,0:T(8,128)(2,1)S(1)} %get-tuple-element.27.refs_0_), channel_id=1, source_target_pairs={{0,1},{1,0},{2,3},{3,2},{4,5},{5,4},{6,7},{7,6},{8,9},{9,8},{10,11... | collective-permute-start | bytes 884744 | tf_op jit(solution)/shard_map/ppermute | solution.py:172
  2.4 2.6 %collective-permute-start = (bf16[16,4608]{1,0:T(8,128)(2,1)S(1)}, bf16[16,4608]{1,0:T(8,128)(2,1)S(1)}, u32[]{:S(2)}, u32[]{:S(2)}) collective-permute-start(bf16[16,4608]{1,0:T(8,128)(2,1)S(1)} %get-tuple-element.28), channel_id=1, source_target_pairs={{0,4},{1,5},{2,6},{3,7},{4,0},{5,1},{6,2},{7,3},{8,12},{9,13},{10,... | collective-permute-start | bytes 442376 | tf_op jit(solution)/shard_map/ppermute | solution.py:172
  5.0 1.5 %collective-permute-start.5 = (bf16[32,4608]{1,0:T(8,128)(2,1)S(1)}, bf16[32,4608]{1,0:T(8,128)(2,1)S(1)}, u32[]{:S(2)}, u32[]{:S(2)}) collective-permute-start(bf16[32,4608]{1,0:T(8,128)(2,1)S(1)} %get-tuple-element.27.refs_0_), channel_id=1, source_target_pairs={{0,2},{1,3},{2,0},{3,1},{4,6},{5,7},{6,4},{7,5},{8,10},{9,11},{10,... | collective-permute-start | bytes 884744 | tf_op jit(solution)/shard_map/ppermute | solution.py:172
  6.5 2.6 %collective-permute-start.3 = (bf16[16,4608]{1,0:T(8,128)(2,1)S(1)}, bf16[16,4608]{1,0:T(8,128)(2,1)S(1)}, u32[]{:S(2)}, u32[]{:S(2)}) collective-permute-start(bf16[16,4608]{1,0:T(8,128)(2,1)S(1)} %get-tuple-element.28), channel_id=1, source_target_pairs={{0,8},{1,9},{2,10},{3,11},{4,12},{5,13},{6,14},{7,15},{8,0},{9,1},... | collective-permute-start | bytes 442376 | tf_op jit(solution)/shard_map/ppermute | solution.py:172
  9.5 4.5 %collective-permute-start.4 = (bf16[16,4608]{1,0:T(8,128)(2,1)S(1)}, bf16[16,4608]{1,0:T(8,128)(2,1)S(1)}, u32[]{:S(2)}, u32[]{:S(2)}) collective-permute-start(bf16[16,4608]{1,0:T(8,128)(2,1)S(1)} %collective-permute-done), channel_id=1, source_target_pairs={{0,2},{1,3},{2,0},{3,1},{4,6},{5,7},{6,4},{7,5},{8,10},{9,11},{10,... | collective-permute-start | bytes 442376 | tf_op jit(solution)/shard_map/ppermute | solution.py:172
  14.0 1.5 %collective-permute-start.7 = (bf16[16,4608]{1,0:T(8,128)(2,1)S(1)}, bf16[16,4608]{1,0:T(8,128)(2,1)S(1)}, u32[]{:S(2)}, u32[]{:S(2)}) collective-permute-start(bf16[16,4608]{1,0:T(8,128)(2,1)S(1)} %collective-permute-done), channel_id=1, source_target_pairs={{0,16},{16,0},{1,17},{17,1},{2,18},{18,2},{3,19},{19,3},{4,20},{20... | collective-permute-start | bytes 442376 | tf_op jit(solution)/shard_map/ppermute | solution.py:175
  15.5 2.5 %collective-permute-start.2 = (bf16[16,4608]{1,0:T(8,128)(2,1)S(1)}, bf16[16,4608]{1,0:T(8,128)(2,1)S(1)}, u32[]{:S(2)}, u32[]{:S(2)}) collective-permute-start(bf16[16,4608]{1,0:T(8,128)(2,1)S(1)} %get-tuple-element.28), channel_id=1, source_target_pairs={{0,12},{1,13},{2,14},{3,15},{4,8},{5,9},{6,10},{7,11},{8,4},{9,5},... | collective-permute-start | bytes 442376 | tf_op jit(solution)/shard_map/ppermute | solution.py:172
  18.0 1.2 %collective-permute-start.6 = (bf16[16,4608]{1,0:T(8,128)(2,1)S(1)}, bf16[16,4608]{1,0:T(8,128)(2,1)S(1)}, u32[]{:S(2)}, u32[]{:S(2)}) collective-permute-start(bf16[16,4608]{1,0:T(8,128)(2,1)S(1)} %collective-permute-done.3), channel_id=1, source_target_pairs={{0,2},{1,3},{2,0},{3,1},{4,6},{5,7},{6,4},{7,5},{8,10},{9,11},{10,... | collective-permute-start | bytes 442376 | tf_op jit(solution)/shard_map/ppermute | solution.py:172
  19.2 1.6 %collective-permute-start.9 = (bf16[32,4608]{1,0:T(8,128)(2,1)S(1)}, bf16[32,4608]{1,0:T(8,128)(2,1)S(1)}, u32[]{:S(2)}, u32[]{:S(2)}) collective-permute-start(bf16[32,4608]{1,0:T(8,128)(2,1)S(1)} %pad_maximum_fusion), channel_id=1, source_target_pairs={{0,16},{16,0},{1,17},{17,1},{2,18},{18,2},{3,19},{19,3},{4,20},{20... | collective-permute-start | bytes 884744 | tf_op jit(solution)/shard_map/ppermute | solution.py:175
  20.9 0.6 %copy-done.4 = s32[64]{0:T(128)S(1)} copy-done((s32[64]{0:T(128)S(1)}, s32[64]{0:T(128)}, u32[]{:S(2)}) %copy-start.4) | copy-done | bytes 280
  21.6 0.6 %shard_map.56 = (f32[8,128]{1,0:T(8,128)S(1)}, f32[4,128,64]{2,1,0:T(8,128)S(1)}) custom-call(s32[64]{0:T(128)S(1)} %copy-done.4, bf16[16,4608]{1,0:T(8,128)(2,1)S(1)} %collective-permute-done.7.after_ref), custom_call_target="tpu_custom_call" | custom-call | flops 1 | bytes 1 | tf_op jit(solution)/shard_map/pallas_call | solution.py:250
  22.5 0.6 %collective-permute-done.6 = bf16[16,4608]{1,0:T(8,128)(2,1)S(1)} collective-permute-done((bf16[16,4608]{1,0:T(8,128)(2,1)S(1)}, bf16[16,4608]{1,0:T(8,128)(2,1)S(1)}, u32[]{:S(2)}, u32[]{:S(2)}) %collective-permute-start.6) | collective-permute-done | bytes 147488 | tf_op jit(solution)/shard_map/ppermute | solution.py:172
  23.2 0.8 %collective-permute-start.13 = (bf16[16,4608]{1,0:T(8,128)(2,1)S(1)}, bf16[16,4608]{1,0:T(8,128)(2,1)S(1)}, u32[]{:S(2)}, u32[]{:S(2)}) collective-permute-start(bf16[16,4608]{1,0:T(8,128)(2,1)S(1)} %collective-permute-done.2), channel_id=1, source_target_pairs={{0,16},{16,0},{1,17},{17,1},{2,18},{18,2},{3,19},{19,3},{4,20},{20... | collective-permute-start | bytes 442376 | tf_op jit(solution)/shard_map/ppermute | solution.py:175
  24.0 1.8 %collective-permute-start.8 = (bf16[16,4608]{1,0:T(8,128)(2,1)S(1)}, bf16[16,4608]{1,0:T(8,128)(2,1)S(1)}, u32[]{:S(2)}, u32[]{:S(2)}) collective-permute-start(bf16[16,4608]{1,0:T(8,128)(2,1)S(1)} %collective-permute-done.2), channel_id=1, source_target_pairs={{0,2},{1,3},{2,0},{3,1},{4,6},{5,7},{6,4},{7,5},{8,10},{9,11},{10,... | collective-permute-start | bytes 442376 | tf_op jit(solution)/shard_map/ppermute | solution.py:172
  25.8 3.1 %copy-done = bf16[128,28672]{1,0:T(8,128)(2,1)S(1)} copy-done((bf16[128,28672]{1,0:T(8,128)(2,1)S(1)}, bf16[128,28672]{1,0:T(8,128)(2,1)}, u32[]{:S(2)}) %copy-start) | copy-done | bytes 7340056
  29.2 1.8 %collective-permute-start.14 = (bf16[16,4608]{1,0:T(8,128)(2,1)S(1)}, bf16[16,4608]{1,0:T(8,128)(2,1)S(1)}, u32[]{:S(2)}, u32[]{:S(2)}) collective-permute-start(bf16[16,4608]{1,0:T(8,128)(2,1)S(1)} %slice.3), channel_id=1, source_target_pairs={{0,2},{1,3},{2,0},{3,1},{4,6},{5,7},{6,4},{7,5},{8,10},{9,11},{10,... | collective-permute-start | bytes 442376 | tf_op jit(solution)/shard_map/ppermute | solution.py:172
  31.0 0.5 %collective-permute-start.10 = (bf16[16,4608]{1,0:T(8,128)(2,1)S(1)}, bf16[16,4608]{1,0:T(8,128)(2,1)S(1)}, u32[]{:S(2)}, u32[]{:S(2)}) collective-permute-start(bf16[16,4608]{1,0:T(8,128)(2,1)S(1)} %collective-permute-done.8), channel_id=1, source_target_pairs={{0,16},{16,0},{1,17},{17,1},{2,18},{18,2},{3,19},{19,3},{4,20},{20... | collective-permute-start | bytes 442376 | tf_op jit(solution)/shard_map/ppermute | solution.py:175
  31.7 2.8 %shard_map.59.norm_ref = f32[1,128]{1,0:T(1,128)S(1)} custom-call(f32[8,128]{1,0:T(8,128)S(1)} %get-tuple-element.41.member_ref, f32[128,128]{1,0:T(8,128)S(1)} %shard_map.57.head_ref, bf16[128,8192]{1,0:T(8,128)(2,1)S(1)} %copy-done.1, bf16[128,28672]{1,0:T(8,128)(2,1)S(1)} %copy-done), custom_call_target="tpu_custom_call" | custom-call | flops 1 | bytes 1 | tf_op jit(solution)/shard_map/pallas_call | solution.py:274
  34.6 1.6 %shard_map.58.held_ref = f32[2,128,64]{2,1,0:T(8,128)S(1)} custom-call(bf16[128,8192]{1,0:T(8,128)(2,1)S(1)} %copy-done.1, bf16[128,28672]{1,0:T(8,128)(2,1)S(1)} %bitcast.1, bf16[32,4608]{1,0:T(8,128)(2,1)S(1)} %get-tuple-element.27.refs_0_, bf16[32,4608]{1,0:T(8,128)(2,1)S(1)} %collective-permute-done.1.refs_1_, ...), custom_call_target="tpu_custom_call" | custom-call | flops 1 | bytes 1 | tf_op jit(solution)/shard_map/pallas_call | solution.py:285
  36.3 0.6 %collective-permute-start.15 = (bf16[48,4608]{1,0:T(8,128)(2,1)S(1)}, bf16[48,4608]{1,0:T(8,128)(2,1)S(1)}, u32[]{:S(2)}, u32[]{:S(2)}) collective-permute-start(bf16[48,4608]{1,0:T(8,128)(2,1)S(1)} %constant_dynamic-update-slice_fusion.9.refs_6_), channel_id=1, source_target_pairs={{0,1},{1,0},{2,3},{3,2},{4,5},{5,4},{6,7},{7,6},{8,9},{9,8},{10,11... | collective-permute-start | bytes 1327112 | tf_op jit(solution)/shard_map/ppermute | solution.py:172
  36.8 1.4 %collective-permute-done.15.refs_7_ = bf16[48,4608]{1,0:T(8,128)(2,1)S(1)} collective-permute-done((bf16[48,4608]{1,0:T(8,128)(2,1)S(1)}, bf16[48,4608]{1,0:T(8,128)(2,1)S(1)}, u32[]{:S(2)}, u32[]{:S(2)}) %collective-permute-start.15) | collective-permute-done | bytes 442400 | tf_op jit(solution)/shard_map/ppermute | solution.py:172
  38.2 2.3 %shard_map.60 = f32[2,4]{1,0:T(2,128)} custom-call(f32[1,128]{1,0:T(1,128)S(1)} %shard_map.59.norm_ref, f32[4,128,64]{2,1,0:T(8,128)S(1)} %get-tuple-element.44.spread_ref, f32[2,128,64]{2,1,0:T(8,128)S(1)} %shard_map.58.held_ref, bf16[128,8192]{1,0:T(8,128)(2,1)S(1)} %copy-done.1, bf16[128,28672]{1,0:T(8,128)(2,1)S(1)} %bitcast.1, ...), custom_call_target="tpu_custom_call" | custom-call | flops 1 | bytes 1 | tf_op jit(solution)/shard_map/pallas_call | solution.py:305
  (43 shorter events, 1.5 us)
Async XLA Ops:
  0.0 0.9 %copy-start.2 = (bf16[4,28672]{1,0:T(4,128)(2,1)S(1)}, bf16[4,28672]{1,0:T(4,128)(2,1)}, u32[]{:S(2)}) copy-start(bf16[4,28672]{1,0:T(4,128)(2,1)} %v_ref.1) | copy-start | bytes 688132
  0.9 0.8 %copy-start.3 = (bf16[4,8192]{1,0:T(4,128)(2,1)S(1)}, bf16[4,8192]{1,0:T(4,128)(2,1)}, u32[]{:S(2)}) copy-start(bf16[4,8192]{1,0:T(4,128)(2,1)} %u_ref.1) | copy-start | bytes 196612
  1.8 29.9 %copy-start.1 = (bf16[128,8192]{1,0:T(8,128)(2,1)S(1)}, bf16[128,8192]{1,0:T(8,128)(2,1)}, u32[]{:S(2)}) copy-start(bf16[128,8192]{1,0:T(8,128)(2,1)} %out_ref.5) | copy-start | bytes 6291460
  1.9 7.6 %collective-permute-start.1 = (bf16[32,4608]{1,0:T(8,128)(2,1)S(1)}, bf16[32,4608]{1,0:T(8,128)(2,1)S(1)}, u32[]{:S(2)}, u32[]{:S(2)}) collective-permute-start(bf16[32,4608]{1,0:T(8,128)(2,1)S(1)} %get-tuple-element.27.refs_0_), channel_id=1, source_target_pairs={{0,1},{1,0},{2,3},{3,2},{4,5},{5,4},{6,7},{7,6},{8,9},{9,8},{10,11... | collective-permute-start | bytes 884744 | tf_op jit(solution)/shard_map/ppermute | solution.py:172
  2.4 7.1 %collective-permute-start = (bf16[16,4608]{1,0:T(8,128)(2,1)S(1)}, bf16[16,4608]{1,0:T(8,128)(2,1)S(1)}, u32[]{:S(2)}, u32[]{:S(2)}) collective-permute-start(bf16[16,4608]{1,0:T(8,128)(2,1)S(1)} %get-tuple-element.28), channel_id=1, source_target_pairs={{0,4},{1,5},{2,6},{3,7},{4,0},{5,1},{6,2},{7,3},{8,12},{9,13},{10,... | collective-permute-start | bytes 442376 | tf_op jit(solution)/shard_map/ppermute | solution.py:172
  5.0 12.9 %collective-permute-start.5 = (bf16[32,4608]{1,0:T(8,128)(2,1)S(1)}, bf16[32,4608]{1,0:T(8,128)(2,1)S(1)}, u32[]{:S(2)}, u32[]{:S(2)}) collective-permute-start(bf16[32,4608]{1,0:T(8,128)(2,1)S(1)} %get-tuple-element.27.refs_0_), channel_id=1, source_target_pairs={{0,2},{1,3},{2,0},{3,1},{4,6},{5,7},{6,4},{7,5},{8,10},{9,11},{10,... | collective-permute-start | bytes 884744 | tf_op jit(solution)/shard_map/ppermute | solution.py:172
  6.5 11.4 %collective-permute-start.3 = (bf16[16,4608]{1,0:T(8,128)(2,1)S(1)}, bf16[16,4608]{1,0:T(8,128)(2,1)S(1)}, u32[]{:S(2)}, u32[]{:S(2)}) collective-permute-start(bf16[16,4608]{1,0:T(8,128)(2,1)S(1)} %get-tuple-element.28), channel_id=1, source_target_pairs={{0,8},{1,9},{2,10},{3,11},{4,12},{5,13},{6,14},{7,15},{8,0},{9,1},... | collective-permute-start | bytes 442376 | tf_op jit(solution)/shard_map/ppermute | solution.py:172
  9.5 8.5 %collective-permute-start.4 = (bf16[16,4608]{1,0:T(8,128)(2,1)S(1)}, bf16[16,4608]{1,0:T(8,128)(2,1)S(1)}, u32[]{:S(2)}, u32[]{:S(2)}) collective-permute-start(bf16[16,4608]{1,0:T(8,128)(2,1)S(1)} %collective-permute-done), channel_id=1, source_target_pairs={{0,2},{1,3},{2,0},{3,1},{4,6},{5,7},{6,4},{7,5},{8,10},{9,11},{10,... | collective-permute-start | bytes 442376 | tf_op jit(solution)/shard_map/ppermute | solution.py:172
  14.0 6.8 %collective-permute-start.7 = (bf16[16,4608]{1,0:T(8,128)(2,1)S(1)}, bf16[16,4608]{1,0:T(8,128)(2,1)S(1)}, u32[]{:S(2)}, u32[]{:S(2)}) collective-permute-start(bf16[16,4608]{1,0:T(8,128)(2,1)S(1)} %collective-permute-done), channel_id=1, source_target_pairs={{0,16},{16,0},{1,17},{17,1},{2,18},{18,2},{3,19},{19,3},{4,20},{20... | collective-permute-start | bytes 442376 | tf_op jit(solution)/shard_map/ppermute | solution.py:175
  15.5 7.0 %collective-permute-start.2 = (bf16[16,4608]{1,0:T(8,128)(2,1)S(1)}, bf16[16,4608]{1,0:T(8,128)(2,1)S(1)}, u32[]{:S(2)}, u32[]{:S(2)}) collective-permute-start(bf16[16,4608]{1,0:T(8,128)(2,1)S(1)} %get-tuple-element.28), channel_id=1, source_target_pairs={{0,12},{1,13},{2,14},{3,15},{4,8},{5,9},{6,10},{7,11},{8,4},{9,5},... | collective-permute-start | bytes 442376 | tf_op jit(solution)/shard_map/ppermute | solution.py:172
  18.0 5.2 %collective-permute-start.6 = (bf16[16,4608]{1,0:T(8,128)(2,1)S(1)}, bf16[16,4608]{1,0:T(8,128)(2,1)S(1)}, u32[]{:S(2)}, u32[]{:S(2)}) collective-permute-start(bf16[16,4608]{1,0:T(8,128)(2,1)S(1)} %collective-permute-done.3), channel_id=1, source_target_pairs={{0,2},{1,3},{2,0},{3,1},{4,6},{5,7},{6,4},{7,5},{8,10},{9,11},{10,... | collective-permute-start | bytes 442376 | tf_op jit(solution)/shard_map/ppermute | solution.py:172
  19.2 10.1 %collective-permute-start.9 = (bf16[32,4608]{1,0:T(8,128)(2,1)S(1)}, bf16[32,4608]{1,0:T(8,128)(2,1)S(1)}, u32[]{:S(2)}, u32[]{:S(2)}) collective-permute-start(bf16[32,4608]{1,0:T(8,128)(2,1)S(1)} %pad_maximum_fusion), channel_id=1, source_target_pairs={{0,16},{16,0},{1,17},{17,1},{2,18},{18,2},{3,19},{19,3},{4,20},{20... | collective-permute-start | bytes 884744 | tf_op jit(solution)/shard_map/ppermute | solution.py:175
  20.8 13.7 %collective-permute-start.11 = (bf16[96,4608]{1,0:T(8,128)(2,1)S(1)}, bf16[96,4608]{1,0:T(8,128)(2,1)S(1)}, u32[]{:S(2)}, u32[]{:S(2)}) collective-permute-start(bf16[96,4608]{1,0:T(8,128)(2,1)S(1)} %constant_dynamic-update-slice_fusion.refs_2_), channel_id=1, source_target_pairs={{0,1},{1,0},{2,3},{3,2},{4,5},{5,4},{6,7},{7,6},{8,9},{9,8},{10,11... | collective-permute-start | bytes 2654216 | tf_op jit(solution)/shard_map/ppermute | solution.py:172
  20.9 0.7 %copy-start.4 = (s32[64]{0:T(128)S(1)}, s32[64]{0:T(128)}, u32[]{:S(2)}) copy-start(s32[64]{0:T(128)} %lengths_hbm) | copy-start | bytes 772
  23.2 8.5 %collective-permute-start.13 = (bf16[16,4608]{1,0:T(8,128)(2,1)S(1)}, bf16[16,4608]{1,0:T(8,128)(2,1)S(1)}, u32[]{:S(2)}, u32[]{:S(2)}) collective-permute-start(bf16[16,4608]{1,0:T(8,128)(2,1)S(1)} %collective-permute-done.2), channel_id=1, source_target_pairs={{0,16},{16,0},{1,17},{17,1},{2,18},{18,2},{3,19},{19,3},{4,20},{20... | collective-permute-start | bytes 442376 | tf_op jit(solution)/shard_map/ppermute | solution.py:175
  24.0 5.2 %collective-permute-start.8 = (bf16[16,4608]{1,0:T(8,128)(2,1)S(1)}, bf16[16,4608]{1,0:T(8,128)(2,1)S(1)}, u32[]{:S(2)}, u32[]{:S(2)}) collective-permute-start(bf16[16,4608]{1,0:T(8,128)(2,1)S(1)} %collective-permute-done.2), channel_id=1, source_target_pairs={{0,2},{1,3},{2,0},{3,1},{4,6},{5,7},{6,4},{7,5},{8,10},{9,11},{10,... | collective-permute-start | bytes 442376 | tf_op jit(solution)/shard_map/ppermute | solution.py:172
  25.8 3.1 %copy-start = (bf16[128,28672]{1,0:T(8,128)(2,1)S(1)}, bf16[128,28672]{1,0:T(8,128)(2,1)}, u32[]{:S(2)}) copy-start(bf16[128,28672]{1,0:T(8,128)(2,1)} %in_ref.7) | copy-start | bytes 22020100
  28.9 5.7 %slice-start = ((s8[7340032]{0:T(1024)(128)(4,1)}), s8[4194304]{0:T(1024)(128)(4,1)S(1)}, s32[]{:S(2)}) async-start(s8[7340032]{0:T(1024)(128)(4,1)} %bitcast), calls=%async_computation | async-start | bytes 8388608
  29.2 5.3 %collective-permute-start.14 = (bf16[16,4608]{1,0:T(8,128)(2,1)S(1)}, bf16[16,4608]{1,0:T(8,128)(2,1)S(1)}, u32[]{:S(2)}, u32[]{:S(2)}) collective-permute-start(bf16[16,4608]{1,0:T(8,128)(2,1)S(1)} %slice.3), channel_id=1, source_target_pairs={{0,2},{1,3},{2,0},{3,1},{4,6},{5,7},{6,4},{7,5},{8,10},{9,11},{10,... | collective-permute-start | bytes 442376 | tf_op jit(solution)/shard_map/ppermute | solution.py:172
  31.0 5.2 %collective-permute-start.10 = (bf16[16,4608]{1,0:T(8,128)(2,1)S(1)}, bf16[16,4608]{1,0:T(8,128)(2,1)S(1)}, u32[]{:S(2)}, u32[]{:S(2)}) collective-permute-start(bf16[16,4608]{1,0:T(8,128)(2,1)S(1)} %collective-permute-done.8), channel_id=1, source_target_pairs={{0,16},{16,0},{1,17},{17,1},{2,18},{18,2},{3,19},{19,3},{4,20},{20... | collective-permute-start | bytes 442376 | tf_op jit(solution)/shard_map/ppermute | solution.py:175
  31.6 3.0 %collective-permute-start.12 = (bf16[80,4608]{1,0:T(8,128)(2,1)S(1)}, bf16[80,4608]{1,0:T(8,128)(2,1)S(1)}, u32[]{:S(2)}, u32[]{:S(2)}) collective-permute-start(bf16[80,4608]{1,0:T(8,128)(2,1)S(1)} %constant_dynamic-update-slice_fusion.5.refs_4_), channel_id=1, source_target_pairs={{0,1},{1,0},{2,3},{3,2},{4,5},{5,4},{6,7},{7,6},{8,9},{9,8},{10,11... | collective-permute-start | bytes 2211848 | tf_op jit(solution)/shard_map/ppermute | solution.py:172
  31.7 2.9 %slice-start.1 = ((s8[7340032]{0:T(1024)(128)(4,1)}), s8[3145728]{0:T(1024)(128)(4,1)S(1)}, s32[]{:S(2)}) async-start(s8[7340032]{0:T(1024)(128)(4,1)} %bitcast), calls=%async_computation.1 | async-start | bytes 6291456
  36.3 2.0 %collective-permute-start.15 = (bf16[48,4608]{1,0:T(8,128)(2,1)S(1)}, bf16[48,4608]{1,0:T(8,128)(2,1)S(1)}, u32[]{:S(2)}, u32[]{:S(2)}) collective-permute-start(bf16[48,4608]{1,0:T(8,128)(2,1)S(1)} %constant_dynamic-update-slice_fusion.9.refs_6_), channel_id=1, source_target_pairs={{0,1},{1,0},{2,3},{3,2},{4,5},{5,4},{6,7},{7,6},{8,9},{9,8},{10,11... | collective-permute-start | bytes 1327112 | tf_op jit(solution)/shard_map/ppermute | solution.py:172

commit v11 on v10

--- a/solution.py
+++ b/solution.py
@@ -184,7 +184,8 @@
     member, spread = member_step(lengths, x1)
     z3, y2, member = gate(z3, y2, member)
     head = head_step(member)
-    x3, y3 = across(z3), swap(z3, 2)
+    y3 = swap(z3, 2)
+    x3 = across(lax.optimization_barrier((z3, x1))[0])
     early = stack(y0, z1, y1, z2, x1)
     early_core = swap(early, 1)
     y3, x_near, head, member = gate(y3, x_near, head, member)

time: 40.8 us -> 40.6 us (level)
  starting transfers between devices: 24.1 us -> 23.1 us
  waiting for transfers between devices: 2.79 us -> 3.59 us
    ppermute x12, starting transfers between devices: 19.7 us -> 17.1 us  [swap(): return lax.ppermute(value, 'seq', [(i, i ^ mask) for i in range(devices)])]
    ppermute x4, starting transfers between devices: 4.38 us -> 6 us  [across(): return lax.ppermute(value, 'grp', [(0, 1), (1, 0)])]
    ppermute x12, waiting for transfers between devices: 2.78 us -> 3.58 us  [swap(): return lax.ppermute(value, 'seq', [(i, i ^ mask) for i in range(devices)])]
  transfers between devices with their start and end apart: 16 -> 16, of which waited for: 4 -> 5; matrix products, arithmetic and copies ran while one was open for 1% -> 0% of each run, Pallas kernels for 13% -> 13%
where the time goes in v11:
time: 40.6 us; the launch traced here: 40.3 us
  starting transfers between devices  23.1 us (57%)
  Pallas kernels  7.67 us (19%)
  local copies, waits for them, and re-layouts  5.69 us (14%)
  waiting for transfers between devices  3.59 us (9%)
    ppermute x12, starting transfers between devices, swap(): return lax.ppermute(value, 'seq', [(i, i ^ mask) for i in range(devices)])  17.1 us
    ppermute x4, starting transfers between devices, across(): return lax.ppermute(value, 'grp', [(0, 1), (1, 0)])  6 us
    unnamed x23, local copies, waits for them, and re-layouts  5.63 us
    ppermute x12, waiting for transfers between devices, swap(): return lax.ppermute(value, 'seq', [(i, i ^ mask) for i in range(devices)])  3.58 us
    pallas_call x1, Pallas kernels, norm_step(): pl.pallas_call(norm_kernel, out_shape=jax.ShapeDtypeStruct((1, tok_cap),...  2.79 us
    pallas_call x1, Pallas kernels, local(): pl.pallas_call(functools.partial(score_kernel, rank_rows, paired, places)...  2.32 us
    pallas_call x1, Pallas kernels, partial_step(): pl.pallas_call(functools.partial(partial_kernel, rank_rows, paired, place...  1.6 us
  transfers between devices with their start and end apart: 16, of which 5 were waited for; matrix products, arithmetic and copies ran while one was open for 0% of the time, Pallas kernels for 13%

profile of v11, /device:TPU:0, one launch (start us, length us, event | category | flops | bytes accessed | tf_op | source)
XLA Modules:
  0.0 40.3 jit_solution(9295638636141798067)
XLA Ops:
  0.0 0.9 %copy-done.2 = bf16[4,28672]{1,0:T(4,128)(2,1)S(1)} copy-done((bf16[4,28672]{1,0:T(4,128)(2,1)S(1)}, bf16[4,28672]{1,0:T(4,128)(2,1)}, u32[]{:S(2)}) %copy-start.2) | copy-done | bytes 229400
  0.9 0.8 %copy-done.3 = bf16[4,8192]{1,0:T(4,128)(2,1)S(1)} copy-done((bf16[4,8192]{1,0:T(4,128)(2,1)S(1)}, bf16[4,8192]{1,0:T(4,128)(2,1)}, u32[]{:S(2)}) %copy-start.3) | copy-done | bytes 65560
  1.9 0.5 %collective-permute-start.1 = (bf16[32,4608]{1,0:T(8,128)(2,1)S(1)}, bf16[32,4608]{1,0:T(8,128)(2,1)S(1)}, u32[]{:S(2)}, u32[]{:S(2)}) collective-permute-start(bf16[32,4608]{1,0:T(8,128)(2,1)S(1)} %get-tuple-element.28.refs_0_), channel_id=1, source_target_pairs={{0,1},{1,0},{2,3},{3,2},{4,5},{5,4},{6,7},{7,6},{8,9},{9,8},{10,11... | collective-permute-start | bytes 884744 | tf_op jit(solution)/shard_map/ppermute | solution.py:172
  2.4 2.6 %collective-permute-start = (bf16[16,4608]{1,0:T(8,128)(2,1)S(1)}, bf16[16,4608]{1,0:T(8,128)(2,1)S(1)}, u32[]{:S(2)}, u32[]{:S(2)}) collective-permute-start(bf16[16,4608]{1,0:T(8,128)(2,1)S(1)} %get-tuple-element.29), channel_id=1, source_target_pairs={{0,4},{1,5},{2,6},{3,7},{4,0},{5,1},{6,2},{7,3},{8,12},{9,13},{10,... | collective-permute-start | bytes 442376 | tf_op jit(solution)/shard_map/ppermute | solution.py:172
  5.0 1.5 %collective-permute-start.5 = (bf16[32,4608]{1,0:T(8,128)(2,1)S(1)}, bf16[32,4608]{1,0:T(8,128)(2,1)S(1)}, u32[]{:S(2)}, u32[]{:S(2)}) collective-permute-start(bf16[32,4608]{1,0:T(8,128)(2,1)S(1)} %get-tuple-element.28.refs_0_), channel_id=1, source_target_pairs={{0,2},{1,3},{2,0},{3,1},{4,6},{5,7},{6,4},{7,5},{8,10},{9,11},{10,... | collective-permute-start | bytes 884744 | tf_op jit(solution)/shard_map/ppermute | solution.py:172
  6.5 2.6 %collective-permute-start.3 = (bf16[16,4608]{1,0:T(8,128)(2,1)S(1)}, bf16[16,4608]{1,0:T(8,128)(2,1)S(1)}, u32[]{:S(2)}, u32[]{:S(2)}) collective-permute-start(bf16[16,4608]{1,0:T(8,128)(2,1)S(1)} %get-tuple-element.29), channel_id=1, source_target_pairs={{0,8},{1,9},{2,10},{3,11},{4,12},{5,13},{6,14},{7,15},{8,0},{9,1},... | collective-permute-start | bytes 442376 | tf_op jit(solution)/shard_map/ppermute | solution.py:172
  9.5 4.5 %collective-permute-start.4 = (bf16[16,4608]{1,0:T(8,128)(2,1)S(1)}, bf16[16,4608]{1,0:T(8,128)(2,1)S(1)}, u32[]{:S(2)}, u32[]{:S(2)}) collective-permute-start(bf16[16,4608]{1,0:T(8,128)(2,1)S(1)} %collective-permute-done), channel_id=1, source_target_pairs={{0,2},{1,3},{2,0},{3,1},{4,6},{5,7},{6,4},{7,5},{8,10},{9,11},{10,... | collective-permute-start | bytes 442376 | tf_op jit(solution)/shard_map/ppermute | solution.py:172
  14.0 1.5 %collective-permute-start.7 = (bf16[16,4608]{1,0:T(8,128)(2,1)S(1)}, bf16[16,4608]{1,0:T(8,128)(2,1)S(1)}, u32[]{:S(2)}, u32[]{:S(2)}) collective-permute-start(bf16[16,4608]{1,0:T(8,128)(2,1)S(1)} %collective-permute-done), channel_id=1, source_target_pairs={{0,16},{16,0},{1,17},{17,1},{2,18},{18,2},{3,19},{19,3},{4,20},{20... | collective-permute-start | bytes 442376 | tf_op jit(solution)/shard_map/ppermute | solution.py:175
  15.5 2.5 %collective-permute-start.2 = (bf16[16,4608]{1,0:T(8,128)(2,1)S(1)}, bf16[16,4608]{1,0:T(8,128)(2,1)S(1)}, u32[]{:S(2)}, u32[]{:S(2)}) collective-permute-start(bf16[16,4608]{1,0:T(8,128)(2,1)S(1)} %get-tuple-element.29), channel_id=1, source_target_pairs={{0,12},{1,13},{2,14},{3,15},{4,8},{5,9},{6,10},{7,11},{8,4},{9,5},... | collective-permute-start | bytes 442376 | tf_op jit(solution)/shard_map/ppermute | solution.py:172
  18.0 1.2 %collective-permute-start.6 = (bf16[16,4608]{1,0:T(8,128)(2,1)S(1)}, bf16[16,4608]{1,0:T(8,128)(2,1)S(1)}, u32[]{:S(2)}, u32[]{:S(2)}) collective-permute-start(bf16[16,4608]{1,0:T(8,128)(2,1)S(1)} %collective-permute-done.3), channel_id=1, source_target_pairs={{0,2},{1,3},{2,0},{3,1},{4,6},{5,7},{6,4},{7,5},{8,10},{9,11},{10,... | collective-permute-start | bytes 442376 | tf_op jit(solution)/shard_map/ppermute | solution.py:172
  19.2 1.6 %collective-permute-start.9 = (bf16[32,4608]{1,0:T(8,128)(2,1)S(1)}, bf16[32,4608]{1,0:T(8,128)(2,1)S(1)}, u32[]{:S(2)}, u32[]{:S(2)}) collective-permute-start(bf16[32,4608]{1,0:T(8,128)(2,1)S(1)} %pad_maximum_fusion), channel_id=1, source_target_pairs={{0,16},{16,0},{1,17},{17,1},{2,18},{18,2},{3,19},{19,3},{4,20},{20... | collective-permute-start | bytes 884744 | tf_op jit(solution)/shard_map/ppermute | solution.py:175
  20.9 0.6 %copy-done.4 = s32[64]{0:T(128)S(1)} copy-done((s32[64]{0:T(128)S(1)}, s32[64]{0:T(128)}, u32[]{:S(2)}) %copy-start.4) | copy-done | bytes 280
  21.6 0.6 %shard_map.56 = (f32[8,128]{1,0:T(8,128)S(1)}, f32[4,128,64]{2,1,0:T(8,128)S(1)}) custom-call(s32[64]{0:T(128)S(1)} %copy-done.4, bf16[16,4608]{1,0:T(8,128)(2,1)S(1)} %collective-permute-done.7.after_ref), custom_call_target="tpu_custom_call" | custom-call | flops 1 | bytes 1 | tf_op jit(solution)/shard_map/pallas_call | solution.py:251
  22.2 0.4 collective-permute-done.2
  22.5 0.6 %collective-permute-done.6 = bf16[16,4608]{1,0:T(8,128)(2,1)S(1)} collective-permute-done((bf16[16,4608]{1,0:T(8,128)(2,1)S(1)}, bf16[16,4608]{1,0:T(8,128)(2,1)S(1)}, u32[]{:S(2)}, u32[]{:S(2)}) %collective-permute-start.6) | collective-permute-done | bytes 147488 | tf_op jit(solution)/shard_map/ppermute | solution.py:172
  23.2 1.1 %collective-permute-start.8 = (bf16[16,4608]{1,0:T(8,128)(2,1)S(1)}, bf16[16,4608]{1,0:T(8,128)(2,1)S(1)}, u32[]{:S(2)}, u32[]{:S(2)}) collective-permute-start(bf16[16,4608]{1,0:T(8,128)(2,1)S(1)} %collective-permute-done.2), channel_id=1, source_target_pairs={{0,2},{1,3},{2,0},{3,1},{4,6},{5,7},{6,4},{7,5},{8,10},{9,11},{10,... | collective-permute-start | bytes 442376 | tf_op jit(solution)/shard_map/ppermute | solution.py:172
  24.3 1.5 %collective-permute-start.13 = (bf16[16,4608]{1,0:T(8,128)(2,1)S(1)}, bf16[16,4608]{1,0:T(8,128)(2,1)S(1)}, u32[]{:S(2)}, u32[]{:S(2)}) collective-permute-start(bf16[16,4608]{1,0:T(8,128)(2,1)S(1)} %collective-permute-done.2), channel_id=1, source_target_pairs={{0,16},{16,0},{1,17},{17,1},{2,18},{18,2},{3,19},{19,3},{4,20},{20... | collective-permute-start | bytes 442376 | tf_op jit(solution)/shard_map/ppermute | solution.py:175
  25.8 3.1 %copy-done = bf16[128,28672]{1,0:T(8,128)(2,1)S(1)} copy-done((bf16[128,28672]{1,0:T(8,128)(2,1)S(1)}, bf16[128,28672]{1,0:T(8,128)(2,1)}, u32[]{:S(2)}) %copy-start) | copy-done | bytes 7340056
  29.5 1.5 %collective-permute-start.10 = (bf16[16,4608]{1,0:T(8,128)(2,1)S(1)}, bf16[16,4608]{1,0:T(8,128)(2,1)S(1)}, u32[]{:S(2)}, u32[]{:S(2)}) collective-permute-start(bf16[16,4608]{1,0:T(8,128)(2,1)S(1)} %collective-permute-done.8), channel_id=1, source_target_pairs={{0,16},{16,0},{1,17},{17,1},{2,18},{18,2},{3,19},{19,3},{4,20},{20... | collective-permute-start | bytes 442376 | tf_op jit(solution)/shard_map/ppermute | solution.py:175
  31.2 2.8 %shard_map.59.norm_ref = f32[1,128]{1,0:T(1,128)S(1)} custom-call(f32[8,128]{1,0:T(8,128)S(1)} %get-tuple-element.42.member_ref, f32[128,128]{1,0:T(8,128)S(1)} %shard_map.57.head_ref, bf16[128,8192]{1,0:T(8,128)(2,1)S(1)} %copy-done.1, bf16[128,28672]{1,0:T(8,128)(2,1)S(1)} %copy-done), custom_call_target="tpu_custom_call" | custom-call | flops 1 | bytes 1 | tf_op jit(solution)/shard_map/pallas_call | solution.py:275
  34.0 0.5 %collective-permute-done.14 = bf16[16,4608]{1,0:T(8,128)(2,1)S(1)} collective-permute-done((bf16[16,4608]{1,0:T(8,128)(2,1)S(1)}, bf16[16,4608]{1,0:T(8,128)(2,1)S(1)}, u32[]{:S(2)}, u32[]{:S(2)}) %collective-permute-start.14) | collective-permute-done | bytes 147488 | tf_op jit(solution)/shard_map/ppermute | solution.py:172
  34.5 1.6 %shard_map.58.held_ref = f32[2,128,64]{2,1,0:T(8,128)S(1)} custom-call(bf16[128,8192]{1,0:T(8,128)(2,1)S(1)} %copy-done.1, bf16[128,28672]{1,0:T(8,128)(2,1)S(1)} %bitcast.1, bf16[32,4608]{1,0:T(8,128)(2,1)S(1)} %get-tuple-element.28.refs_0_, bf16[32,4608]{1,0:T(8,128)(2,1)S(1)} %collective-permute-done.1.refs_1_, ...), custom_call_target="tpu_custom_call" | custom-call | flops 1 | bytes 1 | tf_op jit(solution)/shard_map/pallas_call | solution.py:286
  36.3 1.7 %collective-permute-done.15.refs_7_ = bf16[48,4608]{1,0:T(8,128)(2,1)S(1)} collective-permute-done((bf16[48,4608]{1,0:T(8,128)(2,1)S(1)}, bf16[48,4608]{1,0:T(8,128)(2,1)S(1)}, u32[]{:S(2)}, u32[]{:S(2)}) %collective-permute-start.15) | collective-permute-done | bytes 442400 | tf_op jit(solution)/shard_map/ppermute | solution.py:172
  38.0 2.3 %shard_map.60 = f32[2,4]{1,0:T(2,128)} custom-call(f32[1,128]{1,0:T(1,128)S(1)} %shard_map.59.norm_ref, f32[4,128,64]{2,1,0:T(8,128)S(1)} %get-tuple-element.45.spread_ref, f32[2,128,64]{2,1,0:T(8,128)S(1)} %shard_map.58.held_ref, bf16[128,8192]{1,0:T(8,128)(2,1)S(1)} %copy-done.1, bf16[128,28672]{1,0:T(8,128)(2,1)S(1)} %bitcast.1, ...), custom_call_target="tpu_custom_call" | custom-call | flops 1 | bytes 1 | tf_op jit(solution)/shard_map/pallas_call | solution.py:306
  (43 shorter events, 1.5 us)
Async XLA Ops:
  0.0 0.9 %copy-start.2 = (bf16[4,28672]{1,0:T(4,128)(2,1)S(1)}, bf16[4,28672]{1,0:T(4,128)(2,1)}, u32[]{:S(2)}) copy-start(bf16[4,28672]{1,0:T(4,128)(2,1)} %v_ref.1) | copy-start | bytes 688132
  0.9 0.8 %copy-start.3 = (bf16[4,8192]{1,0:T(4,128)(2,1)S(1)}, bf16[4,8192]{1,0:T(4,128)(2,1)}, u32[]{:S(2)}) copy-start(bf16[4,8192]{1,0:T(4,128)(2,1)} %u_ref.1) | copy-start | bytes 196612
  1.8 29.4 %copy-start.1 = (bf16[128,8192]{1,0:T(8,128)(2,1)S(1)}, bf16[128,8192]{1,0:T(8,128)(2,1)}, u32[]{:S(2)}) copy-start(bf16[128,8192]{1,0:T(8,128)(2,1)} %out_ref.5) | copy-start | bytes 6291460
  1.9 7.6 %collective-permute-start.1 = (bf16[32,4608]{1,0:T(8,128)(2,1)S(1)}, bf16[32,4608]{1,0:T(8,128)(2,1)S(1)}, u32[]{:S(2)}, u32[]{:S(2)}) collective-permute-start(bf16[32,4608]{1,0:T(8,128)(2,1)S(1)} %get-tuple-element.28.refs_0_), channel_id=1, source_target_pairs={{0,1},{1,0},{2,3},{3,2},{4,5},{5,4},{6,7},{7,6},{8,9},{9,8},{10,11... | collective-permute-start | bytes 884744 | tf_op jit(solution)/shard_map/ppermute | solution.py:172
  2.4 7.1 %collective-permute-start = (bf16[16,4608]{1,0:T(8,128)(2,1)S(1)}, bf16[16,4608]{1,0:T(8,128)(2,1)S(1)}, u32[]{:S(2)}, u32[]{:S(2)}) collective-permute-start(bf16[16,4608]{1,0:T(8,128)(2,1)S(1)} %get-tuple-element.29), channel_id=1, source_target_pairs={{0,4},{1,5},{2,6},{3,7},{4,0},{5,1},{6,2},{7,3},{8,12},{9,13},{10,... | collective-permute-start | bytes 442376 | tf_op jit(solution)/shard_map/ppermute | solution.py:172
  5.0 12.9 %collective-permute-start.5 = (bf16[32,4608]{1,0:T(8,128)(2,1)S(1)}, bf16[32,4608]{1,0:T(8,128)(2,1)S(1)}, u32[]{:S(2)}, u32[]{:S(2)}) collective-permute-start(bf16[32,4608]{1,0:T(8,128)(2,1)S(1)} %get-tuple-element.28.refs_0_), channel_id=1, source_target_pairs={{0,2},{1,3},{2,0},{3,1},{4,6},{5,7},{6,4},{7,5},{8,10},{9,11},{10,... | collective-permute-start | bytes 884744 | tf_op jit(solution)/shard_map/ppermute | solution.py:172
  6.5 11.4 %collective-permute-start.3 = (bf16[16,4608]{1,0:T(8,128)(2,1)S(1)}, bf16[16,4608]{1,0:T(8,128)(2,1)S(1)}, u32[]{:S(2)}, u32[]{:S(2)}) collective-permute-start(bf16[16,4608]{1,0:T(8,128)(2,1)S(1)} %get-tuple-element.29), channel_id=1, source_target_pairs={{0,8},{1,9},{2,10},{3,11},{4,12},{5,13},{6,14},{7,15},{8,0},{9,1},... | collective-permute-start | bytes 442376 | tf_op jit(solution)/shard_map/ppermute | solution.py:172
  9.5 8.5 %collective-permute-start.4 = (bf16[16,4608]{1,0:T(8,128)(2,1)S(1)}, bf16[16,4608]{1,0:T(8,128)(2,1)S(1)}, u32[]{:S(2)}, u32[]{:S(2)}) collective-permute-start(bf16[16,4608]{1,0:T(8,128)(2,1)S(1)} %collective-permute-done), channel_id=1, source_target_pairs={{0,2},{1,3},{2,0},{3,1},{4,6},{5,7},{6,4},{7,5},{8,10},{9,11},{10,... | collective-permute-start | bytes 442376 | tf_op jit(solution)/shard_map/ppermute | solution.py:172
  14.0 6.8 %collective-permute-start.7 = (bf16[16,4608]{1,0:T(8,128)(2,1)S(1)}, bf16[16,4608]{1,0:T(8,128)(2,1)S(1)}, u32[]{:S(2)}, u32[]{:S(2)}) collective-permute-start(bf16[16,4608]{1,0:T(8,128)(2,1)S(1)} %collective-permute-done), channel_id=1, source_target_pairs={{0,16},{16,0},{1,17},{17,1},{2,18},{18,2},{3,19},{19,3},{4,20},{20... | collective-permute-start | bytes 442376 | tf_op jit(solution)/shard_map/ppermute | solution.py:175
  15.5 7.0 %collective-permute-start.2 = (bf16[16,4608]{1,0:T(8,128)(2,1)S(1)}, bf16[16,4608]{1,0:T(8,128)(2,1)S(1)}, u32[]{:S(2)}, u32[]{:S(2)}) collective-permute-start(bf16[16,4608]{1,0:T(8,128)(2,1)S(1)} %get-tuple-element.29), channel_id=1, source_target_pairs={{0,12},{1,13},{2,14},{3,15},{4,8},{5,9},{6,10},{7,11},{8,4},{9,5},... | collective-permute-start | bytes 442376 | tf_op jit(solution)/shard_map/ppermute | solution.py:172
  18.0 5.2 %collective-permute-start.6 = (bf16[16,4608]{1,0:T(8,128)(2,1)S(1)}, bf16[16,4608]{1,0:T(8,128)(2,1)S(1)}, u32[]{:S(2)}, u32[]{:S(2)}) collective-permute-start(bf16[16,4608]{1,0:T(8,128)(2,1)S(1)} %collective-permute-done.3), channel_id=1, source_target_pairs={{0,2},{1,3},{2,0},{3,1},{4,6},{5,7},{6,4},{7,5},{8,10},{9,11},{10,... | collective-permute-start | bytes 442376 | tf_op jit(solution)/shard_map/ppermute | solution.py:172
  19.2 10.1 %collective-permute-start.9 = (bf16[32,4608]{1,0:T(8,128)(2,1)S(1)}, bf16[32,4608]{1,0:T(8,128)(2,1)S(1)}, u32[]{:S(2)}, u32[]{:S(2)}) collective-permute-start(bf16[32,4608]{1,0:T(8,128)(2,1)S(1)} %pad_maximum_fusion), channel_id=1, source_target_pairs={{0,16},{16,0},{1,17},{17,1},{2,18},{18,2},{3,19},{19,3},{4,20},{20... | collective-permute-start | bytes 884744 | tf_op jit(solution)/shard_map/ppermute | solution.py:175
  20.8 13.6 %collective-permute-start.11 = (bf16[96,4608]{1,0:T(8,128)(2,1)S(1)}, bf16[96,4608]{1,0:T(8,128)(2,1)S(1)}, u32[]{:S(2)}, u32[]{:S(2)}) collective-permute-start(bf16[96,4608]{1,0:T(8,128)(2,1)S(1)} %constant_dynamic-update-slice_fusion.refs_2_), channel_id=1, source_target_pairs={{0,1},{1,0},{2,3},{3,2},{4,5},{5,4},{6,7},{7,6},{8,9},{9,8},{10,11... | collective-permute-start | bytes 2654216 | tf_op jit(solution)/shard_map/ppermute | solution.py:172
  20.9 0.7 %copy-start.4 = (s32[64]{0:T(128)S(1)}, s32[64]{0:T(128)}, u32[]{:S(2)}) copy-start(s32[64]{0:T(128)} %lengths_hbm) | copy-start | bytes 772
  23.2 6.0 %collective-permute-start.8 = (bf16[16,4608]{1,0:T(8,128)(2,1)S(1)}, bf16[16,4608]{1,0:T(8,128)(2,1)S(1)}, u32[]{:S(2)}, u32[]{:S(2)}) collective-permute-start(bf16[16,4608]{1,0:T(8,128)(2,1)S(1)} %collective-permute-done.2), channel_id=1, source_target_pairs={{0,2},{1,3},{2,0},{3,1},{4,6},{5,7},{6,4},{7,5},{8,10},{9,11},{10,... | collective-permute-start | bytes 442376 | tf_op jit(solution)/shard_map/ppermute | solution.py:172
  24.3 6.8 %collective-permute-start.13 = (bf16[16,4608]{1,0:T(8,128)(2,1)S(1)}, bf16[16,4608]{1,0:T(8,128)(2,1)S(1)}, u32[]{:S(2)}, u32[]{:S(2)}) collective-permute-start(bf16[16,4608]{1,0:T(8,128)(2,1)S(1)} %collective-permute-done.2), channel_id=1, source_target_pairs={{0,16},{16,0},{1,17},{17,1},{2,18},{18,2},{3,19},{19,3},{4,20},{20... | collective-permute-start | bytes 442376 | tf_op jit(solution)/shard_map/ppermute | solution.py:175
  25.8 3.1 %copy-start = (bf16[128,28672]{1,0:T(8,128)(2,1)S(1)}, bf16[128,28672]{1,0:T(8,128)(2,1)}, u32[]{:S(2)}) copy-start(bf16[128,28672]{1,0:T(8,128)(2,1)} %in_ref.7) | copy-start | bytes 22020100
  28.9 5.6 %slice-start = ((s8[7340032]{0:T(1024)(128)(4,1)}), s8[4194304]{0:T(1024)(128)(4,1)S(1)}, s32[]{:S(2)}) async-start(s8[7340032]{0:T(1024)(128)(4,1)} %bitcast), calls=%async_computation | async-start | bytes 8388608
  29.2 5.2 %collective-permute-start.14 = (bf16[16,4608]{1,0:T(8,128)(2,1)S(1)}, bf16[16,4608]{1,0:T(8,128)(2,1)S(1)}, u32[]{:S(2)}, u32[]{:S(2)}) collective-permute-start(bf16[16,4608]{1,0:T(8,128)(2,1)S(1)} %slice.3), channel_id=1, source_target_pairs={{0,2},{1,3},{2,0},{3,1},{4,6},{5,7},{6,4},{7,5},{8,10},{9,11},{10,... | collective-permute-start | bytes 442376 | tf_op jit(solution)/shard_map/ppermute | solution.py:172
  29.5 6.6 %collective-permute-start.10 = (bf16[16,4608]{1,0:T(8,128)(2,1)S(1)}, bf16[16,4608]{1,0:T(8,128)(2,1)S(1)}, u32[]{:S(2)}, u32[]{:S(2)}) collective-permute-start(bf16[16,4608]{1,0:T(8,128)(2,1)S(1)} %collective-permute-done.8), channel_id=1, source_target_pairs={{0,16},{16,0},{1,17},{17,1},{2,18},{18,2},{3,19},{19,3},{4,20},{20... | collective-permute-start | bytes 442376 | tf_op jit(solution)/shard_map/ppermute | solution.py:175
  31.0 3.4 %collective-permute-start.12 = (bf16[80,4608]{1,0:T(8,128)(2,1)S(1)}, bf16[80,4608]{1,0:T(8,128)(2,1)S(1)}, u32[]{:S(2)}, u32[]{:S(2)}) collective-permute-start(bf16[80,4608]{1,0:T(8,128)(2,1)S(1)} %constant_dynamic-update-slice_fusion.5.refs_4_), channel_id=1, source_target_pairs={{0,1},{1,0},{2,3},{3,2},{4,5},{5,4},{6,7},{7,6},{8,9},{9,8},{10,11... | collective-permute-start | bytes 2211848 | tf_op jit(solution)/shard_map/ppermute | solution.py:172
  31.2 3.3 %slice-start.1 = ((s8[7340032]{0:T(1024)(128)(4,1)}), s8[3145728]{0:T(1024)(128)(4,1)S(1)}, s32[]{:S(2)}) async-start(s8[7340032]{0:T(1024)(128)(4,1)} %bitcast), calls=%async_computation.1 | async-start | bytes 6291456
  36.1 1.9 %collective-permute-start.15 = (bf16[48,4608]{1,0:T(8,128)(2,1)S(1)}, bf16[48,4608]{1,0:T(8,128)(2,1)S(1)}, u32[]{:S(2)}, u32[]{:S(2)}) collective-permute-start(bf16[48,4608]{1,0:T(8,128)(2,1)S(1)} %constant_dynamic-update-slice_fusion.9.refs_6_), channel_id=1, source_target_pairs={{0,1},{1,0},{2,3},{3,2},{4,5},{5,4},{6,7},{7,6},{8,9},{9,8},{10,11... | collective-permute-start | bytes 1327112 | tf_op jit(solution)/shard_map/ppermute | solution.py:172
